TPU v7x, 32 devices: a whole 2x2x4 slice. The times are simulated.
32 devices in a mesh: fsdp: 4 (over y, core), ctx: 8 (over z, x).
Axes of the slice: x: 2, y: 2, z: 4, core: 2. Of those that a mesh axis runs over, the one named last changes fastest.
Arguments:
- tokens: bfloat16 [4, 8192, 1024], P('fsdp', 'ctx'), may hold values from -6 to 6
- cotangent: bfloat16 [4, 8192, 1024], P('fsdp', 'ctx'), may hold values from -6 to 6
- order: int32 [4, 8192], P('fsdp'), may hold values from 0 to 8191, as said below
- lengths: int32 [4, 3], P('fsdp'), may hold values from 1024 to 6144, as said below
- adapter_ids: int32 [4, 3], P('fsdp'), may hold values from 0 to 7
- in_weight: bfloat16 [1024, 4384], P('fsdp'), may hold values from -0.1875 to 0.1875
- out_weight: bfloat16 [2048, 1024], P('fsdp'), may hold values from -0.125 to 0.125
- in_down: bfloat16 [1024, 128], P(None, 'fsdp'), may hold values from -0.1875 to 0.1875
- in_up: bfloat16 [128, 4384], P('fsdp'), may hold values from -0.75 to 0.75
- out_down: bfloat16 [2048, 128], P(None, 'fsdp'), may hold values from -0.125 to 0.125
- out_up: bfloat16 [128, 1024], P('fsdp'), may hold values from -0.75 to 0.75
- norm_gain: float32 [1024], replicated, may hold values from 0.25 to 1.75
- conv_weight: float32 [4, 2304], replicated, may hold values from -0.5 to 0.5
- conv_bias: float32 [2304], replicated, may hold values from -0.5 to 0.5
- dt_bias: float32 [32], replicated, may hold values from -6 to -1
- a_log: float32 [32], replicated, may hold values from -6 to 2
- skip_gain: float32 [32], replicated, may hold values from 0.5 to 1.5
- gate_gain: float32 [2048], replicated, may hold values from 0.25 to 1.75
Outputs:
- block_output: bfloat16 [4, 8192, 1024], P('fsdp', 'ctx')
- input_grad: bfloat16 [4, 8192, 1024], P('fsdp', 'ctx')
- in_down_grad: float32 [1024, 128], P(None, 'fsdp')
- in_up_grad: float32 [128, 4384], P('fsdp')
- out_down_grad: float32 [2048, 128], P(None, 'fsdp')
- out_up_grad: float32 [128, 1024], P('fsdp')
Inputs may be any that keep to these rules, and one draw needn't show every extreme that they name: order[g] is a permutation of the group's slots; of the 1024 arrival positions of each block of 1024, exactly 128 land in each block of 1024 packed slots. Some sequence of each group has length exactly 6144; the lengths of a group sum to at most 8192, the remaining slots are padding at the group's end.
All inputs are finite; a program needn't handle non-finite values.
Results may differ from a plain program's by a relative error of at most 0.02.
The roundings to bfloat16 on the way count: a program that leaves them out, or rounds other values in their place, can miss the bound.
Values may be sent and summed in bfloat16 or wider, within the bound.
A program may use at most 256 MiB of HBM per device.

v0:
```python
import jax
import jax.numpy as jnp
from jax import lax
from jax.sharding import PartitionSpec as P

HEADS = 32
HEAD = 64
STATE = 128
KERNEL = 4
SPAN = 256
RANK = 16
ADAPTERS = 8
SEQS = 3
CONV_CH = 2304


epsilon = 1e-05


def from_behind(x, axis, by):
    length = lax.axis_size(axis)
    pairs = [(i, i + by) for i in range(length) if 0 <= i + by < length]
    return lax.ppermute(x, axis, pairs)


def prefix(x, axis, combine, identity, reverse):
    length, here = (lax.axis_size(axis), lax.axis_index(axis))
    everything = jax.tree.map(
        lambda part, kind: lax.all_gather(part.astype(kind), axis), x, (jnp.bfloat16, jnp.bfloat16)
    )
    start = jax.tree.map(
        lambda part, zero: jnp.broadcast_to(jnp.asarray(zero, part.dtype), part.shape), x, identity
    )

    def lap(k, before):
        at = length - 1 - k if reverse else k
        reached = at > here if reverse else at < here
        new = combine(
            before, jax.tree.map(lambda part, own: part[at].astype(own.dtype), everything, x)
        )
        return jax.tree.map(lambda a, b: jnp.where(reached, a, b), new, before)

    return lax.fori_loop(0, length, lap, start)


def product(left, right):
    return jnp.dot(left, right, preferred_element_type=jnp.float32)


def inner_rows(left, right):
    return lax.dot_general(
        left, right, (((0,), (0,)), ((), ())), preferred_element_type=jnp.float32
    )


def outer_cols(left, right):
    return lax.dot_general(
        left, right, (((1,), (1,)), ((), ())), preferred_element_type=jnp.float32
    )


def seq_index(positions, ends):
    found = jnp.sum((positions[:, None] >= ends[None, :]).astype(jnp.int32), 1)
    return jnp.where(positions >= 0, found, -1)


def carry_join(early, late):
    return (late[0] * early[0], late[1] + late[0][:, None, None] * early[1])


def local(
    tokens,
    cotangent,
    order,
    lengths,
    adapter_ids,
    in_weight,
    out_weight,
    in_down,
    in_up,
    out_down,
    out_up,
    norm_gain,
    conv_weight,
    conv_bias,
    dt_bias,
    a_log,
    skip_gain,
    gate_gain,
):
    ctx_place = lax.axis_index("ctx")
    rows = tokens.shape[1]
    blocks = rows // SPAN
    inner = HEADS * HEAD
    halo_rows = KERNEL - 1
    perm_full = order[0]
    local_perm = lax.dynamic_slice_in_dim(perm_full, ctx_place * rows, rows)
    send_order = jnp.argsort(local_perm // rows, stable=True)
    sent_tokens = jnp.take(tokens[0], send_order, axis=0)
    sent_cot = jnp.take(cotangent[0], send_order, axis=0)
    got_tokens, got_cot = (
        lax.all_to_all(sent_tokens, "ctx", split_axis=0, concat_axis=0, tiled=True),
        lax.all_to_all(sent_cot, "ctx", split_axis=0, concat_axis=0, tiled=True),
    )
    keys_away = (perm_full // rows != ctx_place).astype(jnp.int32)
    arrived = jnp.argsort(keys_away, stable=True)[:rows]
    slots = jnp.take(perm_full, arrived) % rows
    unsort = jnp.argsort(slots)
    packed_tokens = jnp.take(got_tokens, unsort, axis=0)
    packed_cot = jnp.take(got_cot, unsort, axis=0)
    ends = jnp.cumsum(lengths[0])
    start_pos = ctx_place * rows
    positions = start_pos + jnp.arange(rows, dtype=jnp.int32)
    seq_ids = seq_index(positions, ends)
    valid = (positions < ends[-1]).astype(jnp.float32)
    halo_ids = seq_index(start_pos - halo_rows + jnp.arange(halo_rows, dtype=jnp.int32), ends)
    span_prev = seq_index(start_pos + jnp.arange(blocks, dtype=jnp.int32) * SPAN - 1, ends)
    adapter_tok = jnp.sum(
        jnp.where(
            seq_ids[:, None] == jnp.arange(SEQS, dtype=jnp.int32)[None, :],
            adapter_ids[0][None, :],
            0,
        ),
        1,
    )
    select = (
        (jnp.arange(ADAPTERS * RANK, dtype=jnp.int32) // RANK)[None, :] == adapter_tok[:, None]
    ).astype(jnp.float32) * valid[:, None]
    select_low = select.astype(jnp.bfloat16)
    w_in, w_out, a_in, b_in, a_out, b_out = (
        lax.all_gather(in_weight, "fsdp", axis=0, tiled=True),
        lax.all_gather(out_weight, "fsdp", axis=0, tiled=True),
        lax.all_gather(in_down, "fsdp", axis=1, tiled=True),
        lax.all_gather(in_up, "fsdp", axis=0, tiled=True),
        lax.all_gather(out_down, "fsdp", axis=1, tiled=True),
        lax.all_gather(out_up, "fsdp", axis=0, tiled=True),
    )
    x_in = packed_tokens.astype(jnp.float32) * valid[:, None]

    def norm_in(value):
        return value * lax.rsqrt(jnp.mean(value * value, -1, keepdims=True) + epsilon) * norm_gain

    normed, norm_back = jax.vjp(norm_in, x_in)
    normed_low = normed.astype(jnp.bfloat16)
    lowrank = (product(normed_low, a_in) * select).astype(jnp.bfloat16)
    proj = product(normed_low, w_in) + product(lowrank, b_in)
    gate_in = proj[:, :inner]
    raw = proj[:, inner : inner + CONV_CH].astype(jnp.bfloat16)
    dt_raw = proj[:, inner + CONV_CH :]
    halo = from_behind(raw[rows - halo_rows :], "ctx", 1)
    seq_full = jnp.concatenate([halo_ids, seq_ids], 0)

    def conv_fn(raw_value, halo_value):
        joined = jnp.concatenate([halo_value, raw_value], 0)
        accum = jnp.zeros((rows, CONV_CH), jnp.float32) + conv_bias
        for tap in range(KERNEL):
            same = (seq_full[tap : tap + rows] == seq_ids)[:, None]
            accum = accum + jnp.where(same, joined[tap : tap + rows] * conv_weight[tap], 0.0)
        return jax.nn.silu(accum)

    active, conv_back = jax.vjp(conv_fn, raw.astype(jnp.float32), halo.astype(jnp.float32))
    x_state = active[:, :inner].astype(jnp.bfloat16)
    b_mat = active[:, inner : inner + STATE].astype(jnp.bfloat16)
    c_mat = active[:, inner + STATE :].astype(jnp.bfloat16)

    def step_fn(value):
        return jax.nn.softplus(value + dt_bias)

    step_size, step_back = jax.vjp(step_fn, dt_raw)
    rates = -jnp.exp(a_log)
    seq_blocks = seq_ids.reshape(blocks, SPAN)
    causal = jnp.arange(SPAN)[:, None] >= jnp.arange(SPAN)[None, :]
    same_mask = causal[None] & (seq_blocks[:, :, None] == seq_blocks[:, None, :])
    end_same = (seq_blocks == seq_blocks[:, -1:]).astype(jnp.float32)
    passing = (seq_blocks == span_prev[:, None]).astype(jnp.float32)

    def decays(steps_in):
        steps_t = steps_in.reshape(blocks, SPAN, HEADS).transpose(0, 2, 1)
        cumul = jnp.cumsum(steps_t * rates[None, :, None], axis=2)
        spread = cumul[..., :, None] - cumul[..., None, :]
        kernel = (
            jnp.where(same_mask[:, None], jnp.exp(jnp.minimum(spread, 0.0)), 0.0)
            * steps_t[:, :, None, :]
        )
        weights = jnp.exp(cumul[..., -1:] - cumul) * end_same[:, None] * steps_t
        reach = passing[:, None] * jnp.exp(cumul)
        carry = passing[:, -1][:, None] * jnp.exp(cumul[..., -1])
        return (kernel, weights, reach, carry)

    (kernel, weights, reach, carry), decay_back = jax.vjp(decays, step_size)
    c_blocks = c_mat.reshape(blocks, SPAN, STATE)
    b_blocks = b_mat.reshape(blocks, SPAN, STATE)
    scores = jnp.einsum("ctn,csn->cts", c_blocks, b_blocks, preferred_element_type=jnp.float32)
    mixing = (scores[:, None] * kernel).astype(jnp.bfloat16)
    xs_blocks = x_state.reshape(blocks, SPAN, HEADS, HEAD)
    within = jnp.einsum("chts,cshp->cthp", mixing, xs_blocks, preferred_element_type=jnp.float32)
    weights_t = weights.transpose(0, 2, 1)[..., None]
    weighted = (xs_blocks.astype(jnp.float32) * weights_t).astype(jnp.bfloat16)
    local_state = jnp.einsum(
        "cshp,csn->chpn", weighted, b_blocks, preferred_element_type=jnp.float32
    )
    zero_state = jnp.zeros((HEADS, HEAD, STATE), jnp.float32)
    summary = zero_state
    through = jnp.ones((HEADS,), jnp.float32)
    for block in range(blocks):
        summary = carry[block][:, None, None] * summary + local_state[block]
        through = through * carry[block]
    scanned = prefix(
        (through, summary), "ctx", carry_join, (jnp.ones((HEADS,), jnp.float32), zero_state), False
    )
    running = scanned[1]
    start_list = []
    for block in range(blocks):
        start_list.append(running)
        running = carry[block][:, None, None] * running + local_state[block]
    starts = jnp.stack(start_list)
    starts_low = starts.astype(jnp.bfloat16)
    projected = jnp.einsum(
        "ctn,chpn->cthp", c_blocks, starts_low, preferred_element_type=jnp.float32
    )
    reach_t = reach.transpose(0, 2, 1)[..., None]
    mixed = within + reach_t * projected + skip_gain[:, None] * xs_blocks.astype(jnp.float32)
    mixed = mixed.reshape(rows, inner)

    def gate_fn(mixed_value, gate_value):
        gated = mixed_value * jax.nn.silu(gate_value)
        return gated * lax.rsqrt(jnp.mean(gated * gated, -1, keepdims=True) + epsilon) * gate_gain

    norm_out, gate_back = jax.vjp(gate_fn, mixed, gate_in)
    norm_low = norm_out.astype(jnp.bfloat16)
    lowrank_out = (product(norm_low, a_out) * select).astype(jnp.bfloat16)
    branch = product(norm_low, w_out) + product(lowrank_out, b_out)
    result = ((x_in + branch) * valid[:, None]).astype(jnp.bfloat16)
    d_out = packed_cot.astype(jnp.float32) * valid[:, None]
    d_out_low = d_out.astype(jnp.bfloat16)
    grad_b_out = inner_rows(lowrank_out, d_out_low)
    d_lowrank_out = outer_cols(d_out_low, b_out).astype(jnp.bfloat16) * select_low
    grad_a_out = inner_rows(norm_low, d_lowrank_out)
    d_norm = outer_cols(d_out_low, w_out) + outer_cols(d_lowrank_out, a_out)
    d_mixed, d_gate = gate_back(d_norm)
    d_mixed_low = d_mixed.astype(jnp.bfloat16).reshape(blocks, SPAN, HEADS, HEAD)
    d_mixed_wide = d_mixed_low.astype(jnp.float32)
    d_xs = skip_gain[:, None] * d_mixed_wide
    d_mixing = jnp.einsum(
        "cthp,cshp->chts", d_mixed_low, xs_blocks, preferred_element_type=jnp.float32
    )
    d_xs = d_xs + jnp.einsum(
        "chts,cthp->cshp", mixing, d_mixed_low, preferred_element_type=jnp.float32
    )
    d_proj = (d_mixed_wide * reach_t).astype(jnp.bfloat16)
    d_reach = jnp.sum(d_mixed_wide * projected, -1).transpose(0, 2, 1)
    d_start = jnp.einsum("cthp,ctn->chpn", d_proj, c_blocks, preferred_element_type=jnp.float32)
    d_c = jnp.einsum("cthp,chpn->ctn", d_proj, starts_low, preferred_element_type=jnp.float32)

    def state_back(later_grad):
        accum = later_grad
        local_grads = [None] * blocks
        carry_grads = [None] * blocks
        for block in range(blocks - 1, -1, -1):
            local_grads[block] = accum
            carry_grads[block] = jnp.sum(accum * starts[block], (1, 2))
            accum = d_start[block] + carry[block][:, None, None] * accum
        return (accum, local_grads, carry_grads)

    own_part, _, _ = state_back(zero_state)
    later = prefix(
        (through, own_part), "ctx", carry_join, (jnp.ones((HEADS,), jnp.float32), zero_state), True
    )
    _, local_grads, carry_grads = state_back(later[1])
    d_local = jnp.stack(local_grads).astype(jnp.bfloat16)
    d_carry = jnp.stack(carry_grads)
    d_weighted = jnp.einsum("csn,chpn->cshp", b_blocks, d_local, preferred_element_type=jnp.float32)
    d_xs = d_xs + d_weighted * weights_t
    d_weights = jnp.sum(d_weighted * xs_blocks.astype(jnp.float32), -1).transpose(0, 2, 1)
    d_b = jnp.einsum("cshp,chpn->csn", weighted, d_local, preferred_element_type=jnp.float32)
    d_scores = jnp.sum(d_mixing * kernel, 1).astype(jnp.bfloat16)
    d_kernel = d_mixing * scores[:, None]
    d_c = d_c + jnp.einsum("cts,csn->ctn", d_scores, b_blocks, preferred_element_type=jnp.float32)
    d_b = d_b + jnp.einsum("cts,ctn->csn", d_scores, c_blocks, preferred_element_type=jnp.float32)
    (d_step,) = decay_back((d_kernel, d_weights, d_reach, d_carry))
    (d_dt_raw,) = step_back(d_step)
    d_active = jnp.concatenate(
        [d_xs.reshape(rows, inner), d_b.reshape(rows, STATE), d_c.reshape(rows, STATE)], 1
    )
    d_raw, d_halo = conv_back(d_active)
    from_next = from_behind(d_halo, "ctx", -1)
    d_raw = d_raw.at[rows - halo_rows :].add(from_next)
    d_proj_all = jnp.concatenate([d_gate, d_raw, d_dt_raw], 1).astype(jnp.bfloat16)
    grad_b_in = inner_rows(lowrank, d_proj_all)
    d_lowrank = outer_cols(d_proj_all, b_in).astype(jnp.bfloat16) * select_low
    grad_a_in = inner_rows(normed_low, d_lowrank)
    d_normed = outer_cols(d_proj_all, w_in) + outer_cols(d_lowrank, a_in)
    (d_x_norm,) = norm_back(d_normed)
    d_x = ((d_out + d_x_norm) * valid[:, None]).astype(jnp.bfloat16)
    back_out, back_grad = (
        lax.all_to_all(
            jnp.take(result, slots, axis=0), "ctx", split_axis=0, concat_axis=0, tiled=True
        ),
        lax.all_to_all(
            jnp.take(d_x, slots, axis=0), "ctx", split_axis=0, concat_axis=0, tiled=True
        ),
    )
    restore = jnp.argsort(send_order)
    block_output = jnp.take(back_out, restore, axis=0)[None]
    input_grad = jnp.take(back_grad, restore, axis=0)[None]
    grads = (grad_a_in, grad_b_in, grad_a_out, grad_b_out)
    totals = (
        lax.psum(grads[0].astype(jnp.bfloat16), "ctx").astype(jnp.float32),
        lax.psum(grads[1].astype(jnp.bfloat16), "ctx").astype(jnp.float32),
        lax.psum(grads[2].astype(jnp.bfloat16), "ctx").astype(jnp.float32),
        lax.psum(grads[3].astype(jnp.bfloat16), "ctx").astype(jnp.float32),
    )
    shares = (
        lax.psum_scatter(
            totals[0].astype(jnp.bfloat16), "fsdp", scatter_dimension=1, tiled=True
        ).astype(jnp.float32),
        lax.psum_scatter(
            totals[1].astype(jnp.bfloat16), "fsdp", scatter_dimension=0, tiled=True
        ).astype(jnp.float32),
        lax.psum_scatter(
            totals[2].astype(jnp.bfloat16), "fsdp", scatter_dimension=1, tiled=True
        ).astype(jnp.float32),
        lax.psum_scatter(
            totals[3].astype(jnp.bfloat16), "fsdp", scatter_dimension=0, tiled=True
        ).astype(jnp.float32),
    )
    return (block_output, input_grad, shares[0], shares[1], shares[2], shares[3])


def solution(mesh):
    placed = (
        P("fsdp", "ctx", None),
        P("fsdp", "ctx", None),
        P("fsdp", None),
        P("fsdp", None),
        P("fsdp", None),
        P("fsdp", None),
        P("fsdp", None),
        P(None, "fsdp"),
        P("fsdp", None),
        P(None, "fsdp"),
        P("fsdp", None),
        P(),
        P(),
        P(),
        P(),
        P(),
        P(),
        P(),
    )
    return jax.shard_map(
        local,
        mesh=mesh,
        in_specs=placed,
        out_specs=(
            P("fsdp", "ctx", None),
            P("fsdp", "ctx", None),
            P(None, "fsdp"),
            P("fsdp", None),
            P(None, "fsdp"),
            P("fsdp", None),
        ),
        check_vma=False,
    )
```

profile of v0, /device:TPU:10, one launch (start us, length us, event | category | flops | bytes accessed | tf_op | source)
XLA Modules:
  0.0 887.6 jit_solution(2182002595514277570)
XLA Ops:
  9.4 4.4 sort.65
  13.8 5.3 gather_fusion.5
  19.1 8.3 gather_fusion.1
  27.4 4.1 broadcast_select_fusion.5
  31.6 6.4 all-to-all-start
  38.8 6.8 sort.66
  45.6 6.1 gather_fusion
  54.0 4.4 sort.67
  58.4 7.8 all_gather.33
  67.6 15.3 %all-to-all-done = bf16[8,128,1024]{2,1,0:T(8,128)(2,1)S(1)} async-done(((bf16[8,128,1024]{2,1,0:T(8,128)(2,1)}), bf16[8,128,1024]{2,1,0:T(8,128)(2,1)S(1)}, u32[]{:S(2)}, u32[]{:S(2)}) %all-to-all-start) | async-done | bytes 2097184 | tf_op jit(solution)/shard_map/all_to_all | solution.py:102
  82.9 5.3 gather_fusion.2
  95.0 15.6 %fusion.143 = f32[1024,4384]{0,1:T(8,128)} fusion(bf16[1024,1024]{1,0:T(8,128)(2,1)S(1)} %multiply_convert_fusion.4, bf16[1024,4384]{0,1:T(8,128)(2,1)} %all-gather.7.cloned.1.call-done), kind=kOutput, calls=%fused_computation.308 | convolution fusion | flops 9193914368 | bytes 29032448 | tf_op jit(solution)/shard_map/dot_general | solution.py:47
  110.6 14.3 %fusion.142 = (bf16[1024,4384]{0,1:T(8,128)(2,1)}, f32[1024,4384]{0,1:T(8,128)}) fusion(f32[1024,4384]{0,1:T(8,128)} %fusion.143, bf16[1024,128]{1,0:T(8,128)(2,1)S(1)} %fusion.75, bf16[128,4384]{1,0:T(8,128)(2,1)} %all-gather.9.cloned.1.call-done), kind=kOutput, calls=%fused_computation.307 | convolution fusion | flops 1158217728 | bytes 46276608 | tf_op jit(solution)/shard_map/dot_general | solution.py:47
  131.5 3.6 collective-permute-start
  137.2 7.2 slice_convert_fusion
  145.5 24.6 %multiply_convert_fusion = (bf16[1024,2304]{0,1:T(8,128)(2,1)S(1)}, f32[1024,2304]{0,1:T(8,128)}) fusion(f32[1024,2304]{0,1:T(8,128)} %slice_convert_fusion, f32[2304]{0:T(1024)S(1)} %get-tuple-element.303, f32[2304]{0:T(1024)S(1)} %get-tuple-element.304, f32[3,2304]{0,1:T(8,128)S(1)} %copy.327, pred[1024]{0:T(1024)(128)(4,1)S(1)} %get-tuple-element.361, ...), kind=kLoop, calls=%fused_computation.65 | loop fusion | flops 44826624 | bytes 23669760 | tf_op jit(solution)/shard_map/convert.25
  174.7 7.9 reshape.438
  191.5 6.8 all-to-all-start.2
  198.3 7.4 all_gather.39
  205.8 8.7 all_gather.38
  216.1 54.6 %all-to-all-done.2 = bf16[8,128,1024]{2,1,0:T(8,128)(2,1)S(1)} async-done(((bf16[8,128,1024]{2,1,0:T(8,128)(2,1)}), bf16[8,128,1024]{2,1,0:T(8,128)(2,1)S(1)}, u32[]{:S(2)}, u32[]{:S(2)}) %all-to-all-start.2) | async-done | bytes 2097184 | tf_op jit(solution)/shard_map/all_to_all | solution.py:103
  270.7 5.3 gather_fusion.6
  279.4 9.7 %fusion.135 = f32[1024,2048]{0,1:T(8,128)} fusion(bf16[2048,1024]{1,0:T(8,128)(2,1)} %all-gather.13.cloned.1.call-done, f32[1024]{0:T(1024)S(1)} %get-tuple-element.385, bf16[1024,1024]{1,0:T(8,128)(2,1)S(1)} %copy-done.27, pred[1024]{0:T(1024)(128)(4,1)S(1)} %copy-done.109), kind=kOutput, calls=%fused_computation.305 | convolution fusion | flops 4299161600 | bytes 14685184 | tf_op jit(solution)/shard_map/dot_general | solution.py:57
  289.1 19.6 %all-gather = bf16[8,1,32]{2,1,0:T(2,128)(2,1)S(1)} all-gather(bf16[1,1,32]{2,1,0:T(2,128)(2,1)S(1)} %copy-done.143), channel_id=1, replica_groups=mesh['fsdp'=4,'ctx'=8] {'ctx'}, dimensions={0}, use_global_device_ids=true | all-gather | bytes 576 | tf_op jit(solution)/shard_map/all_gather | solution.py:29
  314.6 10.7 %while.31 = (s32[]{:T(128)}, f32[32,64,128]{2,1,0:T(8,128)S(1)}, s32[]{:T(128)}, bf16[8,32,64,128]{3,2,1,0:T(8,128)(2,1)}, bf16[8,32]{1,0:T(8,128)(2,1)S(1)}, /*index=5*/s32[]{:T(128)}, s32[]{:T(128)}) while((s32[]{:T(128)}, f32[32,64,128]{2,1,0:T(8,128)S(1)}, s32[]{:T(128)}, bf16[8,32,64,128]{3,2,1,0:T(8,128)(2,1)}, ...), condition=%wide.region_12.14_spmd.clone, body=%wide.region_11.13_spmd.clone.sunk | while | flops 1310756 | bytes 2621865 | solution.py:43
  334.4 13.5 %fusion.32 = f32[4,256,32,64]{1,3,2,0:T(8,128)} fusion(f32[4,256,32,64]{1,3,2,0:T(8,128)S(1)} %fusion.93, f32[32]{0:T(128)S(1)} %copy-done.149, f32[4,256,32]{1,2,0:T(8,128)S(1)} %copy-done.77, f32[4,32,256]{2,1,0:T(8,128)S(1)} %copy-done.81, f32[4,32,256]{2,1,0:T(8,128)S(1)} %copy-done.63, f32[4,256,256]{2,1,0:T(8,128)S(1)} %copy-done.55, ...), kind=kOutput, calls=%fused_computation.69 | convolution fusion | flops 1134559232 | bytes 22675584 | tf_op jit(solution)/shard_map/chts,cshp->cthp/dot_general | solution.py:196
  347.9 13.8 %copy.347 = f32[4,256,32,64]{1,0,3,2:T(4,128)} copy(f32[4,256,32,64]{1,3,2,0:T(8,128)} %fusion.32) | data formatting | bytes 16777216 | tf_op jit(solution)/shard_map/add | solution.py:222
  361.7 5.5 copy.410
  367.3 11.4 %multiply_reduce_fusion = (f32[1024]{0:T(1024)S(1)}, f32[1024]{0:T(1024)S(1)}, f32[1024,2048]{0,1:T(8,128)}, f32[1024,2048]{0,1:T(8,128)}) fusion(f32[1024,2048]{0,1:T(8,128)S(1)} %bitcast.262, f32[1024,4384]{0,1:T(8,128)} %get-tuple-element.378, f32[2048]{0:T(1024)S(1)} %copy-done.125, f32[1024,2048]{0,1:T(8,128)} %fusion.135, ...), kind=kOutput, calls=%fused_computation.80 | convolution fusion | flops 559937536 | bytes 42745856 | tf_op jit(solution)/shard_map/dot_general | solution.py:57
  378.7 16.8 %fusion.36 = (bf16[1024,2048]{0,1:T(8,128)(2,1)}, bf16[1024,2048]{0,1:T(8,128)(2,1)}, bf16[1024,2048]{0,1:T(8,128)(2,1)}) fusion(f32[1024,2048]{0,1:T(8,128)S(1)} %bitcast.263, f32[1024,4384]{0,1:T(8,128)} %get-tuple-element.378, f32[1024,2048]{0,1:T(8,128)} %get-tuple-element.335, f32[1024]{0:T(1024)S(1)} %get-tuple-element.362, ...), kind=kLoop, calls=%fused_computation.73 | loop fusion | flops 44040192 | bytes 46153728 | tf_op jit(solution)/shard_map/convert.4
  395.5 7.9 reshape.445
  403.4 3.7 fusion.50
  411.3 33.3 %fusion.43 = (f32[4,32,256]{2,1,0:T(8,128)}, f32[4,32,256]{2,1,0:T(8,128)S(1)}, f32[4,32,256]{2,1,0:T(8,128)S(1)}, bf16[4,256,256]{2,1,0:T(8,128)(2,1)S(1)}) fusion(f32[4,32,256]{2,1,0:T(8,128)S(1)} %copy-done.63, f32[4,32,256]{2,1,0:T(8,128)S(1)} %copy-done.82, f32[4,256,256]{2,1,0:T(8,128)S(1)} %copy-done.55, pred[4,256,256]{2,1,0:T(8,128)(4,1)S(1)} %copy-done.71, ...), kind=kOutput, calls=%fused_computation.89 | convolution fusion | flops 1232764928 | bytes 10878976 | tf_op jit(solution)/shard_map/cthp,cshp->chts/dot_general | solution.py:244
  445.9 6.8 fusion.40
  456.8 3.8 fusion.76
  460.6 6.6 fusion.145
  468.9 5.4 gather_fusion.3
  474.4 9.8 %all-gather.15.cloned.1.call-done = bf16[8,32,64,128]{3,2,1,0:T(8,128)(2,1)} async-done(((bf16[1,32,64,128]{3,2,1,0:T(8,128)(2,1)}), bf16[8,32,64,128]{3,2,1,0:T(8,128)(2,1)}) %all-gather.15.cloned.1.call-update) | async-done | bytes 4194320 | tf_op jit(solution)/shard_map/all_gather | solution.py:29
  484.2 16.1 %while.32 = (s32[]{:T(128)}, f32[32,64,128]{2,1,0:T(8,128)S(1)}, s32[]{:T(128)}, bf16[8,32,64,128]{3,2,1,0:T(8,128)(2,1)}, bf16[8,32]{1,0:T(8,128)(2,1)}, /*index=5*/s32[]{:T(128)}, s32[]{:T(128)}, s32[]{:T(128)}, s32[]{:T(128)}) while((s32[]{:T(128)}, f32[32,64,128]{2,1,0:T(8,128)S(1)}, s32[]{:T(128)}, ...), condition=%wide.region_17.19_spmd.clone, body=%wide.region_16.18_spmd.clone.sunk | while | flops 1310760 | bytes 2621927 | solution.py:43
  513.1 13.1 %fusion.38 = f32[4,256,32,64]{1,3,2,0:T(8,128)} fusion(f32[4,256,32,64]{1,3,2,0:T(8,128)S(1)} %get-tuple-element.381, f32[32]{0:T(128)S(1)} %copy-done.150, f32[4,256,32]{1,2,0:T(8,128)S(1)} %copy-done.76, f32[4,32,256]{2,1,0:T(8,128)S(1)} %copy-done.83, f32[4,32,256]{2,1,0:T(8,128)S(1)} %copy-done.63, f32[4,256,256]{2,1,0:T(8,128)S(1)} %copy-done.56, ...), kind=kOutput, calls=%fused_computation.75 | convolution fusion | flops 1134559232 | bytes 22675584 | tf_op jit(solution)/shard_map/chts,cthp->cshp/dot_general | solution.py:247
  526.3 13.8 %copy.354 = f32[4,256,32,64]{1,0,3,2:T(4,128)} copy(f32[4,256,32,64]{1,3,2,0:T(8,128)} %fusion.38) | data formatting | bytes 16777216 | tf_op jit(solution)/shard_map/add | solution.py:273
  540.1 8.8 copy.411
  549.6 16.9 %broadcast_multiply_fusion = (f32[1024,2304]{0,1:T(8,128)}, f32[1024,2304]{0,1:T(8,128)}) fusion(f32[2304]{0:T(1024)S(1)} %copy-done.91, f32[1024,2304]{0,1:T(8,128)} %get-tuple-element.343, f32[1024,128]{0,1:T(8,128)S(1)} %copy-done.38, f32[1024,128]{0,1:T(8,128)S(1)} %copy.403, f32[1024,2048]{0,1:T(8,128)} %bitcast.264), kind=kLoop, calls=%fused_computation.91 | loop fusion | flops 28311552 | bytes 37757952 | tf_op jit(solution)/shard_map/transpose(jvp())/mul | solution.py:158
  566.5 9.5 %select_multiply_fusion.2 = (f32[1024,2304]{0,1:T(8,128)S(1)}, f32[1024,2304]{0,1:T(8,128)S(1)}, f32[1024,2304]{0,1:T(8,128)}) fusion(f32[1024,2304]{0,1:T(8,128)} %get-tuple-element.330, f32[2304]{0:T(1024)S(1)} %copy-done.89, pred[1024]{0:T(1024)(128)(4,1)S(1)} %copy-done.124, f32[2304]{0:T(1024)S(1)} %copy-done.87, pred[1024]{0:T(1024)(128)(4,1)S(1)} %copy-done.122, ...), kind=kLoop, calls=%fused_computation.64 | loop fusion | flops 14155776 | bytes 37779456 | tf_op jit(solution)/shard_map/transpose(jvp())/mul | solution.py:158
  582.5 13.7 %pad_add_fusion = bf16[1027,2304]{0,1:T(8,128)(2,1)} fusion(f32[1024,2304]{0,1:T(8,128)} %get-tuple-element.348, f32[1024,2304]{0,1:T(8,128)S(1)} %get-tuple-element.347, f32[1024,2304]{0,1:T(8,128)S(1)} %get-tuple-element.346, f32[1024,2304]{0,1:T(8,128)} %get-tuple-element.329), kind=kLoop, calls=%fused_computation.43 | loop fusion | flops 9464832 | bytes 42481152 | tf_op jit(solution)/shard_map/transpose(jvp())/add_any | solution.py:158
  603.1 10.4 %reduce-window.21 = f32[4,32,2,128]{3,1,2,0:T(8,128)S(1)} reduce-window(f32[4,32,2,128]{3,1,2,0:T(8,128)S(1)} %copy.375, f32[]{:T(128)} %constant.233.clone.1), window={size=1x1x1x128 pad=0_0x0_0x0_0x0_127}, to_apply=%region_29.31 | reduce-window | flops 4161536 | bytes 262148 | tf_op jit(solution)/shard_map/reduce-window.3
  615.7 7.3 split.8
  626.6 7.0 scatter-add.4
  633.6 5.7 fusion.77
  639.4 15.0 %fusion.132 = f32[1024,1024]{1,0:T(8,128)S(1)} fusion(bf16[1024,4384]{0,1:T(8,128)(2,1)} %all-gather.7.cloned.1.call-done, bf16[1024,32]{0,1:T(8,128)(2,1)S(1)} %fusion.99, bf16[1024,2304]{0,1:T(8,128)(2,1)S(1)} %copy-done.29, bf16[1024,2048]{0,1:T(8,128)(2,1)} %get-tuple-element.344), kind=kOutput, calls=%fused_computation.304 | convolution fusion | flops 9220849664 | bytes 22151168 | tf_op jit(solution)/shard_map/dot_general | solution.py:57
  658.3 5.5 gather_fusion.7
  663.8 4.7 broadcast_select_fusion
  668.5 5.1 all-to-all-start.1
  676.9 4.5 convolution_convert_fusion.1
  681.4 37.0 %all-to-all-done.1 = bf16[8,128,1024]{2,1,0:T(8,128)(2,1)S(1)} async-done(((bf16[8,128,1024]{2,1,0:T(8,128)(2,1)}), bf16[8,128,1024]{2,1,0:T(8,128)(2,1)S(1)}, u32[]{:S(2)}, u32[]{:S(2)}) %all-to-all-start.1) | async-done | bytes 2097184 | tf_op jit(solution)/shard_map/all_to_all | solution.py:296
  718.5 7.7 all-to-all-start.3
  729.0 7.2 convolution_convert_fusion
  736.3 14.6 %reduce-scatter.5.cloned.1.call-done = bf16[1024,32]{0,1:T(8,128)(2,1)} async-done(((bf16[1024,128]{0,1:T(8,128)(2,1)}), bf16[1024,32]{0,1:T(8,128)(2,1)}) %reduce-scatter.5.cloned.1.call-update) | async-done | bytes 65552 | tf_op jit(solution)/shard_map/reduce_scatter | solution.py:314
  751.0 28.9 %reduce-scatter.7.cloned.1.call-done = bf16[32,4384]{1,0:T(8,128)(2,1)} async-done(((bf16[128,4384]{1,0:T(8,128)(2,1)}), bf16[32,4384]{1,0:T(8,128)(2,1)}) %reduce-scatter.7.cloned.1.call-update) | async-done | bytes 280592 | tf_op jit(solution)/shard_map/reduce_scatter | solution.py:317
  779.9 4.4 sort.68
  784.2 71.8 %all-reduce.9.cloned.1.call-done = (bf16[1024,32]{0,1:T(8,128)(2,1)}, bf16[32,4384]{1,0:T(8,128)(2,1)}, bf16[2048,32]{0,1:T(8,128)(2,1)}, bf16[32,1024]{1,0:T(8,128)(2,1)}) async-done(((bf16[1024,32]{0,1:T(8,128)(2,1)}, bf16[32,4384]{1,0:T(8,128)(2,1)}, bf16[2048,32]{0,1:T(8,128)(2,1)}, bf16[32,1024]{1,0:T(8,128)(2,1)}), (bf16[1024,32]{0,1:T(8,128)(2,1)}, bf16[32,4384]{1,0:T(8,128)(2,1)}, ...) | async-done | bytes 542736 | tf_op jit(solution)/shard_map/psum | solution.py:308
  862.5 5.3 gather_fusion.4
  867.9 8.0 gather_fusion.8
  875.9 4.7 select_bitcast_fusion
  (504 shorter events, 142.2 us)
Async XLA Ops:
  7.2 87.8 %all-gather.7.cloned.1.call-start = ((), (), s32[]{:S(2)}) async-start(), calls=%async_computation.8 | async-start | bytes 11223040 | tf_op jit(solution)/shard_map/all_gather | solution.py:131
  7.9 102.7 %all-gather.9.cloned.1.call-start = ((), (), s32[]{:S(2)}) async-start(), calls=%async_computation.9 | async-start | bytes 1433600 | tf_op jit(solution)/shard_map/all_gather | solution.py:134
  31.5 20.2 %copy-start.147 = (s32[1,3]{1,0:T(1,128)S(1)}, s32[1,3]{1,0:T(1,128)}, u32[]{:S(2)}) copy-start(s32[1,3]{1,0:T(1,128)} %param.29) | copy-start | bytes 40
  31.5 26.8 %copy-start.92 = (bf16[1024,32]{0,1:T(8,128)(2,1)S(1)}, bf16[1024,32]{0,1:T(8,128)(2,1)}, u32[]{:S(2)}) copy-start(bf16[1024,32]{0,1:T(8,128)(2,1)} %param.33) | copy-start | bytes 196612
  31.5 35.0 %copy-start.146 = (s32[1,3]{1,0:T(1,128)S(1)}, s32[1,3]{1,0:T(1,128)}, u32[]{:S(2)}) copy-start(s32[1,3]{1,0:T(1,128)} %param.30) | copy-start | bytes 40
  31.6 35.1 %copy-start.105 = (f32[4,2304]{1,0:T(4,128)S(1)}, f32[4,2304]{1,0:T(4,128)}, u32[]{:S(2)}) copy-start(f32[4,2304]{1,0:T(4,128)} %param.38) | copy-start | bytes 110596
  31.6 35.2 %copy-start.148 = (f32[32]{0:T(128)S(1)}, f32[32]{0:T(128)}, u32[]{:S(2)}) copy-start(f32[32]{0:T(128)} %param.41) | copy-start | bytes 388
  31.6 51.3 %all-to-all-start = ((bf16[8,128,1024]{2,1,0:T(8,128)(2,1)}), bf16[8,128,1024]{2,1,0:T(8,128)(2,1)S(1)}, u32[]{:S(2)}, u32[]{:S(2)}) async-start(bf16[8,128,1024]{2,1,0:T(8,128)(2,1)} %bitcast.267), calls=%async_computation | async-start | bytes 4194304 | tf_op jit(solution)/shard_map/all_to_all | solution.py:102
  38.0 241.4 %all-gather.13.cloned.1.call-start = ((), (), s32[]{:S(2)}) async-start(), calls=%async_computation.11 | async-start | bytes 5242880 | tf_op jit(solution)/shard_map/all_gather | solution.py:132
  38.7 275.9 %all-gather.11.cloned.1.call-start = ((), (), s32[]{:S(2)}) async-start(), calls=%async_computation.10 | async-start | bytes 4718592 | tf_op jit(solution)/shard_map/all_gather | solution.py:29
  52.9 35.4 %copy-start.97 = (f32[4,256]{1,0:T(4,128)}, f32[4,256]{1,0:T(4,128)S(1)}, u32[]{:S(2)}) copy-start(f32[4,256]{1,0:T(4,128)S(1)} %get-tuple-element.340) | copy-start | bytes 12292
  53.3 82.4 %copy-start.32 = (f32[4,256]{0,1:T(8,128)}, f32[4,256]{0,1:T(8,128)S(1)}, u32[]{:S(2)}) copy-start(f32[4,256]{0,1:T(8,128)S(1)} %copy.343) | copy-start | bytes 12292
  66.1 28.1 %copy-start.52 = (bf16[1024,128]{0,1:T(8,128)(2,1)}, bf16[1024,128]{0,1:T(8,128)(2,1)S(1)}, u32[]{:S(2)}) copy-start(bf16[1024,128]{0,1:T(8,128)(2,1)S(1)} %all_gather.33) | copy-start | bytes 786436
  66.1 28.1 %copy-start.151 = (s32[128]{0:T(128)}, s32[128]{0:T(128)S(1)}, u32[]{:S(2)}) copy-start(s32[128]{0:T(128)S(1)} %and_select_fusion) | copy-start | bytes 1540
  66.3 68.7 %copy-start.129 = (f32[4]{0:T(128)}, f32[4]{0:T(128)S(1)}, u32[]{:S(2)}) copy-start(f32[4]{0:T(128)S(1)} %slice_reduce_fusion.5) | copy-start | bytes 52
  66.6 27.6 %copy-start.132 = (s32[1024]{0:T(1024)}, s32[1024]{0:T(1024)S(1)}, u32[]{:S(2)}) copy-start(s32[1024]{0:T(1024)S(1)} %select_reduce_fusion) | copy-start | bytes 12292
  66.7 78.7 %copy-start.84 = (f32[2304]{0:T(1024)}, f32[2304]{0:T(1024)S(1)}, u32[]{:S(2)}) copy-start(f32[2304]{0:T(1024)S(1)} %get-tuple-element.301) | copy-start | bytes 27652
  66.8 78.7 %copy-start.86 = (f32[2304]{0:T(1024)}, f32[2304]{0:T(1024)S(1)}, u32[]{:S(2)}) copy-start(f32[2304]{0:T(1024)S(1)} %get-tuple-element.302) | copy-start | bytes 27652
  66.8 78.7 %copy-start.88 = (f32[2304]{0:T(1024)}, f32[2304]{0:T(1024)S(1)}, u32[]{:S(2)}) copy-start(f32[2304]{0:T(1024)S(1)} %get-tuple-element.304) | copy-start | bytes 27652
  66.8 78.7 %copy-start.90 = (f32[2304]{0:T(1024)}, f32[2304]{0:T(1024)S(1)}, u32[]{:S(2)}) copy-start(f32[2304]{0:T(1024)S(1)} %get-tuple-element.303) | copy-start | bytes 27652
  66.8 59.5 %copy-start.144 = (f32[32]{0:T(128)}, f32[32]{0:T(128)S(1)}, u32[]{:S(2)}) copy-start(f32[32]{0:T(128)S(1)} %exponential_negate_fusion) | copy-start | bytes 388
  66.9 78.6 %copy-start.119 = (pred[1024]{0:T(1024)(128)(4,1)}, pred[1024]{0:T(1024)(128)(4,1)S(1)}, u32[]{:S(2)}) copy-start(pred[1024]{0:T(1024)(128)(4,1)S(1)} %get-tuple-element.359) | copy-start | bytes 3076
  66.9 78.6 %copy-start.121 = (pred[1024]{0:T(1024)(128)(4,1)}, pred[1024]{0:T(1024)(128)(4,1)S(1)}, u32[]{:S(2)}) copy-start(pred[1024]{0:T(1024)(128)(4,1)S(1)} %get-tuple-element.360) | copy-start | bytes 3076
  66.9 78.6 %copy-start.123 = (pred[1024]{0:T(1024)(128)(4,1)}, pred[1024]{0:T(1024)(128)(4,1)S(1)}, u32[]{:S(2)}) copy-start(pred[1024]{0:T(1024)(128)(4,1)S(1)} %get-tuple-element.361) | copy-start | bytes 3076
  67.6 23.1 %copy-start.108 = (pred[1024]{0:T(1024)(128)(4,1)}, pred[1024]{0:T(1024)(128)(4,1)S(1)}, u32[]{:S(2)}) copy-start(pred[1024]{0:T(1024)(128)(4,1)S(1)} %get-tuple-element.384) | copy-start | bytes 3076
  67.6 211.8 %copy-start.73 = (f32[1024]{0:T(1024)}, f32[1024]{0:T(1024)S(1)}, u32[]{:S(2)}) copy-start(f32[1024]{0:T(1024)S(1)} %get-tuple-element.385) | copy-start | bytes 12292
  126.3 18.1 %copy-start.20 = (f32[4,256,32]{2,0,1:T(4,128)}, f32[4,256,32]{2,0,1:T(4,128)S(1)}, u32[]{:S(2)}) copy-start(f32[4,256,32]{2,0,1:T(4,128)S(1)} %copy.330) | copy-start | bytes 393220
  131.5 13.7 %collective-permute-start = (bf16[3,2304]{1,0:T(4,128)(2,1)S(1)}, bf16[3,2304]{1,0:T(4,128)(2,1)S(1)}, u32[]{:S(2)}, u32[]{:S(2)}) collective-permute-start(bf16[3,2304]{1,0:T(4,128)(2,1)S(1)} %copy.326), channel_id=1, source_target_pairs={{0,1},{1,2},{2,3},{3,4},{4,5},{5,6},{6,7},{8,9},{9,10},{10,11},{11... | collective-permute-start | bytes 41480 | tf_op jit(solution)/shard_map/ppermute | solution.py:23
  135.7 52.6 %copy-start.112 = (f32[32]{0:T(128)}, f32[32]{0:T(128)S(1)}, u32[]{:S(2)}) copy-start(f32[32]{0:T(128)S(1)} %get-tuple-element.369) | copy-start | bytes 388
  135.7 52.6 %copy-start.114 = (f32[32]{0:T(128)}, f32[32]{0:T(128)S(1)}, u32[]{:S(2)}) copy-start(f32[32]{0:T(128)S(1)} %get-tuple-element.368) | copy-start | bytes 388
  135.7 52.6 %copy-start.126 = (f32[32]{0:T(128)}, f32[32]{0:T(128)S(1)}, u32[]{:S(2)}) copy-start(f32[32]{0:T(128)S(1)} %get-tuple-element.370) | copy-start | bytes 388
  145.2 39.6 %copy-start.75 = (f32[4,256,32]{1,2,0:T(8,128)}, f32[4,256,32]{1,2,0:T(8,128)S(1)}, u32[]{:S(2)}) copy-start(f32[4,256,32]{1,2,0:T(8,128)S(1)} %copy.344) | copy-start | bytes 393220
  191.5 79.2 %all-to-all-start.2 = ((bf16[8,128,1024]{2,1,0:T(8,128)(2,1)}), bf16[8,128,1024]{2,1,0:T(8,128)(2,1)S(1)}, u32[]{:S(2)}, u32[]{:S(2)}) async-start(bf16[8,128,1024]{2,1,0:T(8,128)(2,1)} %bitcast.265), calls=%async_computation.2 | async-start | bytes 4194304 | tf_op jit(solution)/shard_map/all_to_all | solution.py:103
  198.3 285.9 %all-gather.15.cloned.1.call-start = ((), (), s32[]{:S(2)}) async-start(), calls=%async_computation.12 | async-start | bytes 4718592 | tf_op jit(solution)/shard_map/all_gather | solution.py:29
  411.3 33.3 %copy-start.37 = (bf16[4,256,128]{2,1,0:T(8,128)(2,1)S(1)}, bf16[4,256,128]{2,1,0:T(8,128)(2,1)}, u32[]{:S(2)}) copy-start(bf16[4,256,128]{2,1,0:T(8,128)(2,1)} %copy-done.36) | copy-start | bytes 786436
  411.3 33.3 %copy-start.59 = (f32[4,256,128]{2,1,0:T(8,128)S(1)}, f32[4,256,128]{2,1,0:T(8,128)}, u32[]{:S(2)}) copy-start(f32[4,256,128]{2,1,0:T(8,128)} %fusion.72) | copy-start | bytes 1572868
  549.5 16.9 %copy-start.85 = (f32[2304]{0:T(1024)S(1)}, f32[2304]{0:T(1024)}, u32[]{:S(2)}) copy-start(f32[2304]{0:T(1024)} %copy-done.84) | copy-start | bytes 27652
  549.5 16.9 %copy-start.87 = (f32[2304]{0:T(1024)S(1)}, f32[2304]{0:T(1024)}, u32[]{:S(2)}) copy-start(f32[2304]{0:T(1024)} %copy-done.86) | copy-start | bytes 27652
  549.5 16.9 %copy-start.89 = (f32[2304]{0:T(1024)S(1)}, f32[2304]{0:T(1024)}, u32[]{:S(2)}) copy-start(f32[2304]{0:T(1024)} %copy-done.88) | copy-start | bytes 27652
  549.5 16.9 %copy-start.120 = (pred[1024]{0:T(1024)(128)(4,1)S(1)}, pred[1024]{0:T(1024)(128)(4,1)}, u32[]{:S(2)}) copy-start(pred[1024]{0:T(1024)(128)(4,1)} %copy-done.119) | copy-start | bytes 3076
  549.5 16.9 %copy-start.122 = (pred[1024]{0:T(1024)(128)(4,1)S(1)}, pred[1024]{0:T(1024)(128)(4,1)}, u32[]{:S(2)}) copy-start(pred[1024]{0:T(1024)(128)(4,1)} %copy-done.121) | copy-start | bytes 3076
  549.6 16.9 %copy-start.124 = (pred[1024]{0:T(1024)(128)(4,1)S(1)}, pred[1024]{0:T(1024)(128)(4,1)}, u32[]{:S(2)}) copy-start(pred[1024]{0:T(1024)(128)(4,1)} %copy-done.123) | copy-start | bytes 3076
  582.5 17.7 %copy-start.79 = (f32[4,256,32]{1,2,0:T(8,128)S(1)}, f32[4,256,32]{1,2,0:T(8,128)}, u32[]{:S(2)}) copy-start(f32[4,256,32]{1,2,0:T(8,128)} %get-tuple-element.380) | copy-start | bytes 393220
  582.5 17.9 %copy-start.19 = (f32[4,32,256]{1,0,2:T(4,128)S(1)}, f32[4,32,256]{1,0,2:T(4,128)}, u32[]{:S(2)}) copy-start(f32[4,32,256]{1,0,2:T(4,128)} %copy-done.18) | copy-start | bytes 393220
  582.5 17.9 %copy-start.21 = (f32[4,256,32]{2,0,1:T(4,128)S(1)}, f32[4,256,32]{2,0,1:T(4,128)}, u32[]{:S(2)}) copy-start(f32[4,256,32]{2,0,1:T(4,128)} %copy-done.20) | copy-start | bytes 393220
  582.5 17.9 %copy-start.33 = (f32[4,256]{0,1:T(8,128)S(1)}, f32[4,256]{0,1:T(8,128)}, u32[]{:S(2)}) copy-start(f32[4,256]{0,1:T(8,128)} %copy-done.32) | copy-start | bytes 12292
  582.5 17.9 %copy-start.96 = (f32[4,32]{1,0:T(4,128)S(1)}, f32[4,32]{1,0:T(4,128)}, u32[]{:S(2)}) copy-start(f32[4,32]{1,0:T(4,128)} %copy-done.95) | copy-start | bytes 1540
  582.5 18.3 %copy-start.130 = (f32[4]{0:T(128)S(1)}, f32[4]{0:T(128)}, u32[]{:S(2)}) copy-start(f32[4]{0:T(128)} %copy-done.129) | copy-start | bytes 52
  582.5 18.3 %copy-start.138 = (f32[32]{0:T(128)S(1)}, f32[32]{0:T(128)}, u32[]{:S(2)}) copy-start(f32[32]{0:T(128)} %get-tuple-element.297) | copy-start | bytes 388
  582.5 18.3 %copy-start.139 = (f32[32]{0:T(128)S(1)}, f32[32]{0:T(128)}, u32[]{:S(2)}) copy-start(f32[32]{0:T(128)} %get-tuple-element.298) | copy-start | bytes 388
  582.5 18.3 %copy-start.140 = (f32[32]{0:T(128)S(1)}, f32[32]{0:T(128)}, u32[]{:S(2)}) copy-start(f32[32]{0:T(128)} %get-tuple-element.299) | copy-start | bytes 388
  582.5 18.3 %copy-start.141 = (f32[32]{0:T(128)S(1)}, f32[32]{0:T(128)}, u32[]{:S(2)}) copy-start(f32[32]{0:T(128)} %get-tuple-element.300) | copy-start | bytes 388
  596.6 17.3 %copy-start.42 = (f32[4,32,256]{1,0,2:T(4,128)S(1)}, f32[4,32,256]{1,0,2:T(4,128)}, u32[]{:S(2)}) copy-start(f32[4,32,256]{1,0,2:T(4,128)} %copy.365) | copy-start | bytes 393220
  596.6 17.3 %copy-start.145 = (f32[32]{0:T(128)S(1)}, f32[32]{0:T(128)}, u32[]{:S(2)}) copy-start(f32[32]{0:T(128)} %copy-done.144) | copy-start | bytes 388
  596.6 26.5 %collective-permute-start.1 = (f32[3,2304]{1,0:T(4,128)S(1)}, f32[3,2304]{1,0:T(4,128)S(1)}, u32[]{:S(2)}, u32[]{:S(2)}) collective-permute-start(f32[3,2304]{1,0:T(4,128)S(1)} %copy.362), channel_id=1, source_target_pairs={{1,0},{2,1},{3,2},{4,3},{5,4},{6,5},{7,6},{9,8},{10,9},{11,10},{12... | collective-permute-start | bytes 82952 | tf_op jit(solution)/shard_map/ppermute | solution.py:23
  615.7 23.6 %copy-start.93 = (bf16[1024,32]{0,1:T(8,128)(2,1)}, bf16[1024,32]{0,1:T(8,128)(2,1)S(1)}, u32[]{:S(2)}) copy-start(bf16[1024,32]{0,1:T(8,128)(2,1)S(1)} %fusion.99) | copy-start | bytes 196612
  668.5 49.9 %all-to-all-start.1 = ((bf16[8,128,1024]{2,1,0:T(8,128)(2,1)}), bf16[8,128,1024]{2,1,0:T(8,128)(2,1)S(1)}, u32[]{:S(2)}, u32[]{:S(2)}) async-start(bf16[8,128,1024]{2,1,0:T(8,128)(2,1)} %bitcast.268), calls=%async_computation.1 | async-start | bytes 4194304 | tf_op jit(solution)/shard_map/all_to_all | solution.py:296
  673.6 62.7 %reduce-scatter.11.cloned.1.call-start = ((), (), s32[]{:S(2)}) async-start(), calls=%async_computation.16 | async-start | bytes 327680 | tf_op jit(solution)/shard_map/reduce_scatter | solution.py:323
  676.9 59.5 %reduce-scatter.9.cloned.1.call-start = ((), (), s32[]{:S(2)}) async-start(), calls=%async_computation.15 | async-start | bytes 655360 | tf_op jit(solution)/shard_map/reduce_scatter | solution.py:320
  718.5 149.4 %all-to-all-start.3 = ((bf16[8,128,1024]{2,1,0:T(8,128)(2,1)}), bf16[8,128,1024]{2,1,0:T(8,128)(2,1)}, u32[]{:S(2)}, u32[]{:S(2)}) async-start(bf16[8,128,1024]{2,1,0:T(8,128)(2,1)} %bitcast.266), calls=%async_computation.3 | async-start | bytes 4194304 | tf_op jit(solution)/shard_map/all_to_all | solution.py:299
  726.1 24.8 %reduce-scatter.5.cloned.1.call-start = ((), (), s32[]{:S(2)}) async-start(), calls=%async_computation.13 | async-start | bytes 327680 | tf_op jit(solution)/shard_map/reduce_scatter | solution.py:314
  728.9 50.9 %copy-start.104 = (s32[1024]{0:T(1024)S(1)}, s32[1024]{0:T(1024)}, u32[]{:S(2)}) copy-start(s32[1024]{0:T(1024)} %copy-done.103) | copy-start | bytes 12292
  729.0 50.9 %reduce-scatter.7.cloned.1.call-start = ((), (), s32[]{:S(2)}) async-start(), calls=%async_computation.14 | async-start | bytes 1433600 | tf_op jit(solution)/shard_map/reduce_scatter | solution.py:317
  736.2 119.8 %all-reduce.9.cloned.1.call-start = ((), (), s32[]{:S(2)}) async-start(), calls=%async_computation.17 | async-start | bytes 1097728 | tf_op jit(solution)/shard_map/psum | solution.py:308
  (106 other events, 683.4 us)
Sparse Core Ops, SparseCore 0:
  9.6 65.3 all-gather.6
  76.5 17.2 all-gather.8
  95.4 34.4 all-gather.12
  191.7 102.8 all-gather.10
  411.4 72.7 all-gather.14
  677.0 20.8 reduce-scatter.10
  701.1 21.6 reduce-scatter.8
  730.0 20.9 reduce-scatter.4
  754.3 25.5 reduce-scatter.6
  783.4 72.6 all-reduce.8
where the time goes:
time: 898 us; the launch traced here: 888 us
  waiting for transfers between devices  234 us (26%)
  other arithmetic  211 us (23%)
  matrix products  184 us (20%)
  local copies, waits for them, and re-layouts  164 us (18%)
  blocking collectives  43.5 us (5%)
  starting transfers between devices  33.3 us (4%)
  between operations  16.4 us (2%)
    psum x1, waiting for transfers between devices, local(): lax.psum(grads[0].astype(jnp.bfloat16), 'ctx').astype(jnp.float32)  71.8 us
    another operation x10, other arithmetic  55.6 us
    all_to_all x1, waiting for transfers between devices, local(): lax.all_to_all(sent_cot, 'ctx', split_axis=0, concat_axis=0, tiled=True)  54.6 us
    dot_general x6, matrix products, outer_cols(): lax.dot_general(left, right, (((1,), (1,)), ((), ())), preferred_element_...  46.5 us
    dot_general x6, matrix products, product(): return jnp.dot(left, right, preferred_element_type=jnp.float32)  42.6 us
    all_to_all x1, waiting for transfers between devices, local(): lax.all_to_all(jnp.take(result, slots, axis=0), 'ctx', split_axis=0, conc...  37 us
    dot_general x1, matrix products, local(): jnp.einsum('cthp,cshp->chts', d_mixed_low, xs_blocks, preferred_element_t...  33.3 us
    unnamed x312, local copies, waits for them, and re-layouts  30.8 us
  transfers between devices with their start and end apart: 16, of which 7 were waited for; matrix products, arithmetic and copies ran while one was open for 32% of the time, Pallas kernels for 0%

commit v1 on v0

v1 whole, which is shorter than its diff:
```python
from functools import partial

import jax
import jax.numpy as jnp
from jax import lax
from jax.experimental import pallas as pl
from jax.experimental.pallas import tpu as pltpu
from jax.sharding import PartitionSpec as P

HEADS = 32
HEAD = 64
STATE = 128
KERNEL = 4
SPAN = 256
RANK = 16
ADAPTERS = 8
SEQS = 3
CONV_CH = 2304
INNER = HEADS * HEAD
LOW = ADAPTERS * RANK
LANES = 128
HALF = SPAN // 2
EPS = 1e-05
LOG2E = 1.4426950408889634

F32 = jnp.float32
BF16 = jnp.bfloat16
MIB = 1 << 20


def nn(a, b):
    return jnp.dot(a, b, preferred_element_type=F32)


def nt(a, b):
    return lax.dot_general(a, b, (((1,), (1,)), ((), ())), preferred_element_type=F32)


def tn(a, b):
    return lax.dot_general(a, b, (((0,), (0,)), ((), ())), preferred_element_type=F32)


def iota(shape, dim):
    return lax.broadcasted_iota(jnp.int32, shape, dim)


def one_hot(cond):
    return jnp.where(cond, 1.0, 0.0).astype(BF16)


def split(v, parts):
    out = []
    for _ in range(parts):
        piece = v.astype(BF16)
        out.append(piece)
        v = v - piece.astype(F32)
    return out


def expand(v, e, parts=2):
    return sum(nn(p, e) for p in split(v, parts))


def seq_of(pos, meta):
    found = sum((pos >= meta[k]).astype(jnp.int32) for k in (1, 2, 3))
    return jnp.where(pos >= 0, found, -1)


def valid_of(pos, meta):
    return (pos < meta[3]).astype(F32)


def select_of(pos, meta):
    seq = seq_of(pos, meta)
    ids = jnp.where(seq == 0, meta[4], 0) + jnp.where(seq == 1, meta[5], 0) + jnp.where(seq == 2, meta[6], 0)
    shape = (pos.shape[0], LOW)
    return jnp.where(iota(shape, 1) // RANK == ids, 1.0, 0.0) * valid_of(pos, meta)


def sigmoid(v):
    return 1.0 / (1.0 + jnp.exp(-v))


def col_pos(meta, block, rows=SPAN):
    return meta[0] + block * SPAN + iota((rows, 1), 0)


def running_count(mask):
    width = mask.shape[1]
    tri = one_hot(iota((SPAN, SPAN), 0) <= iota((SPAN, SPAN), 1))
    pieces, before = [], jnp.zeros((mask.shape[0], 1), F32)
    for c in range(0, width, SPAN):
        part = mask[:, c : c + SPAN]
        pieces.append(nn(part.astype(BF16), tri) + before)
        before = before + jnp.sum(part, 1, keepdims=True)
    return jnp.concatenate(pieces, 1)


def two_rows(v):
    first = jnp.broadcast_to(v >> 5, (16, v.shape[1]))
    second = jnp.broadcast_to(v & 31, (16, v.shape[1]))
    row = iota((16, v.shape[1]), 0)
    return jnp.where(row == 0, first, jnp.where(row == 1, second, 0)).astype(F32).astype(BF16)


def from_two(r):
    return (r[0:1] * 32.0 + r[1:2]).astype(jnp.int32)


def send_kernel(shift, share, meta, order_ref, x_ref, out_ref, spos_ref):
    rows = x_ref.shape[0]
    own = order_ref[pl.ds(meta[7], 1), :]
    dest = own >> shift
    hot = jnp.where(iota((order_ref.shape[0], rows), 0) == dest, 1.0, 0.0)
    rank = jnp.sum(hot * (running_count(hot) - 1.0), axis=0, keepdims=True)
    spos = dest * share + rank.astype(jnp.int32)
    spos_ref[...] = spos
    x = x_ref[...]
    for t in range(0, rows, SPAN):
        hit = one_hot(iota((SPAN, rows), 0) + t == spos)
        out_ref[t : t + SPAN, :] = nn(hit, x).astype(BF16)


def invert(idx):
    width = idx.shape[1]
    values = two_rows(iota((1, width), 1))
    pieces = []
    for t in range(0, width, SPAN):
        hit = one_hot(iota((SPAN, width), 0) + t == idx)
        pieces.append(from_two(nt(values, hit)))
    return jnp.concatenate(pieces, 1)


def route_kernel(shift, share, n, meta, order_ref, spos_ref, slot_ref, where_ref, tok_ref):
    rows = spos_ref.shape[1]
    order = order_ref[...]
    mine = jnp.where(order >> shift == meta[7], 1.0, 0.0)
    slot = order & (rows - 1)
    mark = jnp.where(mine > 0.0, running_count(mine) - 1.0, -1.0).astype(jnp.int32)
    for s in range(n):
        hit = one_hot(iota((share, rows), 0) == mark[s : s + 1, :])
        slot_ref[:, s * share : (s + 1) * share] = from_two(nt(two_rows(slot[s : s + 1, :]), hit))
    where_ref[...] = invert(slot_ref[...])
    tok_ref[...] = invert(spos_ref[...])


def permute_kernel(idx_ref, x_ref, out_ref):
    hit = one_hot(iota((out_ref.shape[0], x_ref.shape[0]), 0) + pl.program_id(0) * out_ref.shape[0] == idx_ref[...])
    out_ref[...] = nn(hit, x_ref[...]).astype(BF16)


def in_kernel(meta, slot_ref, got_ref, w_ref, a_ref, b_ref, gain_ref, x_ref, hb_ref, u_ref, z_ref, raw_ref, dtr_ref):
    i = pl.program_id(0)
    rows = got_ref.shape[0]
    pos = col_pos(meta, i)
    hit = one_hot(iota((SPAN, rows), 0) + i * SPAN == slot_ref[...])
    x = nn(hit, got_ref[...]) * valid_of(pos, meta)
    x_ref[...] = x.astype(BF16)
    h = x * lax.rsqrt(jnp.mean(x * x, 1, keepdims=True) + EPS) * gain_ref[...]
    hb = h.astype(BF16)
    hb_ref[...] = hb
    u = (nn(hb, a_ref[...]) * select_of(pos, meta)).astype(BF16)
    u_ref[...] = u

    def part(lo, hi):
        return nn(hb, w_ref[:, lo:hi]) + nn(u, b_ref[:, lo:hi])

    for c in range(0, INNER, 512):
        z_ref[:, c : c + 512] = part(c, c + 512)
    for c in range(0, CONV_CH, 256):
        raw_ref[:, c : c + 256] = part(INNER + c, INNER + c + 256).astype(BF16)
    last = part(INNER + CONV_CH, INNER + CONV_CH + HEADS)
    dtr_ref[...] = jnp.concatenate([last, jnp.zeros((SPAN, LANES - HEADS), F32)], 1)


def softplus(v):
    e = jnp.exp(-jnp.abs(v))
    series = e * (1.0 - e * (0.5 - e * (1.0 / 3.0 - 0.25 * e)))
    return jnp.maximum(v, 0.0) + jnp.where(e < 0.01, series, jnp.log(1.0 + e))


def conv_kernel(
    meta, raw_ref, halo_ref, dtr_ref, cw_ref, cb_ref, bias_ref, rate_ref, e_ref,
    xs_ref, bm_ref, cm_ref, dact_ref, dt_ref, c2_ref, c2t_ref, wts_ref, reach_ref, ls_ref, carry_ref, send_ref,
    tail, state, through,
):
    i = pl.program_id(0)

    @pl.when(i == 0)
    def _():
        tail[...] = halo_ref[8:16, :].astype(F32)
        state[...] = jnp.zeros_like(state)
        through[...] = jnp.ones_like(through)

    pos = col_pos(meta, i)
    seq = seq_of(pos, meta)
    masks = [(seq_of(pos - j, meta) == seq).astype(F32) for j in range(KERNEL)]
    for c in range(0, CONV_CH, 256):
        cur = raw_ref[:, c : c + 256].astype(F32)
        ext = jnp.concatenate([tail[:, c : c + 256], cur], 0)
        acc = cb_ref[:, c : c + 256] + cw_ref[3:4, c : c + 256] * cur
        for j in range(1, KERNEL):
            moved = pltpu.roll(ext, j, 0)[8:]
            acc = acc + (cw_ref[3 - j : 4 - j, c : c + 256] * moved) * masks[j]
        sg = sigmoid(acc)
        act = acc * sg
        dact_ref[:, c : c + 256] = (sg + act * (1.0 - sg)).astype(BF16)
        act = act.astype(BF16)
        if c < INNER:
            xs_ref[:, c : c + 256] = act
        else:
            bm_ref[...] = act[:, :STATE]
            cm_ref[...] = act[:, STATE:]
        tail[:, c : c + 256] = cur[SPAN - 8 :]
    dt = softplus(dtr_ref[...] + bias_ref[...])
    dt_ref[...] = dt
    tri = one_hot(iota((SPAN, SPAN), 0) >= iota((SPAN, SPAN), 1))
    cum = sum(nn(tri, p) for p in split(dt * rate_ref[...], 3))
    cum_end = cum[SPAN - 1 : SPAN, :]
    end = meta[0] + i * SPAN + SPAN - 1
    end_same = (seq == seq_of(end, meta)).astype(F32)
    passing = (seq == seq_of(meta[0] + i * SPAN - 1, meta)).astype(F32)
    wts = jnp.exp(cum_end - cum) * dt * end_same
    wts_ref[...] = wts
    reach = jnp.exp(cum) * passing
    reach_ref[...] = reach
    c2 = cum * LOG2E
    c2_ref[...] = c2
    c2t_ref[0] = c2.T[:HEADS]
    weighted = (xs_ref[...].astype(F32) * expand(wts, e_ref[...])).astype(BF16)
    ls = tn(bm_ref[...], weighted)
    ls_ref[0] = ls
    carry = expand(jnp.broadcast_to(reach[SPAN - 1 : SPAN, :], (16, LANES)), e_ref[...], 3)[:8]
    carry_ref[0] = carry
    state[...] = state[...] * carry[0:1] + ls
    through[...] = through[...] * carry

    @pl.when(i == pl.num_programs(0) - 1)
    def _():
        send_ref[:STATE] = state[...].astype(BF16)
        send_ref[STATE:] = jnp.broadcast_to(through[0:1], (16, INNER)).astype(BF16)


def block_mask(meta, i, transposed):
    col = col_pos(meta, i)
    row = meta[0] + i * SPAN + iota((1, SPAN), 1)
    same = seq_of(col, meta) == seq_of(row, meta)
    return same & ((row >= col) if transposed else (col >= row))


def halves(x):
    lane = iota(x.shape, 1)
    zero = jnp.zeros_like(x)
    return jnp.where(lane < HEAD, x, zero), jnp.where(lane >= HEAD, x, zero)


def within_kernel(meta, xs_ref, bm_ref, cm_ref, dt_ref, c2_ref, c2t_ref, e_ref, y_ref, xdt, sc):
    i = pl.program_id(0)
    sc[...] = jnp.where(block_mask(meta, i, False), nt(cm_ref[...], bm_ref[...]), 0.0)
    xdt[...] = (xs_ref[...].astype(F32) * expand(dt_ref[...], e_ref[...])).astype(BF16)
    c2 = c2_ref[...]

    def group(g, _):
        cols = pltpu.roll(c2, LANES - 8 * g, 1)
        rows = c2t_ref[0, pl.ds(pl.multiple_of(8 * g, 8), 8), :]
        for q in range(4):
            at = pl.ds(pl.multiple_of(g * 512 + q * 128, 128), 128)
            xa, xb = halves(xdt[:, at])
            mixes = []
            for h in (2 * q, 2 * q + 1):
                col, row = cols[:, h : h + 1], rows[h : h + 1, :]

                def mix(t, s):
                    decay = jnp.exp2(jnp.minimum(col[t : t + HALF] - row[:, s : s + HALF], 0.0))
                    return (sc[t : t + HALF, s : s + HALF] * decay).astype(BF16)

                mixes.append((mix(0, 0), mix(HALF, 0), mix(HALF, HALF)))
            (a00, a10, a11), (b00, b10, b11) = mixes
            y_ref[:HALF, at] = nn(jnp.concatenate([a00, b00], 1), jnp.concatenate([xa[:HALF], xb[:HALF]], 0))
            y_ref[HALF:, at] = nn(jnp.concatenate([a10, a11, b10, b11], 1), jnp.concatenate([xa, xb], 0))
        return 0

    lax.fori_loop(0, HEADS // 8, group, 0)


CHUNK = 32


def fold_kernel(reverse, meta, part_ref, through_ref, out_ref):
    k = pl.program_id(0)
    j = pl.num_programs(0) - 1 - k if reverse else k
    reached = j > meta[7] if reverse else j < meta[7]

    @pl.when(k == 0)
    def _():
        out_ref[...] = jnp.zeros_like(out_ref)

    @pl.when(reached)
    def _():
        out_ref[...] = out_ref[...] * through_ref[0].astype(F32)[0:1] + part_ref[0].astype(F32)


def out_kernel(
    meta, y_ref, z_ref, xs_ref, cm_ref, reach_ref, x_ref, ls_ref, carry_ref, all_ref, e_ref, skip_ref, gain_ref,
    w_ref, a_ref, b_ref, where_ref,
    start_ref, next_ref, mixed_ref, nout_ref, v_ref, rstd_ref, sorted_ref,
    run, acc, proj, wide,
):
    i = pl.program_id(0)

    @pl.when(i == 0)
    def _():
        run[...] = all_ref[...]
        acc[...] = jnp.zeros_like(acc)

    start = run[...].astype(BF16)
    start_ref[0] = start
    later = run[...] * carry_ref[0, 0:1, :] + ls_ref[0]
    run[...] = later
    next_ref[0] = later.astype(BF16)
    proj[...] = nn(cm_ref[...], start)
    wide[...] = expand(reach_ref[...], e_ref[...])

    def rows_step(k, _):
        at = pl.ds(pl.multiple_of(k * CHUNK, CHUNK), CHUNK)
        total = jnp.zeros((CHUNK, LANES), F32)
        for c in range(0, INNER, 256):
            cs = slice(c, c + 256)
            mixed = y_ref[at, cs] + wide[at, cs] * proj[at, cs] + skip_ref[:, cs] * xs_ref[at, cs].astype(F32)
            mixed_ref[at, cs] = mixed
            z = z_ref[at, cs]
            gated = mixed * (z * sigmoid(z))
            wide[at, cs] = gated
            sq = gated * gated
            total = total + sq[:, :LANES] + sq[:, LANES:]
        rstd = lax.rsqrt(jnp.sum(total, 1, keepdims=True) * (1.0 / INNER) + EPS)
        rstd_ref[at, :] = jnp.broadcast_to(rstd, (CHUNK, LANES))
        for c in range(0, INNER, 256):
            cs = slice(c, c + 256)
            nout_ref[at, cs] = (wide[at, cs] * rstd * gain_ref[:, cs]).astype(BF16)
        return 0

    lax.fori_loop(0, SPAN // CHUNK, rows_step, 0)
    pos = col_pos(meta, i)
    nout = nout_ref[...]
    v = (nn(nout, a_ref[...]) * select_of(pos, meta)).astype(BF16)
    v_ref[...] = v
    branch = nn(nout, w_ref[...]) + nn(v, b_ref[...])
    result = ((x_ref[...].astype(F32) + branch) * valid_of(pos, meta)).astype(BF16)
    hit = one_hot(iota((acc.shape[0], SPAN), 0) == where_ref[...])
    acc[...] += nn(hit, result)

    @pl.when(i == pl.num_programs(0) - 1)
    def _():
        sorted_ref[...] = acc[...].astype(BF16)


def gate_back_kernel(
    meta, mixed_ref, z_ref, nout_ref, v_ref, rstd_ref, xs_ref, cm_ref, reach_ref, start_ref, carry_ref, cot_ref, slot_ref,
    e_ref, skip_ref, gain_ref, w_ref, a_ref, b_ref,
    dout_ref, dm_ref, dz_ref, rs_ref, dcm_ref, dst_ref, own_ref, gup_ref, gdown_ref,
    own, through, gup, gdown, dn, wide, hi_s, lo_s, dproj,
):
    i = pl.program_id(0)

    @pl.when(i == 0)
    def _():
        own[...] = jnp.zeros_like(own)
        through[...] = jnp.ones_like(through)
        gup[...] = jnp.zeros_like(gup)
        gdown[...] = jnp.zeros_like(gdown)

    pos = col_pos(meta, i)
    rows = cot_ref.shape[0]
    hit = one_hot(iota((SPAN, rows), 0) + i * SPAN == slot_ref[...])
    dout = (nn(hit, cot_ref[...]) * valid_of(pos, meta)).astype(BF16)
    dout_ref[...] = dout
    gup[...] += tn(v_ref[...], dout)
    dv = nt(dout, b_ref[...]).astype(BF16) * select_of(pos, meta).astype(BF16)
    gdown[...] += tn(dv, nout_ref[...])
    dn[...] = nt(dout, w_ref[...]) + nt(dv, a_ref[...])
    wide[...] = expand(reach_ref[...], e_ref[...])

    def rows_step(k, _):
        at = pl.ds(pl.multiple_of(k * CHUNK, CHUNK), CHUNK)
        rstd = rstd_ref[at, :][:, 0:1]
        total = jnp.zeros((CHUNK, LANES), F32)
        for c in range(0, INNER, 256):
            cs = slice(c, c + 256)
            z = z_ref[at, cs]
            d = dn[at, cs] * gain_ref[:, cs]
            dn[at, cs] = d
            g = d * (mixed_ref[at, cs] * (z * sigmoid(z)))
            total = total + g[:, :LANES] + g[:, LANES:]
        back = jnp.sum(total, 1, keepdims=True) * (1.0 / INNER) * rstd * rstd
        for c in range(0, INNER, 256):
            cs = slice(c, c + 256)
            z = z_ref[at, cs]
            sg = sigmoid(z)
            silu = z * sg
            mixed = mixed_ref[at, cs]
            dg = rstd * (dn[at, cs] - mixed * silu * back)
            dm = (dg * silu).astype(BF16)
            dm_ref[at, cs] = dm
            dz_ref[at, cs] = (dg * mixed * (sg + silu * (1.0 - sg))).astype(BF16)
            dm = dm.astype(F32)
            dproj[at, cs] = (dm * wide[at, cs]).astype(BF16)
            hi, lo = split(dm * (mixed - skip_ref[:, cs] * xs_ref[at, cs].astype(F32)), 2)
            hi_s[at, cs] = hi
            lo_s[at, cs] = lo
        return 0

    lax.fori_loop(0, SPAN // CHUNK, rows_step, 0)
    rs_ref[...] = nt(hi_s[...], e_ref[...]) + nt(lo_s[...], e_ref[...])
    dcm_ref[...] = nt(dproj[...], start_ref[0])
    dst = tn(cm_ref[...], dproj[...])
    dst_ref[0] = dst
    own[...] += dst * through[0:1]
    through[...] = through[...] * carry_ref[0]

    @pl.when(i == pl.num_programs(0) - 1)
    def _():
        own_ref[...] = own[...].astype(BF16)
        gup_ref[...] = gup[...].astype(BF16)
        gdown_ref[...] = gdown[...].astype(BF16)


def mix_back_kernel(
    meta, xs_ref, bm_ref, cm_ref, dm_ref, dt_ref, c2_ref, c2t_ref, dcm1_ref, e_ref,
    dxk_ref, dbm_ref, dcm_ref,
    xdt, dte, sct, dsc,
):
    i = pl.program_id(0)
    mask = block_mask(meta, i, True)
    sct[...] = jnp.where(mask, nt(bm_ref[...], cm_ref[...]), 0.0)
    dsc[...] = jnp.zeros_like(dsc)
    dte[...] = expand(dt_ref[...], e_ref[...])
    xdt[...] = (xs_ref[...].astype(F32) * dte[...]).astype(BF16)
    c2 = c2_ref[...]

    def group(g, _):
        cols = pltpu.roll(c2, LANES - 8 * g, 1)
        rows = c2t_ref[0, pl.ds(pl.multiple_of(8 * g, 8), 8), :]
        for q in range(4):
            at = pl.ds(pl.multiple_of(g * 512 + q * 128, 128), 128)
            dm = dm_ref[:, at]
            da, db = halves(dm)
            mixes = []
            for h, x in zip((2 * q, 2 * q + 1), halves(xdt[:, at])):
                col, row = cols[:, h : h + 1], rows[h : h + 1, :]
                top = nt(x[:HALF], dm)
                low = nt(x[HALF:], dm[HALF:])

                def mix(s, t, d):
                    decay = jnp.exp2(jnp.minimum(row[:, t : t + HALF] - col[s : s + HALF], 0.0))
                    dsc[s : s + HALF, t : t + HALF] += d * decay
                    return (sct[s : s + HALF, t : t + HALF] * decay).astype(BF16)

                mixes.append((mix(0, 0, top[:, :HALF]), mix(0, HALF, top[:, HALF:]), mix(HALF, HALF, low)))
            (a00, a01, a11), (b00, b01, b11) = mixes
            g_top = nn(jnp.concatenate([a00, a01, b00, b01], 1), jnp.concatenate([da, db], 0))
            g_low = nn(jnp.concatenate([a11, b11], 1), jnp.concatenate([da[HALF:], db[HALF:]], 0))
            dxk_ref[:HALF, at] = g_top * dte[:HALF, at]
            dxk_ref[HALF:, at] = g_low * dte[HALF:, at]
        return 0

    lax.fori_loop(0, HEADS // 8, group, 0)
    ds = jnp.where(mask, dsc[...], 0.0).astype(BF16)
    dbm_ref[...] = nn(ds, cm_ref[...])
    dcm_ref[...] = dcm1_ref[...] + tn(ds, bm_ref[...])


def later_kernel(
    all_ref, dst_ref, carry_ref, next_ref, e_ref, skip_ref,
    xs_ref, bm_ref, dm_ref, dxk_ref, dbm_ref, dcm_ref, wts_ref, dact_ref,
    dl_ref, dend_ref, head_ref,
    acc,
):
    i = pl.program_id(0)

    @pl.when(i == 0)
    def _():
        acc[...] = all_ref[...]

    a = acc[...]
    dl = a.astype(BF16)
    dl_ref[0] = dl
    total = jnp.sum(a * next_ref[0].astype(F32), 0, keepdims=True)
    total = jnp.broadcast_to(total, (16, INNER))
    dend_ref[0] = sum(nt(p, e_ref[...]) for p in split(total, 3))[:8]
    acc[...] = dst_ref[0] + carry_ref[0, 0:1, :] * a

    @pl.when(i == pl.num_programs(0) - 1)
    def _():
        wide = expand(wts_ref[...], e_ref[...])
        weighted = (xs_ref[...].astype(F32) * wide).astype(BF16)
        dxs = dxk_ref[...] + nn(bm_ref[...], dl) * wide + skip_ref[...] * dm_ref[...].astype(F32)
        head_ref[:, :INNER] = dxs * dact_ref[:, :INNER].astype(F32)
        dbm = dbm_ref[...] + nt(weighted, dl)
        head_ref[:, INNER : INNER + STATE] = dbm * dact_ref[:, INNER : INNER + STATE].astype(F32)
        head_ref[:, INNER + STATE :] = dcm_ref[...] * dact_ref[:, INNER + STATE :].astype(F32)


def in_back_kernel(
    meta, dl_ref, dend_ref, xs_ref, bm_ref, dm_ref, dz_ref, dxk_ref, dbm_ref, dcm_ref, wts_ref, dtr_ref, rs_ref, dact_ref,
    halo_ref, cw_ref, e_ref, skip_ref, bias_ref, rate_ref, w_ref, a_ref, b_ref, u_ref, hb_ref, x_ref, dout_ref, gain_ref,
    where_ref,
    sorted_ref, gup_ref, gdown_ref,
    head, acc, gup, gdown, wide, dacc, hi_s, lo_s, draw,
):
    k = pl.program_id(0)
    i = pl.num_programs(0) - 1 - k

    @pl.when(k == 0)
    def _():
        head[...] = halo_ref[:8, :]
        acc[...] = jnp.zeros_like(acc)
        gup[...] = jnp.zeros_like(gup)
        gdown[...] = jnp.zeros_like(gdown)

    wide[...] = expand(wts_ref[...], e_ref[...])
    dacc[:, :INNER] = nn(bm_ref[...], dl_ref[0])

    def rows_step(r, _):
        at = pl.ds(pl.multiple_of(r * CHUNK, CHUNK), CHUNK)
        for c in range(0, INNER, 256):
            cs = slice(c, c + 256)
            w = wide[at, cs]
            xs = xs_ref[at, cs].astype(F32)
            dx = dxk_ref[at, cs] + dacc[at, cs] * w
            hi, lo = split(xs * dx, 2)
            hi_s[at, cs] = hi
            lo_s[at, cs] = lo
            dx = dx + skip_ref[:, cs] * dm_ref[at, cs].astype(F32)
            dacc[at, cs] = dx * dact_ref[at, cs].astype(F32)
            draw[at, cs] = (xs * w).astype(BF16)
        return 0

    lax.fori_loop(0, SPAN // CHUNK, rows_step, 0)
    dbm = dbm_ref[...] + nt(draw[:, :INNER], dl_ref[0])
    dacc[:, INNER : INNER + STATE] = dbm * dact_ref[:, INNER : INNER + STATE].astype(F32)
    dacc[:, INNER + STATE :] = dcm_ref[...] * dact_ref[:, INNER + STATE :].astype(F32)
    csum = nt(hi_s[...], e_ref[...]) + nt(lo_s[...], e_ref[...])

    pos = col_pos(meta, i)
    seq = seq_of(pos, meta)
    masks = [(seq_of(pos + j, meta) == seq).astype(F32) for j in range(KERNEL)]
    for c in range(0, CONV_CH, 256):
        cs = slice(c, c + 256)
        cur = dacc[:, cs]
        ext = jnp.concatenate([cur, head[:, cs]], 0)
        total = cw_ref[3:4, cs] * cur
        for j in range(1, KERNEL):
            moved = pltpu.roll(ext, SPAN + 8 - j, 0)[:SPAN]
            total = total + (cw_ref[3 - j : 4 - j, cs] * moved) * masks[j]
        draw[:, cs] = total.astype(BF16)
        head[:, cs] = cur[:8]

    last = iota((SPAN, 1), 0) == SPAN - 1
    dcum = rs_ref[...] - csum + jnp.where(last, dend_ref[0, 0:1, :], 0.0)
    tri = one_hot(iota((SPAN, SPAN), 0) <= iota((SPAN, SPAN), 1))
    dsteps = sum(nn(tri, p) for p in split(dcum, 3))
    v = dtr_ref[...] + bias_ref[...]
    sg = sigmoid(v)
    e = jnp.exp(jnp.minimum(v, 0.0))
    ratio = jnp.where(v < -12.0, 1.0 - 0.5 * e, sg / jnp.maximum(softplus(v), 1e-7))
    ddt = (csum * ratio + dsteps * rate_ref[...] * sg).astype(BF16)[:, :HEADS]

    dz = dz_ref[...]
    dr = draw[...]
    u, hb = u_ref[...], hb_ref[...]
    mid, end = INNER + CONV_CH, INNER + CONV_CH + HEADS
    gup[:, :INNER] += tn(u, dz)
    gup[:, INNER:mid] += tn(u, dr)
    gup[:, mid:end] += tn(u, ddt)
    du = nt(dz, b_ref[:, :INNER]) + nt(dr, b_ref[:, INNER:mid]) + nt(ddt, b_ref[:, mid:end])
    du = du.astype(BF16) * select_of(pos, meta).astype(BF16)
    gdown[...] += tn(du, hb)
    dh = nt(dz, w_ref[:, :INNER]) + nt(dr, w_ref[:, INNER:mid]) + nt(ddt, w_ref[:, mid:end]) + nt(du, a_ref[...])
    x = x_ref[...].astype(F32)
    rstd = lax.rsqrt(jnp.mean(x * x, 1, keepdims=True) + EPS)
    g = dh * gain_ref[...]
    back = jnp.mean(g * x, 1, keepdims=True) * rstd * rstd
    dx = rstd * (g - x * back)
    dx = ((dout_ref[...].astype(F32) + dx) * valid_of(pos, meta)).astype(BF16)
    hit = one_hot(iota((acc.shape[0], SPAN), 0) == where_ref[...])
    acc[...] += nn(hit, dx)

    @pl.when(k == pl.num_programs(0) - 1)
    def _():
        sorted_ref[...] = acc[...].astype(BF16)
        gup_ref[...] = gup[...].astype(BF16)
        gdown_ref[...] = gdown[...].astype(BF16)


def shape(*dims, dtype=F32):
    return jax.ShapeDtypeStruct(dims, dtype)


def params(mib=56):
    return pltpu.CompilerParams(vmem_limit_bytes=mib * MIB)


SMEM = pl.BlockSpec(memory_space=pltpu.SMEM)


def fixed(*dims):
    return pl.BlockSpec(dims, lambda i: (0,) * len(dims), pipeline_mode=pl.Buffered(1))


def kept(*dims):
    return pl.BlockSpec(dims, lambda i: (0,) * len(dims))


def row_tile(width):
    return pl.BlockSpec((SPAN, width), lambda i: (i, 0))


def blocked(*dims):
    return pl.BlockSpec((1,) + dims, lambda i: (i,) + (0,) * len(dims))


def permute(idx, x):
    rows, width = x.shape
    return pl.pallas_call(
        permute_kernel,
        grid=(rows // SPAN,),
        in_specs=[fixed(1, rows), fixed(rows, width)],
        out_specs=row_tile(width),
        out_shape=shape(rows, width, dtype=BF16),
        compiler_params=params(),
        name="permute",
    )(idx, x)


def a2a(x):
    return lax.all_to_all(x, "ctx", split_axis=0, concat_axis=0, tiled=True)


def shift_ctx(x, by):
    n = lax.axis_size("ctx")
    return lax.ppermute(x, "ctx", [(i, i + by) for i in range(n) if 0 <= i + by < n])


def local(
    tokens, cotangent, order, lengths, adapter_ids, in_weight, out_weight, in_down, in_up, out_down, out_up,
    norm_gain, conv_weight, conv_bias, dt_bias, a_log, skip_gain, gate_gain,
):
    n = lax.axis_size("ctx")
    me = lax.axis_index("ctx")
    rows, width = tokens.shape[1:]
    nb = rows // SPAN
    share = rows // n
    log_rows = rows.bit_length() - 1
    assert rows == 1 << log_rows and rows <= 1024 and rows % SPAN == 0
    proj_w = in_weight.shape[1]

    ends = jnp.cumsum(lengths[0])
    meta = jnp.concatenate([(me * rows)[None], ends, adapter_ids[0], me[None]]).astype(jnp.int32)
    by_source = order[0].reshape(n, rows)
    by_source = jnp.pad(by_source, ((0, -n % 16), (0, 0)), constant_values=-1)

    sent, spos = pl.pallas_call(
        partial(send_kernel, log_rows, share),
        in_specs=[SMEM] + [pl.BlockSpec(memory_space=pltpu.VMEM)] * 2,
        out_shape=(shape(rows, width, dtype=BF16), shape(1, rows, dtype=jnp.int32)),
        compiler_params=params(),
        name="send_tokens",
    )(meta, by_source, tokens[0])
    got = a2a(sent)
    got_cot = a2a(permute(spos, cotangent[0]))

    w_in = lax.all_gather(in_weight, "fsdp", axis=0, tiled=True)
    a_in = lax.all_gather(in_down, "fsdp", axis=1, tiled=True)
    b_in = lax.all_gather(in_up, "fsdp", axis=0, tiled=True)
    w_out = lax.all_gather(out_weight, "fsdp", axis=0, tiled=True)
    a_out = lax.all_gather(out_down, "fsdp", axis=1, tiled=True)
    b_out = lax.all_gather(out_up, "fsdp", axis=0, tiled=True)

    slot, where, tok = pl.pallas_call(
        partial(route_kernel, log_rows, share, n),
        in_specs=[SMEM] + [pl.BlockSpec(memory_space=pltpu.VMEM)] * 2,
        out_shape=(shape(1, rows, dtype=jnp.int32),) * 3,
        compiler_params=params(),
        name="route",
    )(meta, by_source, spos)

    heads_pad = lambda v: jnp.pad(v, (0, LANES - HEADS))[None]
    e = (jnp.arange(LANES)[:, None] == jnp.arange(INNER)[None, :] // HEAD).astype(BF16)
    bias = heads_pad(dt_bias)
    rate = heads_pad(-jnp.exp(a_log))
    skip = jnp.repeat(skip_gain, HEAD)[None]
    gain = norm_gain[None]
    gate = gate_gain[None]
    cb = conv_bias[None]

    x, hb, u, z, raw, dtr = pl.pallas_call(
        in_kernel,
        grid=(nb,),
        in_specs=[
            SMEM, fixed(1, rows), fixed(rows, width), fixed(width, proj_w), fixed(width, LOW), fixed(LOW, proj_w),
            fixed(1, width),
        ],
        out_specs=[row_tile(width), row_tile(width), row_tile(LOW), row_tile(INNER), row_tile(CONV_CH), row_tile(LANES)],
        out_shape=(
            shape(rows, width, dtype=BF16), shape(rows, width, dtype=BF16), shape(rows, LOW, dtype=BF16),
            shape(rows, INNER), shape(rows, CONV_CH, dtype=BF16), shape(rows, LANES),
        ),
        compiler_params=params(),
        name="in_proj",
    )(meta, slot, got, w_in, a_in, b_in, gain)

    halo = shift_ctx(raw[rows - 16 :], 1)

    xs, bm, cm, dact, dt, c2, c2t, wts, reach, ls, carry, send = pl.pallas_call(
        conv_kernel,
        grid=(nb,),
        in_specs=[
            SMEM, row_tile(CONV_CH), fixed(16, CONV_CH), row_tile(LANES), fixed(KERNEL, CONV_CH), fixed(1, CONV_CH),
            fixed(1, LANES), fixed(1, LANES), fixed(LANES, INNER),
        ],
        out_specs=[
            row_tile(INNER), row_tile(STATE), row_tile(STATE), row_tile(CONV_CH), row_tile(LANES), row_tile(LANES),
            blocked(HEADS, SPAN), row_tile(LANES), row_tile(LANES), blocked(STATE, INNER), blocked(8, INNER),
            kept(STATE + 16, INNER),
        ],
        out_shape=(
            shape(rows, INNER, dtype=BF16), shape(rows, STATE, dtype=BF16), shape(rows, STATE, dtype=BF16),
            shape(rows, CONV_CH, dtype=BF16), shape(rows, LANES), shape(rows, LANES),
            shape(nb, HEADS, SPAN), shape(rows, LANES), shape(rows, LANES), shape(nb, STATE, INNER), shape(nb, 8, INNER),
            shape(STATE + 16, INNER, dtype=BF16),
        ),
        scratch_shapes=[pltpu.VMEM((8, CONV_CH), F32), pltpu.VMEM((STATE, INNER), F32), pltpu.VMEM((8, INNER), F32)],
        compiler_params=params(),
        name="conv_state",
    )(meta, raw, halo, dtr, conv_weight, cb, bias, rate, e)

    states = lax.all_gather(send, "ctx")

    y = pl.pallas_call(
        within_kernel,
        grid=(nb,),
        in_specs=[
            SMEM, row_tile(INNER), row_tile(STATE), row_tile(STATE), row_tile(LANES), row_tile(LANES), blocked(HEADS, SPAN),
            fixed(LANES, INNER),
        ],
        out_specs=row_tile(INNER),
        out_shape=shape(rows, INNER),
        scratch_shapes=[pltpu.VMEM((SPAN, INNER), BF16), pltpu.VMEM((SPAN, SPAN), F32)],
        compiler_params=params(),
        name="within",
    )(meta, xs, bm, cm, dt, c2, c2t, e)

    def fold(parts, reverse):
        at = (lambda k: n - 1 - k) if reverse else (lambda k: k)
        return pl.pallas_call(
            partial(fold_kernel, reverse),
            grid=(n,),
            in_specs=[
                SMEM,
                pl.BlockSpec((1, STATE, INNER), lambda k: (at(k), 0, 0)),
                pl.BlockSpec((1, 16, INNER), lambda k: (at(k), STATE // 16, 0)),
            ],
            out_specs=kept(STATE, INNER),
            out_shape=shape(STATE, INNER),
            compiler_params=params(),
            name="fold",
        )(meta, parts, states)

    start_in = fold(states, False)

    start, after, mixed, nout, v, rstd, result = pl.pallas_call(
        out_kernel,
        grid=(nb,),
        in_specs=[
            SMEM, row_tile(INNER), row_tile(INNER), row_tile(INNER), row_tile(STATE), row_tile(LANES), row_tile(width),
            blocked(STATE, INNER), blocked(8, INNER), fixed(STATE, INNER), fixed(LANES, INNER), fixed(1, INNER),
            fixed(1, INNER), fixed(INNER, width), fixed(INNER, LOW), fixed(LOW, width),
            pl.BlockSpec((1, SPAN), lambda i: (0, i)),
        ],
        out_specs=[
            blocked(STATE, INNER), blocked(STATE, INNER), row_tile(INNER), row_tile(INNER), row_tile(LOW), row_tile(LANES),
            kept(rows, width),
        ],
        out_shape=(
            shape(nb, STATE, INNER, dtype=BF16), shape(nb, STATE, INNER, dtype=BF16), shape(rows, INNER),
            shape(rows, INNER, dtype=BF16), shape(rows, LOW, dtype=BF16), shape(rows, LANES), shape(rows, width, dtype=BF16),
        ),
        scratch_shapes=[
            pltpu.VMEM((STATE, INNER), F32), pltpu.VMEM((rows, width), F32), pltpu.VMEM((SPAN, INNER), F32),
            pltpu.VMEM((SPAN, INNER), F32),
        ],
        compiler_params=params(),
        name="gate_out",
    )(meta, y, z, xs, cm, reach, x, ls, carry, start_in, e, skip, gate, w_out, a_out, b_out, where)

    back_out = a2a(result)

    dout, dm, dz, rs, dcm1, dst, own, g_up_out, g_down_out = pl.pallas_call(
        gate_back_kernel,
        grid=(nb,),
        in_specs=[
            SMEM, row_tile(INNER), row_tile(INNER), row_tile(INNER), row_tile(LOW), row_tile(LANES), row_tile(INNER),
            row_tile(STATE), row_tile(LANES), blocked(STATE, INNER), blocked(8, INNER), fixed(rows, width), fixed(1, rows),
            fixed(LANES, INNER), fixed(1, INNER), fixed(1, INNER), fixed(INNER, width), fixed(INNER, LOW), fixed(LOW, width),
        ],
        out_specs=[
            row_tile(width), row_tile(INNER), row_tile(INNER), row_tile(LANES), row_tile(STATE), blocked(STATE, INNER),
            kept(STATE, INNER), kept(LOW, width), kept(LOW, INNER),
        ],
        out_shape=(
            shape(rows, width, dtype=BF16), shape(rows, INNER, dtype=BF16), shape(rows, INNER, dtype=BF16),
            shape(rows, LANES), shape(rows, STATE), shape(nb, STATE, INNER), shape(STATE, INNER, dtype=BF16),
            shape(LOW, width, dtype=BF16), shape(LOW, INNER, dtype=BF16),
        ),
        scratch_shapes=[
            pltpu.VMEM((STATE, INNER), F32), pltpu.VMEM((8, INNER), F32), pltpu.VMEM((LOW, width), F32),
            pltpu.VMEM((LOW, INNER), F32), pltpu.VMEM((SPAN, INNER), F32), pltpu.VMEM((SPAN, INNER), F32),
            pltpu.VMEM((SPAN, INNER), BF16), pltpu.VMEM((SPAN, INNER), BF16), pltpu.VMEM((SPAN, INNER), BF16),
        ],
        compiler_params=params(),
        name="gate_back",
    )(meta, mixed, z, nout, v, rstd, xs, cm, reach, start, carry, got_cot, slot, e, skip, gate, w_out, a_out, b_out)

    states_back = lax.all_gather(own, "ctx")
    later_in = fold(states_back, True)

    dxk, dbm, dcm = pl.pallas_call(
        mix_back_kernel,
        grid=(nb,),
        in_specs=[
            SMEM, row_tile(INNER), row_tile(STATE), row_tile(STATE), row_tile(INNER), row_tile(LANES), row_tile(LANES),
            blocked(HEADS, SPAN), row_tile(STATE), fixed(LANES, INNER),
        ],
        out_specs=[row_tile(INNER), row_tile(STATE), row_tile(STATE)],
        out_shape=(shape(rows, INNER), shape(rows, STATE), shape(rows, STATE)),
        scratch_shapes=[
            pltpu.VMEM((SPAN, INNER), BF16), pltpu.VMEM((SPAN, INNER), F32), pltpu.VMEM((SPAN, SPAN), F32),
            pltpu.VMEM((SPAN, SPAN), F32),
        ],
        compiler_params=params(),
        name="mix_back",
    )(meta, xs, bm, cm, dm, dt, c2, c2t, dcm1, e)

    back = lambda *dims: pl.BlockSpec((1,) + dims, lambda i: (nb - 1 - i,) + (0,) * len(dims))
    dl, dend, head = pl.pallas_call(
        later_kernel,
        grid=(nb,),
        in_specs=[
            fixed(STATE, INNER), back(STATE, INNER), back(8, INNER), back(STATE, INNER),
            fixed(LANES, INNER), fixed(1, INNER), fixed(16, INNER), fixed(16, STATE), fixed(16, INNER), fixed(16, INNER),
            fixed(16, STATE), fixed(16, STATE), fixed(16, LANES), fixed(16, CONV_CH),
        ],
        out_specs=[back(STATE, INNER), back(8, LANES), kept(16, CONV_CH)],
        out_shape=(shape(nb, STATE, INNER, dtype=BF16), shape(nb, 8, LANES), shape(16, CONV_CH)),
        scratch_shapes=[pltpu.VMEM((STATE, INNER), F32)],
        compiler_params=params(),
        name="later_state",
    )(later_in, dst, carry, after, e, skip, xs, bm, dm, dxk, dbm, dcm, wts, dact)

    from_next = shift_ctx(head, -1)

    tile = lambda w: pl.BlockSpec((SPAN, w), lambda i: (nb - 1 - i, 0))
    grad, g_up_in, g_down_in = pl.pallas_call(
        in_back_kernel,
        grid=(nb,),
        in_specs=[
            SMEM, back(STATE, INNER), back(8, LANES), tile(INNER), tile(STATE), tile(INNER), tile(INNER), tile(INNER),
            tile(STATE), tile(STATE), tile(LANES), tile(LANES), tile(LANES), tile(CONV_CH), fixed(16, CONV_CH),
            fixed(KERNEL, CONV_CH), fixed(LANES, INNER), fixed(1, INNER), fixed(1, LANES), fixed(1, LANES),
            fixed(width, proj_w), fixed(width, LOW), fixed(LOW, proj_w), tile(LOW), tile(width), tile(width), tile(width),
            fixed(1, width), pl.BlockSpec((1, SPAN), lambda i: (0, nb - 1 - i)),
        ],
        out_specs=[kept(rows, width), kept(LOW, proj_w), kept(LOW, width)],
        out_shape=(
            shape(rows, width, dtype=BF16), shape(LOW, proj_w, dtype=BF16), shape(LOW, width, dtype=BF16),
        ),
        scratch_shapes=[
            pltpu.VMEM((8, CONV_CH), F32), pltpu.VMEM((rows, width), F32), pltpu.VMEM((LOW, proj_w), F32),
            pltpu.VMEM((LOW, width), F32), pltpu.VMEM((SPAN, INNER), F32), pltpu.VMEM((SPAN, CONV_CH), F32),
            pltpu.VMEM((SPAN, INNER), BF16), pltpu.VMEM((SPAN, INNER), BF16), pltpu.VMEM((SPAN, CONV_CH), BF16),
        ],
        compiler_params=params(60),
        name="in_back",
    )(
        meta, dl, dend, xs, bm, dm, dz, dxk, dbm, dcm, wts, dtr, rs, dact, from_next, conv_weight, e, skip, bias, rate,
        w_in, a_in, b_in, u, hb, x, dout, gain, where,
    )

    back_grad = a2a(grad)

    def reduced(g):
        part = lax.psum_scatter(g, "fsdp", scatter_dimension=0, tiled=True)
        return lax.psum(part, "ctx").astype(F32)

    g_out = reduced(jnp.concatenate([g_down_out, g_up_out], 1))
    g_in = reduced(jnp.concatenate([g_down_in, g_up_in], 1))
    block_output = permute(tok, back_out)[None]
    input_grad = permute(tok, back_grad)[None]
    return (block_output, input_grad, g_in[:, :width].T, g_in[:, width:], g_out[:, :INNER].T, g_out[:, INNER:])


def solution(mesh):
    placed = (
        P("fsdp", "ctx", None),
        P("fsdp", "ctx", None),
        P("fsdp", None),
        P("fsdp", None),
        P("fsdp", None),
        P("fsdp", None),
        P("fsdp", None),
        P(None, "fsdp"),
        P("fsdp", None),
        P(None, "fsdp"),
        P("fsdp", None),
        P(),
        P(),
        P(),
        P(),
        P(),
        P(),
        P(),
    )
    return jax.shard_map(
        local,
        mesh=mesh,
        in_specs=placed,
        out_specs=(
            P("fsdp", "ctx", None),
            P("fsdp", "ctx", None),
            P(None, "fsdp"),
            P("fsdp", None),
            P(None, "fsdp"),
            P("fsdp", None),
        ),
        check_vma=False,
    )
```

time: 898 us -> 699 us (0.78)
  Pallas kernels: 0 us -> 257 us
  other arithmetic: 211 us -> 6.86 us
  matrix products: 184 us -> 0 us
  local copies, waits for them, and re-layouts: 164 us -> 19.3 us
  waiting for transfers between devices: 234 us -> 329 us
  blocking collectives: 43.5 us -> 18.6 us
  starting transfers between devices: 33.3 us -> 42.4 us
    pallas_call x0 -> x15, Pallas kernels: none -> 257 us  [the longest x1 60.9 us: local(): pl.pallas_call(in_back_kernel, grid=(nb,), in_specs=[SMEM, back(STATE, IN...]
    dot_general x28 -> x0, matrix products: 184 us -> none  [the longest x6 46.5 us: outer_cols(): lax.dot_general(left, right, (((1,), (1,)), ((), ())), preferred_element_...]
    all_gather x5, waiting for transfers between devices: 9.87 us -> 184 us  [the longest x1 68.5 us: local(): states = lax.all_gather(send, 'ctx')]
    all_to_all x4, waiting for transfers between devices: 107 us -> 33.3 us  [a2a(): return lax.all_to_all(x, 'ctx', split_axis=0, concat_axis=0, tiled=True)]
    another operation x14 -> x1, other arithmetic: 59.7 us -> 0.18 us
    gather x9 -> x0, local copies, waits for them, and re-layouts: 54.8 us -> none  [the longest x1 8.32 us: local(): sent_tokens = jnp.take(tokens[0], send_order, axis=0)]
    select_n x24 -> x1, other arithmetic: 30.7 us -> 0.01 us  [local(): jnp.arange(INNER)[None, :] // HEAD]
    mul x8 -> x0, other arithmetic: 27.8 us -> none  [the longest x2 26.4 us: conv_fn(): joined[tap:tap + rows] * conv_weight[tap]]
  transfers between devices with their start and end apart: 16 -> 14, of which waited for: 7 -> 9; matrix products, arithmetic and copies ran while one was open for 32% -> 3% of each run, Pallas kernels for 0% -> 24%
where the time goes in v1:
time: 699 us; the launch traced here: 688 us
  waiting for transfers between devices  329 us (47%)
  Pallas kernels  257 us (37%)
  starting transfers between devices  42.4 us (6%)
  local copies, waits for them, and re-layouts  19.3 us (3%)
  blocking collectives  18.6 us (3%)
  between operations  14.5 us (2%)
    psum x1, waiting for transfers between devices, reduced(): return lax.psum(part, 'ctx').astype(F32)  82.2 us
    all_gather x1, waiting for transfers between devices, local(): states = lax.all_gather(send, 'ctx')  68.5 us
    all_gather x1, waiting for transfers between devices, local(): states_back = lax.all_gather(own, 'ctx')  62.9 us
    pallas_call x1, Pallas kernels, local(): pl.pallas_call(in_back_kernel, grid=(nb,), in_specs=[SMEM, back(STATE, IN...  60.9 us
    pallas_call x1, Pallas kernels, local(): pl.pallas_call(gate_back_kernel, grid=(nb,), in_specs=[SMEM, row_tile(INN...  41.5 us
    all_to_all x4, waiting for transfers between devices, a2a(): return lax.all_to_all(x, 'ctx', split_axis=0, concat_axis=0, tiled=True)  33.3 us
    all_gather x1, waiting for transfers between devices, local(): w_out = lax.all_gather(out_weight, 'fsdp', axis=0, tiled=True)  32.6 us
    pallas_call x1, Pallas kernels, local(): pl.pallas_call(out_kernel, grid=(nb,), in_specs=[SMEM, row_tile(INNER), r...  29.7 us
  transfers between devices with their start and end apart: 14, of which 9 were waited for; matrix products, arithmetic and copies ran while one was open for 3% of the time, Pallas kernels for 24%

profile of v1, /device:TPU:10, one launch (start us, length us, event | category | flops | bytes accessed | tf_op | source)
XLA Modules:
  0.0 687.6 jit_solution(16834743976516577468)
XLA Ops:
  7.2 0.7 all-gather.10.cloned.1.call-update
  7.9 0.0 all-gather.8.cloned.1.call-start
  7.9 4.2 copy.27
  12.2 0.6 copy-done.16
  12.8 0.2 reduce-window.9
  13.0 0.5 broadcast.45
  13.5 0.7 reduce.3
  14.2 0.6 pad.11.order_ref
  14.9 0.6 pad_add_fusion.meta
  15.5 5.5 send_tokens.1
  21.0 6.4 all-to-all-start
  27.4 0.6 broadcast_in_dim.35.cb_ref
  28.0 5.8 all_gather.31
  33.8 0.8 copy.28.a_ref
  34.6 3.5 route.1
  38.1 0.9 fusion.e_ref
  39.0 33.3 %all-to-all-done = bf16[8,128,1024]{2,1,0:T(8,128)(2,1)S(1)} async-done(((bf16[8,128,1024]{2,1,0:T(8,128)(2,1)}), bf16[8,128,1024]{2,1,0:T(8,128)(2,1)S(1)}, u32[]{:S(2)}, u32[]{:S(2)}) %all-to-all-start) | async-done | bytes 2097184 | tf_op jit(solution)/shard_map/all_to_all | solution.py:637
  72.3 20.0 %all-gather.8.cloned.1.call-done.w_ref = bf16[1024,4384]{1,0:T(8,128)(2,1)} async-done(((bf16[256,4384]{1,0:T(8,128)(2,1)}), bf16[1024,4384]{1,0:T(8,128)(2,1)}) %all-gather.8.cloned.1.call-update) | async-done | bytes 8978448 | tf_op jit(solution)/shard_map/all_gather | solution.py:673
  92.4 23.1 %in_proj.1 = (bf16[1024,1024]{1,0:T(8,128)(2,1)}, bf16[1024,1024]{1,0:T(8,128)(2,1)}, bf16[1024,128]{1,0:T(8,128)(2,1)}, f32[1024,2048]{1,0:T(8,128)}, bf16[1024,2304]{1,0:T(8,128)(2,1)}, /*index=5*/f32[1024,128]{1,0:T(8,128)}) custom-call(s32[8]{0:T(128)} %pad_add_fusion.meta, s32[1,1024]{1,0:T(1,128)} %get-tuple-element.56.slot_ref, ...), custom_call_target="tpu_custom_call" | custom-call | tf_op jit(solution)/shard_map/in_proj/pallas_call | solution.py:697
  115.5 0.9 slice.15
  116.3 3.4 collective-permute-start
  119.7 0.5 pad_bitcast_fusion
  120.3 2.4 collective-permute-done.halo_ref
  122.6 0.6 copy-done.8
  123.3 19.5 %conv_state.1 = (bf16[1024,2048]{1,0:T(8,128)(2,1)}, bf16[1024,128]{1,0:T(8,128)(2,1)}, bf16[1024,128]{1,0:T(8,128)(2,1)}, bf16[1024,2304]{1,0:T(8,128)(2,1)}, f...) custom-call(s32[8]{0:T(128)} %pad_add_fusion.meta, ...), custom_call_target="tpu_custom_call" | custom-call | tf_op jit(solution)/shard_map/conv_state/pallas_call | solution.py:715
  142.8 0.3 all-gather.12.cloned.1.call-start
  143.1 0.3 all-gather.12.cloned.1.call-update
  143.3 5.4 permute.4
  148.7 6.2 all-to-all-start.2
  154.9 0.1 broadcast_in_dim.38
  155.0 0.7 broadcast_in_dim_reshape.3.skip_ref
  155.7 6.5 all_gather.36
  162.2 1.0 copy.29.a_ref
  163.2 6.3 all_gather.37.b_ref
  169.5 16.2 %within.1.y_ref = f32[1024,2048]{1,0:T(8,128)} custom-call(s32[8]{0:T(128)} %pad_add_fusion.meta, bf16[1024,2048]{1,0:T(8,128)(2,1)} %get-tuple-element.60.xs_ref, bf16[1024,128]{1,0:T(8,128)(2,1)} %get-tuple-element.61.bm_ref, bf16[1024,128]{1,0:T(8,128)(2,1)} %get-tuple-element.62.cm_ref, f32[1024,128]{1,0:T(8,128)} %get-tuple-element.63.dt_ref, ...), custom_call_target="tpu_custom_call" | custom-call | tf_op jit(solution)/shard_map/within/pallas_call | solution.py:740
  185.7 68.5 %all-gather.14.cloned.1.call-done = bf16[1152,2048]{1,0:T(8,128)(2,1)} async-done(((bf16[144,2048]{1,0:T(8,128)(2,1)}), bf16[1152,2048]{1,0:T(8,128)(2,1)}) %all-gather.14.cloned.1.call-update) | async-done | bytes 4718608 | tf_op jit(solution)/shard_map/all_gather | solution.py:738
  254.2 5.8 fold.2.all_ref
  260.0 32.6 %all-gather.12.cloned.1.call-done.w_ref = bf16[2048,1024]{1,0:T(8,128)(2,1)} async-done(((bf16[512,1024]{1,0:T(8,128)(2,1)}), bf16[2048,1024]{1,0:T(8,128)(2,1)}) %all-gather.12.cloned.1.call-update) | async-done | bytes 4194320 | tf_op jit(solution)/shard_map/all_gather | solution.py:676
  292.6 29.7 %gate_out.1 = (bf16[4,128,2048]{2,1,0:T(8,128)(2,1)}, bf16[4,128,2048]{2,1,0:T(8,128)(2,1)}, f32[1024,2048]{1,0:T(8,128)}, bf16[1024,2048]{1,0:T(8,128)(2,1)}, b...) custom-call(s32[8]{0:T(128)} %pad_add_fusion.meta, f32[1024,2048]{1,0:T(8,128)} %within.1.y_ref, ...), custom_call_target="tpu_custom_call" | custom-call | tf_op jit(solution)/shard_map/gate_out/pallas_call | solution.py:772
  322.3 1.3 copy-done
  323.6 41.5 %gate_back.1 = (bf16[1024,1024]{1,0:T(8,128)(2,1)}, bf16[1024,2048]{1,0:T(8,128)(2,1)}, bf16[1024,2048]{1,0:T(8,128)(2,1)}, f32[1024,128]{1,0:T(8,128)}, f32[102...) custom-call(s32[8]{0:T(128)} %pad_add_fusion.meta, ...), custom_call_target="tpu_custom_call" | custom-call | tf_op jit(solution)/shard_map/gate_back/pallas_call | solution.py:799
  365.1 6.2 all-to-all-start.1
  371.3 0.9 pad_maximum_fusion.1
  372.3 10.2 %reduce-scatter.3.cloned.1.call-start = ((), (), s32[]{:S(2)}) async-start(), calls=%async_computation.9 | async-start | bytes 1761280 | tf_op jit(solution)/shard_map/reduce_scatter | solution.py:893
  382.5 22.1 %mix_back.1 = (f32[1024,2048]{1,0:T(8,128)}, f32[1024,128]{1,0:T(8,128)}, f32[1024,128]{1,0:T(8,128)}) custom-call(s32[8]{0:T(128)} %pad_add_fusion.meta, bf16[1024,2048]{1,0:T(8,128)(2,1)} %get-tuple-element.60.xs_ref, bf16[1024,128]{1,0:T(8,128)(2,1)} %get-tuple-element.61.bm_ref, bf16[1024,128]{1,0:T(8,128)(2,1)} %get-tuple-element.62.cm_ref, ...), custom_call_target="tpu_custom_call" | custom-call | tf_op jit(solution)/shard_map/mix_back/pallas_call | solution.py:828
  404.5 62.9 %all-gather.16.cloned.1.call-done = bf16[1024,2048]{1,0:T(8,128)(2,1)} async-done(((bf16[128,2048]{1,0:T(8,128)(2,1)}), bf16[1024,2048]{1,0:T(8,128)(2,1)}) %all-gather.16.cloned.1.call-update) | async-done | bytes 4194320 | tf_op jit(solution)/shard_map/all_gather | solution.py:825
  467.4 5.8 fold.3.all_ref
  473.2 7.8 %later_state.1 = (bf16[4,128,2048]{2,1,0:T(8,128)(2,1)}, f32[4,8,128]{2,1,0:T(8,128)}, f32[16,2304]{1,0:T(8,128)}) custom-call(f32[128,2048]{1,0:T(8,128)} %fold.3.all_ref, f32[4,128,2048]{2,1,0:T(8,128)} %get-tuple-element.80.dst_ref, f32[4,8,2048]{2,1,0:T(8,128)} %get-tuple-element.70.carry_ref, bf16[4,128,2048]{2,1,0:T(8,128)(2,1)} %get-tuple-element.81.next_ref, ...), custom_call_target="tpu_custom_call" | custom-call | tf_op jit(solution)/shard_map/later_state/pallas_call | solution.py:846
  481.1 2.4 collective-permute-start.1
  483.5 6.4 collective-permute-done.1.halo_ref
  489.9 0.7 copy-done.6
  490.5 60.9 %in_back.1 = (bf16[1024,1024]{1,0:T(8,128)(2,1)}, bf16[128,4384]{1,0:T(8,128)(2,1)}, bf16[128,1024]{1,0:T(8,128)(2,1)}) custom-call(s32[8]{0:T(128)} %pad_add_fusion.meta, bf16[4,128,2048]{2,1,0:T(8,128)(2,1)} %get-tuple-element.89.dl_ref, f32[4,8,128]{2,1,0:T(8,128)} %get-tuple-element.90.dend_ref, bf16[1024,2048]{1,0:T(8,128)(2,1)} %get-tuple-element.60.xs_ref, ...), custom_call_target="tpu_custom_call" | custom-call | tf_op jit(solution)/shard_map/in_back/pallas_call | solution.py:864
  551.4 2.5 pad_maximum_fusion
  553.9 1.3 copy-done.1
  555.3 7.3 %all-to-all-start.3 = ((bf16[8,128,1024]{2,1,0:T(8,128)(2,1)}), bf16[8,128,1024]{2,1,0:T(8,128)(2,1)}, u32[]{:S(2)}, u32[]{:S(2)}) async-start(bf16[8,128,1024]{2,1,0:T(8,128)(2,1)} %bitcast.42), calls=%async_computation.3 | async-start | bytes 4194304 | tf_op jit(solution)/shard_map/all_to_all | solution.py:637
  562.6 19.3 %reduce-scatter.3.cloned.1.call-done = bf16[32,5408]{1,0:T(8,128)(2,1)} async-done(((bf16[128,5408]{1,0:T(8,128)(2,1)}), bf16[32,5408]{1,0:T(8,128)(2,1)}) %reduce-scatter.3.cloned.1.call-update) | async-done | bytes 346128 | tf_op jit(solution)/shard_map/reduce_scatter | solution.py:893
  581.9 5.4 permute.3
  587.3 82.2 %all-reduce.6.cloned.1.call-done = (bf16[32,5408]{1,0:T(8,128)(2,1)}, bf16[32,3072]{1,0:T(8,128)(2,1)}) async-done(((bf16[32,5408]{1,0:T(8,128)(2,1)}, bf16[32,3072]{1,0:T(8,128)(2,1)}), (bf16[32,5408]{1,0:T(8,128)(2,1)}, bf16[32,3072]{1,0:T(8,128)(2,1)})) %all-reduce.6.cloned.1.call-update) | async-done | bytes 542736 | tf_op jit(solution)/shard_map/psum | solution.py:894
  669.5 1.6 slice.23
  671.0 1.0 convert_element_type.26
  672.0 1.8 slice.21
  673.8 0.7 slice_bitcast_fusion.1
  674.5 0.7 slice_bitcast_fusion
  675.2 5.3 permute.5
  (51 shorter events, 0.3 us)
Async XLA Ops:
  7.2 31.9 %all-gather.10.cloned.1.call-start = ((), (), s32[]{:S(2)}) async-start(), calls=%async_computation.7 | async-start | bytes 1433600 | tf_op jit(solution)/shard_map/all_gather | solution.py:675
  7.9 84.5 %all-gather.8.cloned.1.call-start = ((), (), s32[]{:S(2)}) async-start(), calls=%async_computation.6 | async-start | bytes 11468800 | tf_op jit(solution)/shard_map/all_gather | solution.py:673
  12.2 0.7 copy-start.16
  12.2 1.3 copy-start.11
  12.2 2.7 copy-start.13
  21.0 6.4 copy-start.12
  21.0 7.0 %copy-start.9 = (bf16[1024,32]{0,1:T(8,128)(2,1)S(1)}, bf16[1024,32]{0,1:T(8,128)(2,1)}, u32[]{:S(2)}) copy-start(bf16[1024,32]{0,1:T(8,128)(2,1)} %param.25) | copy-start | bytes 196612
  21.0 17.1 %copy-start.17 = (f32[32]{0:T(128)S(1)}, f32[32]{0:T(128)}, u32[]{:S(2)}) copy-start(f32[32]{0:T(128)} %param.33) | copy-start | bytes 388
  21.0 51.3 %all-to-all-start = ((bf16[8,128,1024]{2,1,0:T(8,128)(2,1)}), bf16[8,128,1024]{2,1,0:T(8,128)(2,1)S(1)}, u32[]{:S(2)}, u32[]{:S(2)}) async-start(bf16[8,128,1024]{2,1,0:T(8,128)(2,1)} %bitcast.43), calls=%async_computation | async-start | bytes 4194304 | tf_op jit(solution)/shard_map/all_to_all | solution.py:637
  27.4 226.8 %all-gather.14.cloned.1.call-start = ((), (), s32[]{:S(2)}) async-start(), calls=%async_computation.11 | async-start | bytes 5308416 | tf_op jit(solution)/shard_map/all_gather | solution.py:738
  72.3 20.0 %copy-start.2 = (bf16[8,128,1024]{2,1,0:T(8,128)(2,1)}, bf16[8,128,1024]{2,1,0:T(8,128)(2,1)S(1)}, u32[]{:S(2)}) copy-start(bf16[8,128,1024]{2,1,0:T(8,128)(2,1)S(1)} %all-to-all-done) | copy-start | bytes 6291460
  92.4 27.4 %copy-start.15 = (f32[32]{0:T(128)S(1)}, f32[32]{0:T(128)}, u32[]{:S(2)}) copy-start(f32[32]{0:T(128)} %param.32) | copy-start | bytes 388
  116.3 6.3 collective-permute-start
  122.6 0.6 copy-start.8
  142.8 149.8 %all-gather.12.cloned.1.call-start = ((), (), s32[]{:S(2)}) async-start(), calls=%async_computation.8 | async-start | bytes 5242880 | tf_op jit(solution)/shard_map/all_gather | solution.py:676
  148.7 6.2 copy-start.14
  148.7 7.0 %copy-start.7 = (bf16[2048,32]{0,1:T(8,128)(2,1)S(1)}, bf16[2048,32]{0,1:T(8,128)(2,1)}, u32[]{:S(2)}) copy-start(bf16[2048,32]{0,1:T(8,128)(2,1)} %param.27) | copy-start | bytes 393220
  148.7 14.4 %copy-start.10 = (bf16[32,1024]{1,0:T(8,128)(2,1)S(1)}, bf16[32,1024]{1,0:T(8,128)(2,1)}, u32[]{:S(2)}) copy-start(bf16[32,1024]{1,0:T(8,128)(2,1)} %param.28) | copy-start | bytes 196612
  148.7 173.5 %all-to-all-start.2 = ((bf16[8,128,1024]{2,1,0:T(8,128)(2,1)}), bf16[8,128,1024]{2,1,0:T(8,128)(2,1)S(1)}, u32[]{:S(2)}, u32[]{:S(2)}) async-start(bf16[8,128,1024]{2,1,0:T(8,128)(2,1)} %bitcast.34), calls=%async_computation.2 | async-start | bytes 4194304 | tf_op jit(solution)/shard_map/all_to_all | solution.py:637
  154.9 312.5 %all-gather.16.cloned.1.call-start = ((), (), s32[]{:S(2)}) async-start(), calls=%async_computation.12 | async-start | bytes 4718592 | tf_op jit(solution)/shard_map/all_gather | solution.py:825
  322.3 1.3 copy-start
  365.1 6.2 copy-start.4
  365.1 6.2 copy-start.5
  365.1 188.8 %all-to-all-start.1 = ((bf16[8,128,1024]{2,1,0:T(8,128)(2,1)}), bf16[8,128,1024]{2,1,0:T(8,128)(2,1)S(1)}, u32[]{:S(2)}, u32[]{:S(2)}) async-start(bf16[8,128,1024]{2,1,0:T(8,128)(2,1)} %bitcast.41), calls=%async_computation.1 | async-start | bytes 4194304 | tf_op jit(solution)/shard_map/all_to_all | solution.py:637
  371.3 191.3 %reduce-scatter.5.cloned.1.call-start = ((), (), s32[]{:S(2)}) async-start(), calls=%async_computation.10 | async-start | bytes 983040 | tf_op jit(solution)/shard_map/reduce_scatter | solution.py:893
  372.3 209.6 %reduce-scatter.3.cloned.1.call-start = ((), (), s32[]{:S(2)}) async-start(), calls=%async_computation.9 | async-start | bytes 1761280 | tf_op jit(solution)/shard_map/reduce_scatter | solution.py:893
  481.1 8.8 %collective-permute-start.1 = (f32[16,2304]{1,0:T(8,128)}, f32[16,2304]{1,0:T(8,128)S(1)}, u32[]{:S(2)}, u32[]{:S(2)}) collective-permute-start(f32[16,2304]{1,0:T(8,128)} %get-tuple-element.93), channel_id=1, source_target_pairs={{1,0},{2,1},{3,2},{4,3},{5,4},{6,5},{7,6},{9,8},{10,9},{11,10},{12... | collective-permute-start | bytes 442376 | tf_op jit(solution)/shard_map/ppermute | solution.py:642
  489.9 0.7 copy-start.6
  553.9 1.3 copy-start.1
  555.3 120.0 %all-to-all-start.3 = ((bf16[8,128,1024]{2,1,0:T(8,128)(2,1)}), bf16[8,128,1024]{2,1,0:T(8,128)(2,1)}, u32[]{:S(2)}, u32[]{:S(2)}) async-start(bf16[8,128,1024]{2,1,0:T(8,128)(2,1)} %bitcast.42), calls=%async_computation.3 | async-start | bytes 4194304 | tf_op jit(solution)/shard_map/all_to_all | solution.py:637
  562.6 106.9 %all-reduce.6.cloned.1.call-start = ((), (), s32[]{:S(2)}) async-start(), calls=%async_computation.13 | async-start | bytes 1097728 | tf_op jit(solution)/shard_map/psum | solution.py:894
  669.5 4.3 copy-start.3
Sparse Core Ops, SparseCore 0:
  9.6 18.4 all-gather.9
  29.6 62.7 all-gather.7
  142.9 111.2 all-gather.13
  255.6 36.8 all-gather.11
  365.2 102.1 all-gather.15
  469.8 24.6 reduce-scatter.4
  554.0 27.8 reduce-scatter.2
  585.4 84.0 all-reduce.5

commit v2 on v1

--- a/solution.py
+++ b/solution.py
@@ -26,6 +26,7 @@
 F32 = jnp.float32
 BF16 = jnp.bfloat16
 MIB = 1 << 20
+MESH = pl.DeviceIdType.MESH
 
 
 def nn(a, b):
@@ -107,20 +108,6 @@
     return (r[0:1] * 32.0 + r[1:2]).astype(jnp.int32)
 
 
-def send_kernel(shift, share, meta, order_ref, x_ref, out_ref, spos_ref):
-    rows = x_ref.shape[0]
-    own = order_ref[pl.ds(meta[7], 1), :]
-    dest = own >> shift
-    hot = jnp.where(iota((order_ref.shape[0], rows), 0) == dest, 1.0, 0.0)
-    rank = jnp.sum(hot * (running_count(hot) - 1.0), axis=0, keepdims=True)
-    spos = dest * share + rank.astype(jnp.int32)
-    spos_ref[...] = spos
-    x = x_ref[...]
-    for t in range(0, rows, SPAN):
-        hit = one_hot(iota((SPAN, rows), 0) + t == spos)
-        out_ref[t : t + SPAN, :] = nn(hit, x).astype(BF16)
-
-
 def invert(idx):
     width = idx.shape[1]
     values = two_rows(iota((1, width), 1))
@@ -131,17 +118,232 @@
     return jnp.concatenate(pieces, 1)
 
 
-def route_kernel(shift, share, n, meta, order_ref, spos_ref, slot_ref, where_ref, tok_ref):
-    rows = spos_ref.shape[1]
+def peers(axis):
+    n, me = lax.axis_size(axis), lax.axis_index(axis)
+    return [(k, lax.rem(me + k, n), lax.rem(me + n - k, n)) for k in range(1, n)]
+
+
+def send(src, dst, send_sem, recv_sem, **where):
+    return pltpu.make_async_remote_copy(
+        src_ref=src, dst_ref=dst, send_sem=send_sem, recv_sem=recv_sem, device_id=where, device_id_type=MESH
+    )
+
+
+def greet(targets):
+    barrier = pltpu.get_barrier_semaphore()
+    for where in targets:
+        pl.semaphore_signal(barrier, inc=1, device_id=where, device_id_type=MESH)
+    pl.semaphore_wait(barrier, len(targets))
+
+
+def arrive_kernel(
+    log_rows, share, order_ref, x_ref, cot_ref, w_ref, ad_ref,
+    got_ref, cots_ref, slot_ref, where_ref, tok_ref, wall_ref, adall_ref,
+    sorted_ref, s_tok, r_tok, s_w, r_w, s_c, r_c, local_sem,
+):
+    n, me = lax.axis_size("ctx"), lax.axis_index("ctx")
+    nf, f = lax.axis_size("fsdp"), lax.axis_index("fsdp")
+    pair = f + 1 - 2 * lax.rem(f, 2)
+    sides = [lax.rem(f + 2 * k, nf) for k in range(1, nf // 2)]
+    backs = [lax.rem(f + nf - 2 * k, nf) for k in range(1, nf // 2)]
+    rows = x_ref.shape[0]
+    kw, ka = w_ref.shape[0], ad_ref.shape[0]
+
+    greet([{"ctx": p} for _, p, _ in peers("ctx")] + [{"fsdp": p} for p in sides + [pair]])
+
+    def shard(ref, which, k):
+        return ref.at[pl.ds(pl.multiple_of(which * k, k), k), :]
+
+    own = [(ad_ref, adall_ref, ka), (w_ref, wall_ref, kw)]
+    across = []
+    for k, side in enumerate(sides):
+        across.append([send(src, shard(dst, f, h), s_w.at[k, m], r_w.at[k, m], fsdp=side) for m, (src, dst, h) in enumerate(own)])
+        for c in across[-1]:
+            c.start()
+    inside = []
+    for m, (src, dst, h) in enumerate(own):
+        c = send(src, shard(dst, f, h), s_c.at[0, m], r_c.at[0, m], fsdp=pair)
+        c.start()
+        inside.append(c)
+    keep = [pltpu.make_async_copy(src, shard(dst, f, h), local_sem.at[m]) for m, (src, dst, h) in enumerate(own)]
+    for c in keep:
+        c.start()
+
+    own_order = order_ref[pl.ds(me, 1), :]
+    dest = own_order >> log_rows
+    hot = jnp.where(iota((order_ref.shape[0], rows), 0) == dest, 1.0, 0.0)
+    rank = jnp.sum(hot * (running_count(hot) - 1.0), axis=0, keepdims=True)
+    spos = dest * share + rank.astype(jnp.int32)
+    x = x_ref[...]
+
+    def place(which):
+        return pl.ds(pl.multiple_of(which * share, share), share)
+
+    tokens = []
+    for k, to, _ in peers("ctx"):
+        hit = one_hot(iota((share, rows), 0) + to * share == spos)
+        sorted_ref[place(to), :] = nn(hit, x).astype(BF16)
+        c = send(sorted_ref.at[place(to), :], got_ref.at[place(me), :], s_tok.at[k - 1], r_tok.at[k - 1], ctx=to)
+        c.start()
+        tokens.append(c)
+    hit = one_hot(iota((share, rows), 0) + me * share == spos)
+    sorted_ref[place(me), :] = nn(hit, x).astype(BF16)
+    mine_copy = pltpu.make_async_copy(sorted_ref.at[place(me), :], got_ref.at[place(me), :], local_sem.at[2])
+    mine_copy.start()
+
+    cot = cot_ref[...]
+    for t in range(0, rows, SPAN):
+        cots_ref[t : t + SPAN, :] = nn(one_hot(iota((SPAN, rows), 0) + t == spos), cot).astype(BF16)
     order = order_ref[...]
-    mine = jnp.where(order >> shift == meta[7], 1.0, 0.0)
+    mine = jnp.where(order >> log_rows == me, 1.0, 0.0)
     slot = order & (rows - 1)
     mark = jnp.where(mine > 0.0, running_count(mine) - 1.0, -1.0).astype(jnp.int32)
     for s in range(n):
         hit = one_hot(iota((share, rows), 0) == mark[s : s + 1, :])
         slot_ref[:, s * share : (s + 1) * share] = from_two(nt(two_rows(slot[s : s + 1, :]), hit))
     where_ref[...] = invert(slot_ref[...])
-    tok_ref[...] = invert(spos_ref[...])
+    tok_ref[...] = invert(spos)
+
+    for k, back in enumerate(backs):
+        for m, (src, dst, h) in enumerate(own):
+            across[k][m].wait_recv()
+            c = send(shard(dst, back, h), shard(dst, back, h), s_c.at[k + 1, m], r_c.at[k + 1, m], fsdp=pair)
+            c.start()
+            inside.append(c)
+    for c in inside:
+        c.wait()
+    for group in across:
+        for c in group:
+            c.wait_send()
+    for c in tokens:
+        c.wait()
+    for c in keep + [mine_copy]:
+        c.wait()
+
+
+def owners_of(n):
+    return min(n, INNER // LANES)
+
+
+def each_owner(n, which, act):
+    if owners_of(n) == n:
+        act()
+    else:
+        pl.when(which < owners_of(n))(act)
+
+
+class Exchange:
+    def __init__(self, parts, through, first, starts, landed, sems, reverse):
+        self.parts, self.through, self.first, self.starts, self.landed = parts, through, first, starts, landed
+        self.s1, self.r1, self.s2, self.r2 = sems
+        self.reverse = reverse
+        self.n, self.me = lax.axis_size("ctx"), lax.axis_index("ctx")
+
+    def out(self, k, to):
+        return send(self.parts.at[to], self.first.at[self.me], self.s1.at[k - 1], self.r1.at[k - 1], ctx=to)
+
+    def back(self, k, to):
+        return send(self.starts.at[to], self.landed.at[self.me], self.s2.at[k - 1], self.r2.at[k - 1], ctx=to)
+
+    def begin(self):
+        greet([{"ctx": p} for _, p, _ in peers("ctx")])
+        for k, to, _ in peers("ctx"):
+            each_owner(self.n, to, lambda: self.out(k, to).start())
+
+    def middle(self):
+        n, me = self.n, self.me
+
+        def act():
+            self.first[me] = self.parts[me]
+            for k, to, _ in peers("ctx"):
+                self.out(k, to).wait_recv()
+
+            def lap(t, running):
+                j = n - 1 - t if self.reverse else t
+                self.starts[j] = running.astype(BF16)
+                part = self.first[j].astype(F32)
+                through = self.through(self.first, j)
+                return running * through + part[:STATE]
+
+            lax.fori_loop(0, n, lap, jnp.zeros((STATE, self.first.shape[2]), F32))
+            self.landed[me] = self.starts[me]
+            for k, to, _ in peers("ctx"):
+                self.back(k, to).start()
+
+        each_owner(n, me, act)
+
+    def finish(self, result):
+        n, me = self.n, self.me
+        for k, to, back in peers("ctx"):
+            each_owner(n, back, lambda: self.back(k, to).wait_recv())
+        w = self.landed.shape[2]
+        for j in range(owners_of(n)):
+            result[:, j * w : (j + 1) * w] = self.landed[j]
+        for k, to, _ in peers("ctx"):
+            each_owner(n, to, lambda: self.out(k, to).wait_send())
+
+        def act():
+            for k, to, _ in peers("ctx"):
+                self.back(k, to).wait_send()
+
+        each_owner(n, me, act)
+
+
+def reduce_kernel(g_ref, out_ref, pair_in, pair_sum, side_in, total, ctx_in, piece, all_in, sems):
+    n, me = lax.axis_size("ctx"), lax.axis_index("ctx")
+    nf, f = lax.axis_size("fsdp"), lax.axis_index("fsdp")
+    core = lax.rem(f, 2)
+    pair = f + 1 - 2 * core
+    sides = [lax.rem(f + 2 * k, nf) for k in range(1, nf // 2)]
+    h = g_ref.shape[0] // nf
+    cw = g_ref.shape[1] // n
+    greet([{"ctx": p} for _, p, _ in peers("ctx")] + [{"fsdp": p} for p in sides + [pair]])
+
+    def rows(which):
+        return pl.ds(pl.multiple_of(which * h, h), h)
+
+    first = []
+    for y in range(nf // 2):
+        c = send(g_ref.at[rows(2 * y + 1 - core), :], pair_in.at[y], sems.at[0, y], sems.at[1, y], fsdp=pair)
+        c.start()
+        first.append(c)
+    for y in range(nf // 2):
+        first[y].wait_recv()
+        both = g_ref[rows(2 * y + core), :].astype(F32) + pair_in[y].astype(F32)
+        pair_sum[y] = both.astype(BF16)
+    second = []
+    for k, side in enumerate(sides):
+        c = send(pair_sum.at[side // 2], side_in.at[k], sems.at[2, k], sems.at[3, k], fsdp=side)
+        c.start()
+        second.append(c)
+    mine = pair_sum[f // 2].astype(F32)
+    for k, c in enumerate(second):
+        c.wait_recv()
+        mine = mine + side_in[k].astype(F32)
+    for j in range(n):
+        total[j] = mine[:, j * cw : (j + 1) * cw].astype(BF16)
+    third = []
+    for k, to, _ in peers("ctx"):
+        c = send(total.at[to], ctx_in.at[k - 1], sems.at[4, k - 1], sems.at[5, k - 1], ctx=to)
+        c.start()
+        third.append(c)
+    mine = total[me].astype(F32)
+    for k, c in enumerate(third):
+        c.wait_recv()
+        mine = mine + ctx_in[k].astype(F32)
+    piece[...] = mine.astype(BF16)
+    fourth = []
+    for k, to, _ in peers("ctx"):
+        c = send(piece, all_in.at[me], sems.at[6, k - 1], sems.at[7, k - 1], ctx=to)
+        c.start()
+        fourth.append(c)
+    all_in[me] = piece[...]
+    for c in fourth:
+        c.wait_recv()
+    for j in range(n):
+        out_ref[:, j * cw : (j + 1) * cw] = all_in[j].astype(F32)
+    for c in first + second + third + fourth:
+        c.wait_send()
 
 
 def permute_kernel(idx_ref, x_ref, out_ref):
@@ -149,7 +351,7 @@
     out_ref[...] = nn(hit, x_ref[...]).astype(BF16)
 
 
-def in_kernel(meta, slot_ref, got_ref, w_ref, a_ref, b_ref, gain_ref, x_ref, hb_ref, u_ref, z_ref, raw_ref, dtr_ref):
+def in_kernel(meta, slot_ref, got_ref, w_ref, ad_ref, gain_ref, x_ref, hb_ref, u_ref, z_ref, raw_ref, dtr_ref):
     i = pl.program_id(0)
     rows = got_ref.shape[0]
     pos = col_pos(meta, i)
@@ -159,11 +361,13 @@
     h = x * lax.rsqrt(jnp.mean(x * x, 1, keepdims=True) + EPS) * gain_ref[...]
     hb = h.astype(BF16)
     hb_ref[...] = hb
-    u = (nn(hb, a_ref[...]) * select_of(pos, meta)).astype(BF16)
+    d = hb.shape[1]
+    u = (nt(hb, ad_ref[:, :d]) * select_of(pos, meta)).astype(BF16)
     u_ref[...] = u
+    base = 2 * d + INNER
 
     def part(lo, hi):
-        return nn(hb, w_ref[:, lo:hi]) + nn(u, b_ref[:, lo:hi])
+        return nn(hb, w_ref[:, lo:hi]) + nn(u, ad_ref[:, base + lo : base + hi])
 
     for c in range(0, INNER, 512):
         z_ref[:, c : c + 512] = part(c, c + 512)
@@ -237,8 +441,11 @@
 
     @pl.when(i == pl.num_programs(0) - 1)
     def _():
-        send_ref[:STATE] = state[...].astype(BF16)
-        send_ref[STATE:] = jnp.broadcast_to(through[0:1], (16, INNER)).astype(BF16)
+        w = send_ref.shape[2]
+        for j in range(send_ref.shape[0]):
+            at = slice(j * w, (j + 1) * w)
+            send_ref[j, :STATE] = state[:, at].astype(BF16)
+            send_ref[j, STATE:] = jnp.broadcast_to(through[0:1, at], (16, w)).astype(BF16)
 
 
 def block_mask(meta, i, transposed):
@@ -254,8 +461,16 @@
     return jnp.where(lane < HEAD, x, zero), jnp.where(lane >= HEAD, x, zero)
 
 
-def within_kernel(meta, xs_ref, bm_ref, cm_ref, dt_ref, c2_ref, c2t_ref, e_ref, y_ref, xdt, sc):
+def within_kernel(
+    meta, xs_ref, bm_ref, cm_ref, dt_ref, c2_ref, c2t_ref, e_ref, parts_ref, pin_ref,
+    y_ref, start_ref, thr_ref,
+    xdt, sc, first, starts, landed, *sems,
+):
     i = pl.program_id(0)
+    exchange = Exchange(
+        parts_ref, lambda first, j: first[j, STATE:].astype(F32)[0:1], first, starts, landed, sems, False
+    )
+    pl.when(i == 0)(exchange.begin)
     sc[...] = jnp.where(block_mask(meta, i, False), nt(cm_ref[...], bm_ref[...]), 0.0)
     xdt[...] = (xs_ref[...].astype(F32) * expand(dt_ref[...], e_ref[...])).astype(BF16)
     c2 = c2_ref[...]
@@ -281,28 +496,22 @@
         return 0
 
     lax.fori_loop(0, HEADS // 8, group, 0)
+    steps = pl.num_programs(0)
+    pl.when(i == steps - 2)(exchange.middle)
+
+    @pl.when(i == steps - 1)
+    def _():
+        exchange.finish(start_ref)
+        for j in range(thr_ref.shape[0]):
+            thr_ref[j] = first[j, STATE:]
 
 
 CHUNK = 32
-
-
-def fold_kernel(reverse, meta, part_ref, through_ref, out_ref):
-    k = pl.program_id(0)
-    j = pl.num_programs(0) - 1 - k if reverse else k
-    reached = j > meta[7] if reverse else j < meta[7]
-
-    @pl.when(k == 0)
-    def _():
-        out_ref[...] = jnp.zeros_like(out_ref)
-
-    @pl.when(reached)
-    def _():
-        out_ref[...] = out_ref[...] * through_ref[0].astype(F32)[0:1] + part_ref[0].astype(F32)
 
 
 def out_kernel(
     meta, y_ref, z_ref, xs_ref, cm_ref, reach_ref, x_ref, ls_ref, carry_ref, all_ref, e_ref, skip_ref, gain_ref,
-    w_ref, a_ref, b_ref, where_ref,
+    w_ref, ad_ref, where_ref,
     start_ref, next_ref, mixed_ref, nout_ref, v_ref, rstd_ref, sorted_ref,
     run, acc, proj, wide,
 ):
@@ -310,7 +519,7 @@
 
     @pl.when(i == 0)
     def _():
-        run[...] = all_ref[...]
+        run[...] = all_ref[...].astype(F32)
         acc[...] = jnp.zeros_like(acc)
 
     start = run[...].astype(BF16)
@@ -343,9 +552,10 @@
     lax.fori_loop(0, SPAN // CHUNK, rows_step, 0)
     pos = col_pos(meta, i)
     nout = nout_ref[...]
-    v = (nn(nout, a_ref[...]) * select_of(pos, meta)).astype(BF16)
+    d = x_ref.shape[1]
+    v = (nt(nout, ad_ref[:, d : d + INNER]) * select_of(pos, meta)).astype(BF16)
     v_ref[...] = v
-    branch = nn(nout, w_ref[...]) + nn(v, b_ref[...])
+    branch = nn(nout, w_ref[...]) + nn(v, ad_ref[:, d + INNER : 2 * d + INNER])
     result = ((x_ref[...].astype(F32) + branch) * valid_of(pos, meta)).astype(BF16)
     hit = one_hot(iota((acc.shape[0], SPAN), 0) == where_ref[...])
     acc[...] += nn(hit, result)
@@ -357,8 +567,8 @@
 
 def gate_back_kernel(
     meta, mixed_ref, z_ref, nout_ref, v_ref, rstd_ref, xs_ref, cm_ref, reach_ref, start_ref, carry_ref, cot_ref, slot_ref,
-    e_ref, skip_ref, gain_ref, w_ref, a_ref, b_ref,
-    dout_ref, dm_ref, dz_ref, rs_ref, dcm_ref, dst_ref, own_ref, gup_ref, gdown_ref,
+    e_ref, skip_ref, gain_ref, w_ref, ad_ref,
+    dout_ref, dm_ref, dz_ref, rs_ref, dcm_ref, dst_ref, own_ref, g_ref,
     own, through, gup, gdown, dn, wide, hi_s, lo_s, dproj,
 ):
     i = pl.program_id(0)
@@ -376,9 +586,10 @@
     dout = (nn(hit, cot_ref[...]) * valid_of(pos, meta)).astype(BF16)
     dout_ref[...] = dout
     gup[...] += tn(v_ref[...], dout)
-    dv = nt(dout, b_ref[...]).astype(BF16) * select_of(pos, meta).astype(BF16)
+    d = dout_ref.shape[1]
+    dv = nt(dout, ad_ref[:, d + INNER : 2 * d + INNER]).astype(BF16) * select_of(pos, meta).astype(BF16)
     gdown[...] += tn(dv, nout_ref[...])
-    dn[...] = nt(dout, w_ref[...]) + nt(dv, a_ref[...])
+    dn[...] = nt(dout, w_ref[...]) + nn(dv, ad_ref[:, d : d + INNER])
     wide[...] = expand(reach_ref[...], e_ref[...])
 
     def rows_step(k, _):
@@ -420,17 +631,21 @@
 
     @pl.when(i == pl.num_programs(0) - 1)
     def _():
-        own_ref[...] = own[...].astype(BF16)
-        gup_ref[...] = gup[...].astype(BF16)
-        gdown_ref[...] = gdown[...].astype(BF16)
+        w = own_ref.shape[2]
+        for j in range(own_ref.shape[0]):
+            own_ref[j] = own[:, j * w : (j + 1) * w].astype(BF16)
+        g_ref[:, :INNER] = gdown[...].astype(BF16)
+        g_ref[:, INNER:] = gup[...].astype(BF16)
 
 
 def mix_back_kernel(
-    meta, xs_ref, bm_ref, cm_ref, dm_ref, dt_ref, c2_ref, c2t_ref, dcm1_ref, e_ref,
-    dxk_ref, dbm_ref, dcm_ref,
-    xdt, dte, sct, dsc,
+    meta, xs_ref, bm_ref, cm_ref, dm_ref, dt_ref, c2_ref, c2t_ref, dcm1_ref, e_ref, parts_ref, thr_ref,
+    dxk_ref, dbm_ref, dcm_ref, later_ref,
+    xdt, dte, sct, dsc, first, starts, landed, *sems,
 ):
     i = pl.program_id(0)
+    exchange = Exchange(parts_ref, lambda first, j: thr_ref[j].astype(F32)[0:1], first, starts, landed, sems, True)
+    pl.when(i == 0)(exchange.begin)
     mask = block_mask(meta, i, True)
     sct[...] = jnp.where(mask, nt(bm_ref[...], cm_ref[...]), 0.0)
     dsc[...] = jnp.zeros_like(dsc)
@@ -468,11 +683,14 @@
     ds = jnp.where(mask, dsc[...], 0.0).astype(BF16)
     dbm_ref[...] = nn(ds, cm_ref[...])
     dcm_ref[...] = dcm1_ref[...] + tn(ds, bm_ref[...])
+    steps = pl.num_programs(0)
+    pl.when(i == steps - 2)(exchange.middle)
+    pl.when(i == steps - 1)(lambda: exchange.finish(later_ref))
 
 
 def later_kernel(
     all_ref, dst_ref, carry_ref, next_ref, e_ref, skip_ref,
-    xs_ref, bm_ref, dm_ref, dxk_ref, dbm_ref, dcm_ref, wts_ref, dact_ref,
+    xs_ref, bm_ref, dm_ref, dxk_ref, dbm_ref, dcm_ref, wts_ref, dact_ref, pin_ref,
     dl_ref, dend_ref, head_ref,
     acc,
 ):
@@ -480,7 +698,7 @@
 
     @pl.when(i == 0)
     def _():
-        acc[...] = all_ref[...]
+        acc[...] = all_ref[...].astype(F32)
 
     a = acc[...]
     dl = a.astype(BF16)
@@ -503,9 +721,9 @@
 
 def in_back_kernel(
     meta, dl_ref, dend_ref, xs_ref, bm_ref, dm_ref, dz_ref, dxk_ref, dbm_ref, dcm_ref, wts_ref, dtr_ref, rs_ref, dact_ref,
-    halo_ref, cw_ref, e_ref, skip_ref, bias_ref, rate_ref, w_ref, a_ref, b_ref, u_ref, hb_ref, x_ref, dout_ref, gain_ref,
-    where_ref,
-    sorted_ref, gup_ref, gdown_ref,
+    halo_ref, cw_ref, e_ref, skip_ref, bias_ref, rate_ref, w_ref, ad_ref, u_ref, hb_ref, x_ref, dout_ref, gain_ref,
+    where_ref, gout_ref,
+    sorted_ref, g_ref,
     head, acc, gup, gdown, wide, dacc, hi_s, lo_s, draw,
 ):
     k = pl.program_id(0)
@@ -573,10 +791,16 @@
     gup[:, :INNER] += tn(u, dz)
     gup[:, INNER:mid] += tn(u, dr)
     gup[:, mid:end] += tn(u, ddt)
-    du = nt(dz, b_ref[:, :INNER]) + nt(dr, b_ref[:, INNER:mid]) + nt(ddt, b_ref[:, mid:end])
+    d = hb.shape[1]
+    base = 2 * d + INNER
+    du = (
+        nt(dz, ad_ref[:, base : base + INNER])
+        + nt(dr, ad_ref[:, base + INNER : base + mid])
+        + nt(ddt, ad_ref[:, base + mid : base + end])
+    )
     du = du.astype(BF16) * select_of(pos, meta).astype(BF16)
     gdown[...] += tn(du, hb)
-    dh = nt(dz, w_ref[:, :INNER]) + nt(dr, w_ref[:, INNER:mid]) + nt(ddt, w_ref[:, mid:end]) + nt(du, a_ref[...])
+    dh = nt(dz, w_ref[:, :INNER]) + nt(dr, w_ref[:, INNER:mid]) + nt(ddt, w_ref[:, mid:end]) + nn(du, ad_ref[:, :d])
     x = x_ref[...].astype(F32)
     rstd = lax.rsqrt(jnp.mean(x * x, 1, keepdims=True) + EPS)
     g = dh * gain_ref[...]
@@ -589,19 +813,34 @@
     @pl.when(k == pl.num_programs(0) - 1)
     def _():
         sorted_ref[...] = acc[...].astype(BF16)
-        gup_ref[...] = gup[...].astype(BF16)
-        gdown_ref[...] = gdown[...].astype(BF16)
+        g_ref[:, :d] = gdown[...].astype(BF16)
+        g_ref[:, d:base] = gout_ref[...]
+        g_ref[:, base : base + end] = gup[...].astype(BF16)
+        rest = g_ref.shape[1] - base - end
+        g_ref[:, base + end :] = jnp.zeros((LOW, rest), BF16)
 
 
 def shape(*dims, dtype=F32):
     return jax.ShapeDtypeStruct(dims, dtype)
 
 
-def params(mib=56):
-    return pltpu.CompilerParams(vmem_limit_bytes=mib * MIB)
+def params(mib=56, remote=None):
+    if remote is None:
+        return pltpu.CompilerParams(vmem_limit_bytes=mib * MIB)
+    return pltpu.CompilerParams(vmem_limit_bytes=mib * MIB, collective_id=remote, has_side_effects=True)
 
 
 SMEM = pl.BlockSpec(memory_space=pltpu.SMEM)
+VMEM = pl.BlockSpec(memory_space=pltpu.VMEM)
+ANY = pl.BlockSpec(memory_space=pl.ANY)
+
+
+def exchange_scratch(n, rows):
+    owners = owners_of(n)
+    w = INNER // owners
+    return [
+        pltpu.VMEM((n, rows, w), BF16), pltpu.VMEM((n, STATE, w), BF16), pltpu.VMEM((owners, STATE, w), BF16),
+    ] + [pltpu.SemaphoreType.DMA((n - 1,))] * 4
 
 
 def fixed(*dims):
@@ -660,31 +899,32 @@
     by_source = order[0].reshape(n, rows)
     by_source = jnp.pad(by_source, ((0, -n % 16), (0, 0)), constant_values=-1)
 
-    sent, spos = pl.pallas_call(
-        partial(send_kernel, log_rows, share),
-        in_specs=[SMEM] + [pl.BlockSpec(memory_space=pltpu.VMEM)] * 2,
-        out_shape=(shape(rows, width, dtype=BF16), shape(1, rows, dtype=jnp.int32)),
-        compiler_params=params(),
-        name="send_tokens",
-    )(meta, by_source, tokens[0])
-    got = a2a(sent)
-    got_cot = a2a(permute(spos, cotangent[0]))
-
-    w_in = lax.all_gather(in_weight, "fsdp", axis=0, tiled=True)
-    a_in = lax.all_gather(in_down, "fsdp", axis=1, tiled=True)
-    b_in = lax.all_gather(in_up, "fsdp", axis=0, tiled=True)
+    nf = lax.axis_size("fsdp")
+    assert nf % 2 == 0 and share % 16 == 0
+    adapters = jnp.concatenate([in_down.T, out_down.T, out_up, in_up], 1)
+    kw, ka, cols = in_weight.shape[0], adapters.shape[0], adapters.shape[1]
+    dma = pltpu.SemaphoreType.DMA
+    got, cot_sorted, slot, where, tok, w_in, ad = pl.pallas_call(
+        partial(arrive_kernel, log_rows, share),
+        in_specs=[VMEM, VMEM, VMEM, ANY, ANY],
+        out_specs=[ANY, VMEM, VMEM, VMEM, VMEM, ANY, ANY],
+        out_shape=(
+            shape(rows, width, dtype=BF16), shape(rows, width, dtype=BF16), shape(1, rows, dtype=jnp.int32),
+            shape(1, rows, dtype=jnp.int32), shape(1, rows, dtype=jnp.int32), shape(kw * nf, proj_w, dtype=BF16),
+            shape(ka * nf, cols, dtype=BF16),
+        ),
+        scratch_shapes=[
+            pltpu.VMEM((rows, width), BF16), dma((n - 1,)), dma((n - 1,)), dma((nf // 2 - 1, 2)), dma((nf // 2 - 1, 2)),
+            dma((nf // 2, 2)), dma((nf // 2, 2)), dma((3,)),
+        ],
+        compiler_params=params(remote=1),
+        name="arrive",
+    )(by_source, tokens[0], cotangent[0], in_weight, adapters)
+    got_cot = a2a(cot_sorted)
     w_out = lax.all_gather(out_weight, "fsdp", axis=0, tiled=True)
-    a_out = lax.all_gather(out_down, "fsdp", axis=1, tiled=True)
-    b_out = lax.all_gather(out_up, "fsdp", axis=0, tiled=True)
-
-    slot, where, tok = pl.pallas_call(
-        partial(route_kernel, log_rows, share, n),
-        in_specs=[SMEM] + [pl.BlockSpec(memory_space=pltpu.VMEM)] * 2,
-        out_shape=(shape(1, rows, dtype=jnp.int32),) * 3,
-        compiler_params=params(),
-        name="route",
-    )(meta, by_source, spos)
-
+
+    owners = owners_of(n)
+    cw = -(-cols // (n * LANES)) * LANES
     heads_pad = lambda v: jnp.pad(v, (0, LANES - HEADS))[None]
     e = (jnp.arange(LANES)[:, None] == jnp.arange(INNER)[None, :] // HEAD).astype(BF16)
     bias = heads_pad(dt_bias)
@@ -698,8 +938,7 @@
         in_kernel,
         grid=(nb,),
         in_specs=[
-            SMEM, fixed(1, rows), fixed(rows, width), fixed(width, proj_w), fixed(width, LOW), fixed(LOW, proj_w),
-            fixed(1, width),
+            SMEM, fixed(1, rows), fixed(rows, width), fixed(width, proj_w), fixed(LOW, cols), fixed(1, width),
         ],
         out_specs=[row_tile(width), row_tile(width), row_tile(LOW), row_tile(INNER), row_tile(CONV_CH), row_tile(LANES)],
         out_shape=(
@@ -708,11 +947,11 @@
         ),
         compiler_params=params(),
         name="in_proj",
-    )(meta, slot, got, w_in, a_in, b_in, gain)
+    )(meta, slot, got, w_in, ad, gain)
 
     halo = shift_ctx(raw[rows - 16 :], 1)
 
-    xs, bm, cm, dact, dt, c2, c2t, wts, reach, ls, carry, send = pl.pallas_call(
+    xs, bm, cm, dact, dt, c2, c2t, wts, reach, ls, carry, parts = pl.pallas_call(
         conv_kernel,
         grid=(nb,),
         in_specs=[
@@ -722,52 +961,32 @@
         out_specs=[
             row_tile(INNER), row_tile(STATE), row_tile(STATE), row_tile(CONV_CH), row_tile(LANES), row_tile(LANES),
             blocked(HEADS, SPAN), row_tile(LANES), row_tile(LANES), blocked(STATE, INNER), blocked(8, INNER),
-            kept(STATE + 16, INNER),
+            kept(owners, STATE + 16, INNER // owners),
         ],
         out_shape=(
             shape(rows, INNER, dtype=BF16), shape(rows, STATE, dtype=BF16), shape(rows, STATE, dtype=BF16),
             shape(rows, CONV_CH, dtype=BF16), shape(rows, LANES), shape(rows, LANES),
             shape(nb, HEADS, SPAN), shape(rows, LANES), shape(rows, LANES), shape(nb, STATE, INNER), shape(nb, 8, INNER),
-            shape(STATE + 16, INNER, dtype=BF16),
+            shape(owners, STATE + 16, INNER // owners, dtype=BF16),
         ),
         scratch_shapes=[pltpu.VMEM((8, CONV_CH), F32), pltpu.VMEM((STATE, INNER), F32), pltpu.VMEM((8, INNER), F32)],
         compiler_params=params(),
         name="conv_state",
     )(meta, raw, halo, dtr, conv_weight, cb, bias, rate, e)
 
-    states = lax.all_gather(send, "ctx")
-
-    y = pl.pallas_call(
+    y, start_in, thr = pl.pallas_call(
         within_kernel,
         grid=(nb,),
         in_specs=[
             SMEM, row_tile(INNER), row_tile(STATE), row_tile(STATE), row_tile(LANES), row_tile(LANES), blocked(HEADS, SPAN),
-            fixed(LANES, INNER),
-        ],
-        out_specs=row_tile(INNER),
-        out_shape=shape(rows, INNER),
-        scratch_shapes=[pltpu.VMEM((SPAN, INNER), BF16), pltpu.VMEM((SPAN, SPAN), F32)],
-        compiler_params=params(),
+            fixed(LANES, INNER), VMEM, ANY,
+        ],
+        out_specs=[row_tile(INNER), kept(STATE, INNER), kept(n, 16, INNER // owners)],
+        out_shape=(shape(rows, INNER), shape(STATE, INNER, dtype=BF16), shape(n, 16, INNER // owners, dtype=BF16)),
+        scratch_shapes=[pltpu.VMEM((SPAN, INNER), BF16), pltpu.VMEM((SPAN, SPAN), F32)] + exchange_scratch(n, STATE + 16),
+        compiler_params=params(remote=2),
         name="within",
-    )(meta, xs, bm, cm, dt, c2, c2t, e)
-
-    def fold(parts, reverse):
-        at = (lambda k: n - 1 - k) if reverse else (lambda k: k)
-        return pl.pallas_call(
-            partial(fold_kernel, reverse),
-            grid=(n,),
-            in_specs=[
-                SMEM,
-                pl.BlockSpec((1, STATE, INNER), lambda k: (at(k), 0, 0)),
-                pl.BlockSpec((1, 16, INNER), lambda k: (at(k), STATE // 16, 0)),
-            ],
-            out_specs=kept(STATE, INNER),
-            out_shape=shape(STATE, INNER),
-            compiler_params=params(),
-            name="fold",
-        )(meta, parts, states)
-
-    start_in = fold(states, False)
+    )(meta, xs, bm, cm, dt, c2, c2t, e, parts, got_cot)
 
     start, after, mixed, nout, v, rstd, result = pl.pallas_call(
         out_kernel,
@@ -775,7 +994,7 @@
         in_specs=[
             SMEM, row_tile(INNER), row_tile(INNER), row_tile(INNER), row_tile(STATE), row_tile(LANES), row_tile(width),
             blocked(STATE, INNER), blocked(8, INNER), fixed(STATE, INNER), fixed(LANES, INNER), fixed(1, INNER),
-            fixed(1, INNER), fixed(INNER, width), fixed(INNER, LOW), fixed(LOW, width),
+            fixed(1, INNER), fixed(INNER, width), fixed(LOW, cols),
             pl.BlockSpec((1, SPAN), lambda i: (0, i)),
         ],
         out_specs=[
@@ -792,26 +1011,26 @@
         ],
         compiler_params=params(),
         name="gate_out",
-    )(meta, y, z, xs, cm, reach, x, ls, carry, start_in, e, skip, gate, w_out, a_out, b_out, where)
+    )(meta, y, z, xs, cm, reach, x, ls, carry, start_in, e, skip, gate, w_out, ad, where)
 
     back_out = a2a(result)
 
-    dout, dm, dz, rs, dcm1, dst, own, g_up_out, g_down_out = pl.pallas_call(
+    dout, dm, dz, rs, dcm1, dst, own, g_out = pl.pallas_call(
         gate_back_kernel,
         grid=(nb,),
         in_specs=[
             SMEM, row_tile(INNER), row_tile(INNER), row_tile(INNER), row_tile(LOW), row_tile(LANES), row_tile(INNER),
             row_tile(STATE), row_tile(LANES), blocked(STATE, INNER), blocked(8, INNER), fixed(rows, width), fixed(1, rows),
-            fixed(LANES, INNER), fixed(1, INNER), fixed(1, INNER), fixed(INNER, width), fixed(INNER, LOW), fixed(LOW, width),
+            fixed(LANES, INNER), fixed(1, INNER), fixed(1, INNER), fixed(INNER, width), fixed(LOW, cols),
         ],
         out_specs=[
             row_tile(width), row_tile(INNER), row_tile(INNER), row_tile(LANES), row_tile(STATE), blocked(STATE, INNER),
-            kept(STATE, INNER), kept(LOW, width), kept(LOW, INNER),
+            kept(owners, STATE, INNER // owners), kept(LOW, INNER + width),
         ],
         out_shape=(
             shape(rows, width, dtype=BF16), shape(rows, INNER, dtype=BF16), shape(rows, INNER, dtype=BF16),
-            shape(rows, LANES), shape(rows, STATE), shape(nb, STATE, INNER), shape(STATE, INNER, dtype=BF16),
-            shape(LOW, width, dtype=BF16), shape(LOW, INNER, dtype=BF16),
+            shape(rows, LANES), shape(rows, STATE), shape(nb, STATE, INNER), shape(owners, STATE, INNER // owners, dtype=BF16),
+            shape(LOW, INNER + width, dtype=BF16),
         ),
         scratch_shapes=[
             pltpu.VMEM((STATE, INNER), F32), pltpu.VMEM((8, INNER), F32), pltpu.VMEM((LOW, width), F32),
@@ -820,27 +1039,24 @@
         ],
         compiler_params=params(),
         name="gate_back",
-    )(meta, mixed, z, nout, v, rstd, xs, cm, reach, start, carry, got_cot, slot, e, skip, gate, w_out, a_out, b_out)
-
-    states_back = lax.all_gather(own, "ctx")
-    later_in = fold(states_back, True)
-
-    dxk, dbm, dcm = pl.pallas_call(
+    )(meta, mixed, z, nout, v, rstd, xs, cm, reach, start, carry, got_cot, slot, e, skip, gate, w_out, ad)
+
+    dxk, dbm, dcm, later_in = pl.pallas_call(
         mix_back_kernel,
         grid=(nb,),
         in_specs=[
             SMEM, row_tile(INNER), row_tile(STATE), row_tile(STATE), row_tile(INNER), row_tile(LANES), row_tile(LANES),
-            blocked(HEADS, SPAN), row_tile(STATE), fixed(LANES, INNER),
-        ],
-        out_specs=[row_tile(INNER), row_tile(STATE), row_tile(STATE)],
-        out_shape=(shape(rows, INNER), shape(rows, STATE), shape(rows, STATE)),
+            blocked(HEADS, SPAN), row_tile(STATE), fixed(LANES, INNER), VMEM, VMEM,
+        ],
+        out_specs=[row_tile(INNER), row_tile(STATE), row_tile(STATE), kept(STATE, INNER)],
+        out_shape=(shape(rows, INNER), shape(rows, STATE), shape(rows, STATE), shape(STATE, INNER, dtype=BF16)),
         scratch_shapes=[
             pltpu.VMEM((SPAN, INNER), BF16), pltpu.VMEM((SPAN, INNER), F32), pltpu.VMEM((SPAN, SPAN), F32),
             pltpu.VMEM((SPAN, SPAN), F32),
-        ],
-        compiler_params=params(),
+        ] + exchange_scratch(n, STATE),
+        compiler_params=params(remote=3),
         name="mix_back",
-    )(meta, xs, bm, cm, dm, dt, c2, c2t, dcm1, e)
+    )(meta, xs, bm, cm, dm, dt, c2, c2t, dcm1, e, own, thr)
 
     back = lambda *dims: pl.BlockSpec((1,) + dims, lambda i: (nb - 1 - i,) + (0,) * len(dims))
     dl, dend, head = pl.pallas_call(
@@ -849,32 +1065,30 @@
         in_specs=[
             fixed(STATE, INNER), back(STATE, INNER), back(8, INNER), back(STATE, INNER),
             fixed(LANES, INNER), fixed(1, INNER), fixed(16, INNER), fixed(16, STATE), fixed(16, INNER), fixed(16, INNER),
-            fixed(16, STATE), fixed(16, STATE), fixed(16, LANES), fixed(16, CONV_CH),
+            fixed(16, STATE), fixed(16, STATE), fixed(16, LANES), fixed(16, CONV_CH), ANY,
         ],
         out_specs=[back(STATE, INNER), back(8, LANES), kept(16, CONV_CH)],
         out_shape=(shape(nb, STATE, INNER, dtype=BF16), shape(nb, 8, LANES), shape(16, CONV_CH)),
         scratch_shapes=[pltpu.VMEM((STATE, INNER), F32)],
         compiler_params=params(),
         name="later_state",
-    )(later_in, dst, carry, after, e, skip, xs, bm, dm, dxk, dbm, dcm, wts, dact)
+    )(later_in, dst, carry, after, e, skip, xs, bm, dm, dxk, dbm, dcm, wts, dact, back_out)
 
     from_next = shift_ctx(head, -1)
 
     tile = lambda w: pl.BlockSpec((SPAN, w), lambda i: (nb - 1 - i, 0))
-    grad, g_up_in, g_down_in = pl.pallas_call(
+    grad, g_all = pl.pallas_call(
         in_back_kernel,
         grid=(nb,),
         in_specs=[
             SMEM, back(STATE, INNER), back(8, LANES), tile(INNER), tile(STATE), tile(INNER), tile(INNER), tile(INNER),
             tile(STATE), tile(STATE), tile(LANES), tile(LANES), tile(LANES), tile(CONV_CH), fixed(16, CONV_CH),
             fixed(KERNEL, CONV_CH), fixed(LANES, INNER), fixed(1, INNER), fixed(1, LANES), fixed(1, LANES),
-            fixed(width, proj_w), fixed(width, LOW), fixed(LOW, proj_w), tile(LOW), tile(width), tile(width), tile(width),
-            fixed(1, width), pl.BlockSpec((1, SPAN), lambda i: (0, nb - 1 - i)),
-        ],
-        out_specs=[kept(rows, width), kept(LOW, proj_w), kept(LOW, width)],
-        out_shape=(
-            shape(rows, width, dtype=BF16), shape(LOW, proj_w, dtype=BF16), shape(LOW, width, dtype=BF16),
-        ),
+            fixed(width, proj_w), fixed(LOW, cols), tile(LOW), tile(width), tile(width), tile(width),
+            fixed(1, width), pl.BlockSpec((1, SPAN), lambda i: (0, nb - 1 - i)), fixed(LOW, INNER + width),
+        ],
+        out_specs=[kept(rows, width), kept(LOW, n * cw)],
+        out_shape=(shape(rows, width, dtype=BF16), shape(LOW, n * cw, dtype=BF16)),
         scratch_shapes=[
             pltpu.VMEM((8, CONV_CH), F32), pltpu.VMEM((rows, width), F32), pltpu.VMEM((LOW, proj_w), F32),
             pltpu.VMEM((LOW, width), F32), pltpu.VMEM((SPAN, INNER), F32), pltpu.VMEM((SPAN, CONV_CH), F32),
@@ -884,20 +1098,33 @@
         name="in_back",
     )(
         meta, dl, dend, xs, bm, dm, dz, dxk, dbm, dcm, wts, dtr, rs, dact, from_next, conv_weight, e, skip, bias, rate,
-        w_in, a_in, b_in, u, hb, x, dout, gain, where,
+        w_in, ad, u, hb, x, dout, gain, where, g_out,
     )
 
     back_grad = a2a(grad)
 
-    def reduced(g):
-        part = lax.psum_scatter(g, "fsdp", scatter_dimension=0, tiled=True)
-        return lax.psum(part, "ctx").astype(F32)
-
-    g_out = reduced(jnp.concatenate([g_down_out, g_up_out], 1))
-    g_in = reduced(jnp.concatenate([g_down_in, g_up_in], 1))
+    half, low = nf // 2, LOW // nf
+    sums = pl.pallas_call(
+        reduce_kernel,
+        in_specs=[VMEM],
+        out_specs=VMEM,
+        out_shape=shape(low, n * cw),
+        scratch_shapes=[
+            pltpu.VMEM((half, low, n * cw), BF16), pltpu.VMEM((half, low, n * cw), BF16),
+            pltpu.VMEM((max(half - 1, 1), low, n * cw), BF16), pltpu.VMEM((n, low, cw), BF16),
+            pltpu.VMEM((n - 1, low, cw), BF16), pltpu.VMEM((low, cw), BF16), pltpu.VMEM((n, low, cw), BF16),
+            dma((8, max(n, half))),
+        ],
+        compiler_params=params(remote=4),
+        name="reduce",
+    )(g_all)
     block_output = permute(tok, back_out)[None]
     input_grad = permute(tok, back_grad)[None]
-    return (block_output, input_grad, g_in[:, :width].T, g_in[:, width:], g_out[:, :INNER].T, g_out[:, INNER:])
+    base = 2 * width + INNER
+    return (
+        block_output, input_grad, sums[:, :width].T, sums[:, base : base + proj_w], sums[:, width : width + INNER].T,
+        sums[:, width + INNER : base],
+    )
 
 
 def solution(mesh):

time: 699 us -> 520 us (0.74)
  waiting for transfers between devices: 329 us -> 22.2 us
  Pallas kernels: 257 us -> 428 us
  starting transfers between devices: 42.4 us -> 22.3 us
  blocking collectives: 18.6 us -> 0 us
    all_gather x4 -> x0, waiting for transfers between devices: 151 us -> none  [the longest x1 68.5 us: local(): states = lax.all_gather(send, 'ctx')]
    pallas_call x4 -> x2, Pallas kernels: 20.6 us -> 163 us  [the longest x1 95 us: local(): pl.pallas_call(partial(arrive_kernel, log_rows, share), in_specs=[VMEM, V...]
    psum x1 -> x0, waiting for transfers between devices: 82.2 us -> none  [reduced(): return lax.psum(part, 'ctx').astype(F32)]
    all_to_all x4 -> x3, waiting for transfers between devices: 33.3 us -> 0.01 us  [a2a(): return lax.all_to_all(x, 'ctx', split_axis=0, concat_axis=0, tiled=True)]
    all_gather x1, waiting for transfers between devices: 32.6 us -> 0.02 us  [local(): w_out = lax.all_gather(out_weight, 'fsdp', axis=0, tiled=True)]
    reduce_scatter x2 -> x0, waiting for transfers between devices: 19.3 us -> none  [reduced(): part = lax.psum_scatter(g, 'fsdp', scatter_dimension=0, tiled=True)]
    all_gather x3 -> x0, blocking collectives: 18.6 us -> none  [the longest x1 6.5 us: local(): a_out = lax.all_gather(out_down, 'fsdp', axis=1, tiled=True)]
    pallas_call x1, Pallas kernels: 16.2 us -> 32.2 us  [local(): pl.pallas_call(within_kernel, grid=(nb,), in_specs=[SMEM, row_tile(INNER)...]
  transfers between devices with their start and end apart: 14 -> 6, of which waited for: 9 -> 2; matrix products, arithmetic and copies ran while one was open for 3% -> 3% of each run, Pallas kernels for 24% -> 62%
where the time goes in v2:
time: 520 us; the launch traced here: 510 us
  Pallas kernels  428 us (82%)
  starting transfers between devices  22.3 us (4%)
  waiting for transfers between devices  22.2 us (4%)
  local copies, waits for them, and re-layouts  18.8 us (4%)
  between operations  14.7 us (3%)
    pallas_call x1, Pallas kernels, local(): pl.pallas_call(partial(arrive_kernel, log_rows, share), in_specs=[VMEM, V...  95 us
    pallas_call x1, Pallas kernels, local(): pl.pallas_call(reduce_kernel, in_specs=[VMEM], out_specs=VMEM, out_shape=...  67.8 us
    pallas_call x1, Pallas kernels, local(): pl.pallas_call(in_back_kernel, grid=(nb,), in_specs=[SMEM, back(STATE, IN...  61.6 us
    pallas_call x1, Pallas kernels, local(): pl.pallas_call(gate_back_kernel, grid=(nb,), in_specs=[SMEM, row_tile(INN...  41.5 us
    pallas_call x1, Pallas kernels, local(): pl.pallas_call(out_kernel, grid=(nb,), in_specs=[SMEM, row_tile(INNER), r...  36.6 us
    pallas_call x1, Pallas kernels, local(): pl.pallas_call(within_kernel, grid=(nb,), in_specs=[SMEM, row_tile(INNER)...  32.2 us
    pallas_call x1, Pallas kernels, local(): pl.pallas_call(mix_back_kernel, grid=(nb,), in_specs=[SMEM, row_tile(INNE...  32.1 us
    pallas_call x1, Pallas kernels, local(): pl.pallas_call(in_kernel, grid=(nb,), in_specs=[SMEM, fixed(1, rows), fix...  23.9 us
  transfers between devices with their start and end apart: 6, of which 2 were waited for; matrix products, arithmetic and copies ran while one was open for 3% of the time, Pallas kernels for 62%

profile of v2, /device:TPU:10, one launch (start us, length us, event | category | flops | bytes accessed | tf_op | source)
XLA Modules:
  0.0 510.5 jit_solution(18190398596919139980)
XLA Ops:
  7.2 0.0 all-gather.2.cloned.1.call-start
  7.2 0.7 all-gather.2.cloned.1.call-update
  7.9 0.5 broadcast.45
  8.4 1.5 reduce.4
  9.9 0.0 copy-start.3
  9.9 0.0 copy-start.5
  9.9 0.0 copy-start.7
  9.9 0.0 copy-start.8
  10.0 4.3 copy.24.w_ref
  14.2 0.6 pad.11.order_ref
  14.9 0.0 copy-done.3
  14.9 0.0 copy-done.5
  14.9 0.0 copy-done.7
  14.9 0.0 copy-done.8
  14.9 0.8 pad_maximum_fusion.ad_ref
  15.7 95.0 %arrive.1 = (bf16[1024,1024]{1,0:T(8,128)(2,1)}, bf16[1024,1024]{1,0:T(8,128)(2,1)}, s32[1,1024]{1,0:T(1,128)}, s32[1,1024]{1,0:T(1,128)}, s32[1,1024]{1,0:T(1,1...) custom-call(s32[16,1024]{1,0:T(8,128)} %pad.11.order_ref, bf16[1024,1024]{1,0:T(8,128)(2,1)} %bitcast.37, ...), custom_call_target="tpu_custom_call" | custom-call | tf_op jit(solution)/shard_map/arrive/pallas_call | solution.py:907
  110.7 0.0 copy-start.13
  110.7 0.0 copy-start.10
  110.7 6.1 %all-to-all-start = ((bf16[8,128,1024]{2,1,0:T(8,128)(2,1)}), bf16[8,128,1024]{2,1,0:T(8,128)(2,1)S(1)}, u32[]{:S(2)}, u32[]{:S(2)}) async-start(bf16[8,128,1024]{2,1,0:T(8,128)(2,1)} %bitcast.34), calls=%async_computation | async-start | bytes 4194304 | tf_op jit(solution)/shard_map/all_to_all | solution.py:876
  116.8 0.0 copy-done.13
  116.8 0.2 reduce-window.9
  116.9 0.0 copy-done.10
  117.0 0.7 pad_add_fusion.meta
  117.6 23.9 %in_proj.1 = (bf16[1024,1024]{1,0:T(8,128)(2,1)}, bf16[1024,1024]{1,0:T(8,128)(2,1)}, bf16[1024,128]{1,0:T(8,128)(2,1)}, f32[1024,2048]{1,0:T(8,128)}, bf16[1024,2304]{1,0:T(8,128)(2,1)}, /*index=5*/f32[1024,128]{1,0:T(8,128)}) custom-call(s32[8]{0:T(128)} %pad_add_fusion.meta, s32[1,1024]{1,0:T(1,128)} %get-tuple-element.59.slot_ref, ...), custom_call_target="tpu_custom_call" | custom-call | tf_op jit(solution)/shard_map/in_proj/pallas_call | solution.py:937
  141.5 0.9 slice.15
  142.4 3.6 collective-permute-start
  145.9 0.0 copy-done.9
  146.0 0.6 broadcast_in_dim.35.cb_ref
  146.6 0.0 copy-done.11
  146.6 0.1 broadcast_in_dim.38
  146.6 0.7 broadcast_in_dim_reshape.3.skip_ref
  147.3 0.0 copy-done.14
  147.3 0.9 fusion.e_ref
  148.2 0.0 copy-done.12
  148.2 0.6 pad_bitcast_fusion
  148.8 14.9 %collective-permute-done.halo_ref = bf16[16,2304]{1,0:T(8,128)(2,1)S(1)} collective-permute-done((bf16[16,2304]{1,0:T(8,128)(2,1)S(1)}, bf16[16,2304]{1,0:T(8,128)(2,1)S(1)}, u32[]{:S(2)}, u32[]{:S(2)}) %collective-permute-start) | collective-permute-done | bytes 73760 | tf_op jit(solution)/shard_map/ppermute | solution.py:881
  163.7 0.6 copy-done.6
  164.4 19.5 %conv_state.1 = (bf16[1024,2048]{1,0:T(8,128)(2,1)}, bf16[1024,128]{1,0:T(8,128)(2,1)}, bf16[1024,128]{1,0:T(8,128)(2,1)}, bf16[1024,2304]{1,0:T(8,128)(2,1)}, f...) custom-call(s32[8]{0:T(128)} %pad_add_fusion.meta, ...), custom_call_target="tpu_custom_call" | custom-call | tf_op jit(solution)/shard_map/conv_state/pallas_call | solution.py:954
  183.9 0.0 all-to-all-done
  183.9 0.0 copy-start
  183.9 1.3 copy-done
  185.2 32.2 %within.1 = (f32[1024,2048]{1,0:T(8,128)}, bf16[128,2048]{1,0:T(8,128)(2,1)}, bf16[8,16,256]{2,1,0:T(8,128)(2,1)}) custom-call(s32[8]{0:T(128)} %pad_add_fusion.meta, bf16[1024,2048]{1,0:T(8,128)(2,1)} %get-tuple-element.65.xs_ref, bf16[1024,128]{1,0:T(8,128)(2,1)} %get-tuple-element.66.bm_ref, bf16[1024,128]{1,0:T(8,128)(2,1)} %get-tuple-element.67.cm_ref, ...), custom_call_target="tpu_custom_call" | custom-call | tf_op jit(solution)/shard_map/within/pallas_call | solution.py:977
  217.4 0.0 all-gather.2.cloned.1.call-done.w_ref
  217.4 36.6 %gate_out.1 = (bf16[4,128,2048]{2,1,0:T(8,128)(2,1)}, bf16[4,128,2048]{2,1,0:T(8,128)(2,1)}, f32[1024,2048]{1,0:T(8,128)}, bf16[1024,2048]{1,0:T(8,128)(2,1)}, b...) custom-call(s32[8]{0:T(128)} %pad_add_fusion.meta, ...), custom_call_target="tpu_custom_call" | custom-call | tf_op jit(solution)/shard_map/gate_out/pallas_call | solution.py:991
  254.0 6.2 %all-to-all-start.1 = ((bf16[8,128,1024]{2,1,0:T(8,128)(2,1)}), bf16[8,128,1024]{2,1,0:T(8,128)(2,1)S(1)}, u32[]{:S(2)}, u32[]{:S(2)}) async-start(bf16[8,128,1024]{2,1,0:T(8,128)(2,1)} %bitcast.36), calls=%async_computation.1 | async-start | bytes 4194304 | tf_op jit(solution)/shard_map/all_to_all | solution.py:876
  260.3 41.5 %gate_back.1 = (bf16[1024,1024]{1,0:T(8,128)(2,1)}, bf16[1024,2048]{1,0:T(8,128)(2,1)}, bf16[1024,2048]{1,0:T(8,128)(2,1)}, f32[1024,128]{1,0:T(8,128)}, f32[102...) custom-call(s32[8]{0:T(128)} %pad_add_fusion.meta, ...), custom_call_target="tpu_custom_call" | custom-call | tf_op jit(solution)/shard_map/gate_back/pallas_call | solution.py:1018
  301.8 32.1 %mix_back.1 = (f32[1024,2048]{1,0:T(8,128)}, f32[1024,128]{1,0:T(8,128)}, f32[1024,128]{1,0:T(8,128)}, bf16[128,2048]{1,0:T(8,128)(2,1)}) custom-call(s32[8]{0:T(128)} %pad_add_fusion.meta, bf16[1024,2048]{1,0:T(8,128)(2,1)} %get-tuple-element.65.xs_ref, bf16[1024,128]{1,0:T(8,128)(2,1)} %get-tuple-element.66.bm_ref, ...), custom_call_target="tpu_custom_call" | custom-call | tf_op jit(solution)/shard_map/mix_back/pallas_call | solution.py:1044
  334.0 0.0 all-to-all-done.1
  334.0 0.0 copy-start.1
  334.0 1.3 copy-done.1
  335.3 7.6 %later_state.1 = (bf16[4,128,2048]{2,1,0:T(8,128)(2,1)}, f32[4,8,128]{2,1,0:T(8,128)}, f32[16,2304]{1,0:T(8,128)}) custom-call(bf16[128,2048]{1,0:T(8,128)(2,1)} %get-tuple-element.91.all_ref, f32[4,128,2048]{2,1,0:T(8,128)} %get-tuple-element.92.dst_ref, f32[4,8,2048]{2,1,0:T(8,128)} %get-tuple-element.78.carry_ref, ...), custom_call_target="tpu_custom_call" | custom-call | tf_op jit(solution)/shard_map/later_state/pallas_call | solution.py:1062
  342.9 2.2 collective-permute-start.1
  345.1 6.6 %collective-permute-done.1.halo_ref = f32[16,2304]{1,0:T(8,128)S(1)} collective-permute-done((f32[16,2304]{1,0:T(8,128)}, f32[16,2304]{1,0:T(8,128)S(1)}, u32[]{:S(2)}, u32[]{:S(2)}) %collective-permute-start.1) | collective-permute-done | bytes 147488 | tf_op jit(solution)/shard_map/ppermute | solution.py:881
  351.6 0.7 copy-done.4
  352.3 61.6 %in_back.1 = (bf16[1024,1024]{1,0:T(8,128)(2,1)}, bf16[128,9216]{1,0:T(8,128)(2,1)}) custom-call(s32[8]{0:T(128)} %pad_add_fusion.meta, bf16[4,128,2048]{2,1,0:T(8,128)(2,1)} %get-tuple-element.99.dl_ref, f32[4,8,128]{2,1,0:T(8,128)} %get-tuple-element.100.dend_ref, bf16[1024,2048]{1,0:T(8,128)(2,1)} %get-tuple-element.65.xs_ref, ...), custom_call_target="tpu_custom_call" | custom-call | tf_op jit(solution)/shard_map/in_back/pallas_call | solution.py:1080
  413.9 4.2 all-to-all-start.2
  418.1 5.3 %permute.2 = bf16[1024,1024]{1,0:T(8,128)(2,1)} custom-call(s32[1,1024]{1,0:T(1,128)} %get-tuple-element.58.idx_ref, bf16[1024,1024]{1,0:T(8,128)(2,1)} %bitcast.30), custom_call_target="tpu_custom_call" | custom-call | tf_op jit(solution)/shard_map/permute/pallas_call | solution.py:864
  423.4 67.8 %reduce.5 = f32[32,9216]{1,0:T(8,128)} custom-call(bf16[128,9216]{1,0:T(8,128)(2,1)} %get-tuple-element.109.g_ref), custom_call_target="tpu_custom_call" | custom-call | tf_op jit(solution)/shard_map/reduce/pallas_call | solution.py:1107
  491.3 1.9 slice.17
  493.2 1.7 fusion.4
  494.8 1.7 slice_bitcast_fusion
  496.5 0.0 all-to-all-done.2
  496.5 1.3 copy-done.2
  497.9 5.3 %permute.3 = bf16[1024,1024]{1,0:T(8,128)(2,1)} custom-call(s32[1,1024]{1,0:T(1,128)} %get-tuple-element.58.idx_ref, bf16[1024,1024]{1,0:T(8,128)(2,1)} %bitcast.31), custom_call_target="tpu_custom_call" | custom-call | tf_op jit(solution)/shard_map/permute/pallas_call | solution.py:864
  (10 shorter events, 0.0 us)
Async XLA Ops:
  7.2 210.2 %all-gather.2.cloned.1.call-start = ((), (), s32[]{:S(2)}) async-start(), calls=%async_computation.3 | async-start | bytes 5242880 | tf_op jit(solution)/shard_map/all_gather | solution.py:924
  9.9 4.9 copy-start.3
  9.9 4.9 copy-start.5
  9.9 4.9 copy-start.7
  9.9 4.9 copy-start.8
  110.7 6.1 %copy-start.13 = (s32[1,3]{1,0:T(1,128)S(1)}, s32[1,3]{1,0:T(1,128)}, u32[]{:S(2)}) copy-start(s32[1,3]{1,0:T(1,128)} %param.21) | copy-start | bytes 40
  110.7 6.3 %copy-start.10 = (s32[1,3]{1,0:T(1,128)S(1)}, s32[1,3]{1,0:T(1,128)}, u32[]{:S(2)}) copy-start(s32[1,3]{1,0:T(1,128)} %param.22) | copy-start | bytes 40
  110.7 73.2 %all-to-all-start = ((bf16[8,128,1024]{2,1,0:T(8,128)(2,1)}), bf16[8,128,1024]{2,1,0:T(8,128)(2,1)S(1)}, u32[]{:S(2)}, u32[]{:S(2)}) async-start(bf16[8,128,1024]{2,1,0:T(8,128)(2,1)} %bitcast.34), calls=%async_computation | async-start | bytes 4194304 | tf_op jit(solution)/shard_map/all_to_all | solution.py:876
  117.6 28.3 %copy-start.9 = (f32[2304]{0:T(1024)S(1)}, f32[2304]{0:T(1024)}, u32[]{:S(2)}) copy-start(f32[2304]{0:T(1024)} %param.31) | copy-start | bytes 27652
  117.6 28.9 %copy-start.11 = (f32[32]{0:T(128)S(1)}, f32[32]{0:T(128)}, u32[]{:S(2)}) copy-start(f32[32]{0:T(128)} %param.34) | copy-start | bytes 388
  117.6 29.7 %copy-start.14 = (f32[32]{0:T(128)S(1)}, f32[32]{0:T(128)}, u32[]{:S(2)}) copy-start(f32[32]{0:T(128)} %param.33) | copy-start | bytes 388
  117.6 30.6 %copy-start.12 = (f32[32]{0:T(128)S(1)}, f32[32]{0:T(128)}, u32[]{:S(2)}) copy-start(f32[32]{0:T(128)} %param.32) | copy-start | bytes 388
  142.4 21.4 %collective-permute-start = (bf16[16,2304]{1,0:T(8,128)(2,1)S(1)}, bf16[16,2304]{1,0:T(8,128)(2,1)S(1)}, u32[]{:S(2)}, u32[]{:S(2)}) collective-permute-start(bf16[16,2304]{1,0:T(8,128)(2,1)S(1)} %slice.15), channel_id=1, source_target_pairs={{0,1},{1,2},{2,3},{3,4},{4,5},{5,6},{6,7},{8,9},{9,10},{10,11},{11... | collective-permute-start | bytes 221192 | tf_op jit(solution)/shard_map/ppermute | solution.py:881
  163.7 0.6 copy-start.6
  183.9 1.3 copy-start
  254.0 79.9 %all-to-all-start.1 = ((bf16[8,128,1024]{2,1,0:T(8,128)(2,1)}), bf16[8,128,1024]{2,1,0:T(8,128)(2,1)S(1)}, u32[]{:S(2)}, u32[]{:S(2)}) async-start(bf16[8,128,1024]{2,1,0:T(8,128)(2,1)} %bitcast.36), calls=%async_computation.1 | async-start | bytes 4194304 | tf_op jit(solution)/shard_map/all_to_all | solution.py:876
  334.0 1.3 copy-start.1
  342.9 8.8 %collective-permute-start.1 = (f32[16,2304]{1,0:T(8,128)}, f32[16,2304]{1,0:T(8,128)S(1)}, u32[]{:S(2)}, u32[]{:S(2)}) collective-permute-start(f32[16,2304]{1,0:T(8,128)} %get-tuple-element.103), channel_id=1, source_target_pairs={{1,0},{2,1},{3,2},{4,3},{5,4},{6,5},{7,6},{9,8},{10,9},{11,10},{12... | collective-permute-start | bytes 442376 | tf_op jit(solution)/shard_map/ppermute | solution.py:881
  351.6 0.7 copy-start.4
  413.9 82.6 %all-to-all-start.2 = ((bf16[8,128,1024]{2,1,0:T(8,128)(2,1)}), bf16[8,128,1024]{2,1,0:T(8,128)(2,1)S(1)}, u32[]{:S(2)}, u32[]{:S(2)}) async-start(bf16[8,128,1024]{2,1,0:T(8,128)(2,1)} %bitcast.35), calls=%async_computation.2 | async-start | bytes 4194304 | tf_op jit(solution)/shard_map/all_to_all | solution.py:876
  496.5 1.3 copy-start.2
Sparse Core Ops, SparseCore 0:
  9.6 56.1 all-gather.1

commit v3 on v0

v3 whole, which is shorter than its diff:
```python
from functools import partial

import jax
import jax.numpy as jnp
from jax import lax
from jax.experimental import pallas as pl
from jax.experimental.pallas import tpu as pltpu
from jax.sharding import PartitionSpec as P

HEADS = 32
HEAD = 64
STATE = 128
KERNEL = 4
SPAN = 256
RANK = 16
ADAPTERS = 8
SEQS = 3
CONV_CH = 2304
INNER = HEADS * HEAD
LOW = ADAPTERS * RANK
LANES = 128
HALF = SPAN // 2
EPS = 1e-05
LOG2E = 1.4426950408889634

F32 = jnp.float32
BF16 = jnp.bfloat16
MIB = 1 << 20
MESH = pl.DeviceIdType.MESH


def nn(a, b):
    return jnp.dot(a, b, preferred_element_type=F32)


def nt(a, b):
    return lax.dot_general(a, b, (((1,), (1,)), ((), ())), preferred_element_type=F32)


def tn(a, b):
    return lax.dot_general(a, b, (((0,), (0,)), ((), ())), preferred_element_type=F32)


def iota(shape, dim):
    return lax.broadcasted_iota(jnp.int32, shape, dim)


def one_hot(cond):
    return jnp.where(cond, 1.0, 0.0).astype(BF16)


def split(v, parts):
    out = []
    for _ in range(parts):
        piece = v.astype(BF16)
        out.append(piece)
        v = v - piece.astype(F32)
    return out


def pairs(v):
    return jnp.concatenate(split(v, 2), 1)


class Meta:
    def __init__(self, len_ref, id_ref, rows):
        self.start = lax.axis_index("ctx") * rows
        self.ends = []
        for k in range(SEQS):
            self.ends.append(len_ref[0, k] + (self.ends[-1] if k else 0))
        self.ids = [id_ref[0, k] for k in range(SEQS)]

    def seq(self, pos):
        found = sum((pos >= end).astype(jnp.int32) for end in self.ends)
        return jnp.where(pos >= 0, found, -1)

    def valid(self, pos):
        return (pos < self.ends[-1]).astype(F32)

    def select(self, pos):
        seq = self.seq(pos)
        ids = sum(jnp.where(seq == k, self.ids[k], 0) for k in range(SEQS))
        shape = (pos.shape[0], LOW)
        return jnp.where(iota(shape, 1) // RANK == ids, 1.0, 0.0) * self.valid(pos)

    def cols(self, tile):
        return self.start + tile * SPAN + iota((SPAN, 1), 0)

    def rows(self, tile):
        return self.start + tile * SPAN + iota((1, SPAN), 1)


def sigmoid(v):
    return 0.5 * jnp.tanh(0.5 * v) + 0.5


def running_count(mask):
    width = mask.shape[1]
    tri = one_hot(iota((SPAN, SPAN), 0) <= iota((SPAN, SPAN), 1))
    pieces, before = [], jnp.zeros((mask.shape[0], 1), F32)
    for c in range(0, width, SPAN):
        part = mask[:, c : c + SPAN]
        pieces.append(nn(part.astype(BF16), tri) + before)
        before = before + jnp.sum(part, 1, keepdims=True)
    return jnp.concatenate(pieces, 1)


def two_rows(v):
    first = jnp.broadcast_to(v >> 5, (16, v.shape[1]))
    second = jnp.broadcast_to(v & 31, (16, v.shape[1]))
    row = iota((16, v.shape[1]), 0)
    return jnp.where(row == 0, first, jnp.where(row == 1, second, 0)).astype(F32).astype(BF16)


def from_two(r):
    return (r[0:1] * 32.0 + r[1:2]).astype(jnp.int32)


def invert(idx):
    width = idx.shape[1]
    values = two_rows(iota((1, width), 1))
    pieces = []
    for t in range(0, width, SPAN):
        hit = one_hot(iota((SPAN, width), 0) + t == idx)
        pieces.append(from_two(nt(values, hit)))
    return jnp.concatenate(pieces, 1)


def peers(axis):
    n, me = lax.axis_size(axis), lax.axis_index(axis)
    return [(k, lax.rem(me + k, n), lax.rem(me + n - k, n)) for k in range(1, n)]


def send(src, dst, send_sem, recv_sem, **where):
    return pltpu.make_async_remote_copy(
        src_ref=src, dst_ref=dst, send_sem=send_sem, recv_sem=recv_sem, device_id=where, device_id_type=MESH
    )


def hail(targets):
    barrier = pltpu.get_barrier_semaphore()
    for where in targets:
        pl.semaphore_signal(barrier, inc=1, device_id=where, device_id_type=MESH)


def hailed(targets):
    pl.semaphore_wait(pltpu.get_barrier_semaphore(), len(targets))


def place(which, share):
    return pl.ds(pl.multiple_of(which * share, share), share)


def spread_sems(n):
    return [pltpu.SemaphoreType.DMA((n - 1,)), pltpu.SemaphoreType.DMA((n - 1,)), pltpu.SemaphoreType.DMA]


def ring_targets():
    n, me = lax.axis_size("ctx"), lax.axis_index("ctx")
    return [{"ctx": lax.rem(me + 1, n)}, {"ctx": lax.rem(me + n - 1, n)}]


def ctx_targets():
    return [{"ctx": p} for _, p, _ in peers("ctx")]


def fsdp_sides():
    nf, f = lax.axis_size("fsdp"), lax.axis_index("fsdp")
    sides = [lax.rem(f + 2 * k, nf) for k in range(1, nf // 2)]
    backs = [lax.rem(f + nf - 2 * k, nf) for k in range(1, nf // 2)]
    return f, f + 1 - 2 * lax.rem(f, 2), sides, backs


def fsdp_targets():
    _, pair, sides, _ = fsdp_sides()
    return [{"fsdp": p} for p in sides + [pair]]


class Gather:
    def __init__(self, pieces, sems):
        s_y, r_y, s_c, r_c, keep = sems
        f, pair, sides, backs = fsdp_sides()
        self.across = [
            [send(src, dst(f), s_y.at[k, m], r_y.at[k, m], fsdp=side) for m, (src, dst) in enumerate(pieces)]
            for k, side in enumerate(sides)
        ]
        self.inside = [[send(src, dst(f), s_c.at[0, m], r_c.at[0, m], fsdp=pair) for m, (src, dst) in enumerate(pieces)]]
        self.inside += [
            [send(dst(back), dst(back), s_c.at[k + 1, m], r_c.at[k + 1, m], fsdp=pair) for m, (src, dst) in enumerate(pieces)]
            for k, back in enumerate(backs)
        ]
        self.keep = [pltpu.make_async_copy(src, dst(f), keep.at[m]) for m, (src, dst) in enumerate(pieces)]

    def begin(self):
        for group in self.across:
            for c in group:
                c.start()
        for c in self.inside[0] + self.keep:
            c.start()

    def relay(self, lo=0, hi=None):
        for k, group in enumerate(self.across):
            for c, forward in list(zip(group, self.inside[k + 1]))[lo:hi]:
                c.wait_recv()
                forward.start()

    def finish(self):
        for group in self.inside:
            for c in group:
                c.wait()
        for group in self.across:
            for c in group:
                c.wait_send()
        for c in self.keep:
            c.wait()


def gather_sems(nf, pieces):
    dma = pltpu.SemaphoreType.DMA
    side = max(nf // 2 - 1, 1)
    return [dma((side, pieces)), dma((side, pieces)), dma((nf // 2, pieces)), dma((nf // 2, pieces)), dma((pieces,))]


def stacked(ref, h):
    return lambda which: ref.at[place(which, h), :]


def chunks_of(total, parts):
    step = -(-total // (16 * parts)) * 16
    return [(lo, min(lo + step, total)) for lo in range(0, total, step)]


WEIGHT_PARTS = 4


def arrive_kernel(
    log_rows, share, order_ref, x_ref, cot_ref, wt_ref, down_ref, up_ref, bias_in, log_in, skip_in,
    got_ref, cots_ref, slot_ref, where_ref, tok_ref, wall_ref, dall_ref, uall_ref, e_ref, skip_ref, bias_ref, rate_ref,
    sorted_ref, s_tok, r_tok, own_sem, *sems,
):
    n, me = lax.axis_size("ctx"), lax.axis_index("ctx")
    rows = x_ref.shape[0]
    targets = ctx_targets() + fsdp_targets()
    hail(targets)
    pieces = [(down_ref, stacked(dall_ref, down_ref.shape[0])), (up_ref, stacked(uall_ref, up_ref.shape[0]))]
    for lo, hi in chunks_of(wt_ref.shape[0], WEIGHT_PARTS):
        pieces.append((wt_ref.at[lo:hi, :], lambda which, lo=lo, hi=hi: wall_ref.at[which, lo:hi, :]))
    gather = Gather(pieces, sems)

    own_order = order_ref[:, pl.ds(pl.multiple_of(me * rows, rows), rows)]
    dest = own_order >> log_rows
    hot = jnp.where(iota((max(n, 16), rows), 0) == dest, 1.0, 0.0)
    rank = jnp.sum(hot * (running_count(hot) - 1.0), axis=0, keepdims=True)
    spos = dest * share + rank.astype(jnp.int32)
    sort_rows(spos, x_ref, sorted_ref)
    hailed(targets)
    gather.begin()
    tokens = [
        send(
            sorted_ref.at[place(to, share), :], got_ref.at[place(me, share), :], s_tok.at[k - 1], r_tok.at[k - 1], ctx=to
        )
        for k, to, _ in peers("ctx")
    ]
    for c in tokens:
        c.start()
    own = pltpu.make_async_copy(sorted_ref.at[place(me, share), :], got_ref.at[place(me, share), :], own_sem)
    own.start()

    sort_rows(spos, cot_ref, cots_ref)
    by_source = [order_ref[:, s * rows : (s + 1) * rows] for s in range(n)]
    order = jnp.concatenate(by_source + [jnp.full((1, rows), -1, jnp.int32)] * (-n % 16), 0)
    mine = jnp.where(order >> log_rows == me, 1.0, 0.0)
    mark = jnp.where(mine > 0.0, running_count(mine) - 1.0, -1.0).astype(jnp.int32)
    for s in range(n):
        hit = one_hot(iota((share, rows), 0) == mark[s : s + 1, :])
        slot = by_source[s] & (rows - 1)
        slot_ref[:, s * share : (s + 1) * share] = from_two(nt(two_rows(slot), hit))
    where_ref[...] = invert(slot_ref[...])
    tok_ref[...] = invert(spos)
    e_ref[...] = one_hot((iota((2 * LANES, INNER), 0) & (LANES - 1)) == iota((2 * LANES, INNER), 1) // HEAD)
    pad = jnp.zeros((1, LANES - HEADS), F32)
    wide = jnp.broadcast_to(jnp.concatenate([skip_in[...], pad], 1), (16, LANES))
    skip_ref[...] = sum(nn(p, e_ref[:LANES, :]) for p in split(wide, 3))[0:1]
    bias_ref[...] = jnp.concatenate([bias_in[...], pad], 1)
    rate_ref[...] = jnp.concatenate([-jnp.exp(log_in[...]), pad], 1)

    gather.relay()
    gather.finish()
    for c in tokens:
        c.wait()
    own.wait()


def sort_rows(idx, src, dst):
    rows = src.shape[0]
    for t in range(0, rows, SPAN):
        hit = one_hot(iota((SPAN, rows), 0) + t == idx)
        dst[t : t + SPAN, :] = nn(hit, src[...]).astype(BF16)


def owners_of(n):
    return min(n, INNER // LANES)


def each_owner(n, which, act):
    if owners_of(n) == n:
        act()
    else:
        pl.when(which < owners_of(n))(act)


class Exchange:
    def __init__(self, parts, through, first, starts, landed, sems, reverse):
        self.parts, self.through, self.first, self.starts, self.landed = parts, through, first, starts, landed
        self.s1, self.r1, self.s2, self.r2 = sems
        self.reverse = reverse
        self.n, self.me = lax.axis_size("ctx"), lax.axis_index("ctx")

    def out(self, k, to):
        return send(self.parts.at[to], self.first.at[self.me], self.s1.at[k - 1], self.r1.at[k - 1], ctx=to)

    def back(self, k, to):
        return send(self.starts.at[to], self.landed.at[self.me], self.s2.at[k - 1], self.r2.at[k - 1], ctx=to)

    def begin(self):
        for k, to, _ in peers("ctx"):
            each_owner(self.n, to, lambda: self.out(k, to).start())

    def middle(self):
        n, me = self.n, self.me

        def act():
            self.first[me] = self.parts[me]
            for k, to, _ in peers("ctx"):
                self.out(k, to).wait_recv()

            def lap(t, running):
                j = n - 1 - t if self.reverse else t
                self.starts[j] = running.astype(BF16)
                part = self.first[j].astype(F32)
                through = self.through(self.first, j)
                return running * through + part[:STATE]

            lax.fori_loop(0, n, lap, jnp.zeros((STATE, self.first.shape[2]), F32))
            self.landed[me] = self.starts[me]
            for k, to, _ in peers("ctx"):
                self.back(k, to).start()

        each_owner(n, me, act)

    def finish(self, result):
        n, me = self.n, self.me
        for k, to, back in peers("ctx"):
            each_owner(n, back, lambda: self.back(k, to).wait_recv())
        w = self.landed.shape[2]
        for j in range(owners_of(n)):
            result[:, j * w : (j + 1) * w] = self.landed[j].astype(result.dtype)
        for k, to, _ in peers("ctx"):
            each_owner(n, to, lambda: self.out(k, to).wait_send())

        def act():
            for k, to, _ in peers("ctx"):
                self.back(k, to).wait_send()

        each_owner(n, me, act)


class Reduce:
    def __init__(self, g_ref, out_ref, bufs):
        self.g, self.out = g_ref, out_ref
        self.pair_in, self.pair_sum, self.side_in, self.total, self.ctx_in, self.piece, self.all_in, sems = bufs
        self.n, self.me = lax.axis_size("ctx"), lax.axis_index("ctx")
        nf = lax.axis_size("fsdp")
        self.f, pair, sides, _ = fsdp_sides()
        self.core = lax.rem(self.f, 2)
        self.h, self.cw = g_ref.shape[0] // nf, g_ref.shape[1] // self.n
        self.first = [
            send(g_ref.at[place(2 * y + 1 - self.core, self.h), :], self.pair_in.at[y], sems.at[0, y], sems.at[1, y], fsdp=pair)
            for y in range(nf // 2)
        ]
        self.second = [
            send(self.pair_sum.at[side // 2], self.side_in.at[k], sems.at[2, k], sems.at[3, k], fsdp=side)
            for k, side in enumerate(sides)
        ]
        self.third = [
            send(self.total.at[to], self.ctx_in.at[k - 1], sems.at[4, k - 1], sems.at[5, k - 1], ctx=to)
            for k, to, _ in peers("ctx")
        ]
        self.fourth = [
            send(self.piece, self.all_in.at[self.me], sems.at[6, k - 1], sems.at[7, k - 1], ctx=to)
            for k, to, _ in peers("ctx")
        ]

    def begin(self):
        for c in self.first:
            c.start()

    def over_y(self):
        for y, c in enumerate(self.first):
            c.wait_recv()
            both = self.g[place(2 * y + self.core, self.h), :].astype(F32) + self.pair_in[y].astype(F32)
            self.pair_sum[y] = both.astype(BF16)
        for c in self.second:
            c.start()

    def scatter(self):
        mine = self.pair_sum[self.f // 2].astype(F32)
        for k, c in enumerate(self.second):
            c.wait_recv()
            mine = mine + self.side_in[k].astype(F32)
        for j in range(self.n):
            self.total[j] = mine[:, j * self.cw : (j + 1) * self.cw].astype(BF16)
        for c in self.third:
            c.start()

    def gather(self):
        mine = self.total[self.me].astype(F32)
        for k, c in enumerate(self.third):
            c.wait_recv()
            mine = mine + self.ctx_in[k].astype(F32)
        self.piece[...] = mine.astype(BF16)
        for c in self.fourth:
            c.start()
        self.all_in[self.me] = self.piece[...]

    def finish(self):
        for c in self.fourth:
            c.wait_recv()
        for j in range(self.n):
            self.out[:, j * self.cw : (j + 1) * self.cw] = self.all_in[j].astype(F32)
        for c in self.first + self.second + self.third + self.fourth:
            c.wait_send()


def reduce_scratch(n, nf, cw):
    half, low = nf // 2, LOW // nf
    return [
        pltpu.VMEM((half, low, n * cw), BF16), pltpu.VMEM((half, low, n * cw), BF16),
        pltpu.VMEM((max(half - 1, 1), low, n * cw), BF16), pltpu.VMEM((n, low, cw), BF16),
        pltpu.VMEM((n - 1, low, cw), BF16), pltpu.VMEM((low, cw), BF16), pltpu.VMEM((n, low, cw), BF16),
        pltpu.SemaphoreType.DMA((8, max(n, half))),
    ]


class Resident:
    def __init__(self, wall_ref, dst, sems, lo, hi):
        nf, _, kw = wall_ref.shape
        self.copies = [
            pltpu.make_async_copy(wall_ref.at[f, lo:hi, :], dst.at[:, f * kw : (f + 1) * kw], sems.at[f]) for f in range(nf)
        ]

    def begin(self):
        for c in self.copies:
            c.start()

    def finish(self):
        for c in self.copies:
            c.wait()


def softplus(v):
    e = jnp.exp(-jnp.abs(v))
    series = e * (1.0 - e * (0.5 - e * (1.0 / 3.0 - 0.25 * e)))
    return jnp.maximum(v, 0.0) + jnp.where(e < 0.01, series, jnp.log(1.0 + e))


def in_conv_kernel(
    len_ref, id_ref, slot_ref, got_ref, wall_ref, down_ref, up_ref, gain_ref, cw_ref, cb_ref, bias_ref, rate_ref, e_ref,
    wo_ref, od_ref, ou_ref,
    x_ref, hb_ref, u_ref, dtr_ref, xs_ref, bm_ref, cm_ref, dact_ref, dt_ref, c2_ref, c2t_ref, wts_ref, reach_ref, ls_ref,
    carry_ref, send_ref, woall_ref, odall_ref, ouall_ref,
    wv, raw_s, dtr_s, ls_s, carry_s, tail, edge, landed, w_sem, s_halo, r_halo, *sems,
):
    s = pl.program_id(0)
    nb = pl.num_programs(0) // 2
    n, me = lax.axis_size("ctx"), lax.axis_index("ctx")
    rows = got_ref.shape[0]
    meta = Meta(len_ref, id_ref, rows)
    mid = INNER + CONV_CH
    weights = Resident(wall_ref, wv, w_sem, INNER, wall_ref.shape[1])
    targets = ring_targets() + fsdp_targets()
    halo = send(edge.at[5:8, :], landed.at[5:8, :], s_halo, r_halo, ctx=lax.rem(me + 1, n))
    pieces = [(od_ref, stacked(odall_ref, od_ref.shape[0])), (ou_ref, stacked(ouall_ref, ou_ref.shape[0]))]
    kw = wo_ref.shape[0]
    for lo, hi in chunks_of(kw, 2):
        at = lambda which, lo=lo, hi=hi: woall_ref.at[pl.ds(pl.multiple_of(which * kw + lo, 16), hi - lo), :]
        pieces.append((wo_ref.at[lo:hi, :], at))
    gather = Gather(pieces, sems)

    @pl.when(s == 0)
    def _():
        weights.begin()
        landed[...] = jnp.zeros_like(landed)
        hail(targets)

    @pl.when(s < nb)
    def _():
        t = lax.rem(s + nb - 1, nb)
        pos = meta.cols(t)
        hit = one_hot(iota((SPAN, rows), 0) + t * SPAN == slot_ref[...])
        x = nn(hit, got_ref[...]) * meta.valid(pos)
        x_ref[...] = x.astype(BF16)
        h = x * lax.rsqrt(jnp.mean(x * x, 1, keepdims=True) + EPS) * gain_ref[...]
        hb = h.astype(BF16)
        hb_ref[...] = hb
        u = (nt(hb, down_ref[...]) * meta.select(pos)).astype(BF16)
        u_ref[...] = u
        pl.when(s == 0)(weights.finish)
        for c in range(0, CONV_CH, 256):
            part = nt(hb, wv[c : c + 256, :]) + nn(u, up_ref[:, INNER + c : INNER + c + 256])
            raw_s[t, :, c : c + 256] = part.astype(BF16)
        last = nt(hb, wv[CONV_CH:, :]) + nn(u, up_ref[:, mid:])
        last = jnp.concatenate([last, jnp.zeros((SPAN, LANES - HEADS), F32)], 1)
        dtr_s[t] = last
        dtr_ref[...] = last

    @pl.when(s == 0)
    def _():
        edge[...] = raw_s[nb - 1, SPAN - 16 :, :].astype(F32)[8:]
        hailed(targets)
        pl.when(me < n - 1)(halo.start)
        gather.begin()

    @pl.when(s >= nb)
    def _():
        t = lax.rem(s - nb + 1, nb)

        @pl.when(t > 0)
        def _():
            tail[...] = raw_s[t - 1, SPAN - 16 :, :].astype(F32)[8:]

        pos = meta.cols(t)
        seq = meta.seq(pos)
        masks = [(meta.seq(pos - j) == seq).astype(F32) for j in range(KERNEL)]
        for c in range(0, CONV_CH, 256):
            cur = raw_s[t, :, c : c + 256].astype(F32)
            ext = jnp.concatenate([tail[:, c : c + 256], cur], 0)
            acc = cb_ref[:, c : c + 256] + cw_ref[3:4, c : c + 256] * cur
            for j in range(1, KERNEL):
                moved = pltpu.roll(ext, j, 0)[8:]
                acc = acc + (cw_ref[3 - j : 4 - j, c : c + 256] * moved) * masks[j]
            sg = sigmoid(acc)
            act = acc * sg
            dact_ref[:, c : c + 256] = (sg + act * (1.0 - sg)).astype(BF16)
            act = act.astype(BF16)
            if c < INNER:
                xs_ref[:, c : c + 256] = act
            else:
                bm_ref[...] = act[:, :STATE]
                cm_ref[...] = act[:, STATE:]
        dt = softplus(dtr_s[t] + bias_ref[...])
        dt_ref[...] = dt
        tri = one_hot(iota((SPAN, SPAN), 0) >= iota((SPAN, SPAN), 1))
        cum = sum(nn(tri, p) for p in split(dt * rate_ref[...], 3))
        cum_end = cum[SPAN - 1 : SPAN, :]
        first = meta.start + t * SPAN
        end_same = (seq == meta.seq(first + SPAN - 1)).astype(F32)
        passing = (seq == meta.seq(first - 1)).astype(F32)
        wts = jnp.exp(cum_end - cum) * dt * end_same
        wts_ref[...] = wts
        reach = jnp.exp(cum) * passing
        reach_ref[...] = reach
        c2 = cum * LOG2E
        c2_ref[...] = c2
        c2t_ref[0] = c2.T[:HEADS]
        both = pairs(wts)
        ends = [p for p in split(jnp.broadcast_to(reach[SPAN - 1 : SPAN, :], (16, LANES)), 3)]
        for c in range(0, INNER, 256):
            cs = slice(c, c + 256)
            weighted = (xs_ref[:, cs].astype(F32) * nn(both, e_ref[:, cs])).astype(BF16)
            ls = tn(bm_ref[...], weighted)
            ls_ref[0, :, cs] = ls
            ls_s[t, :, cs] = ls
        carry = sum(nn(p, e_ref[:LANES, :]) for p in ends)[:8]
        carry_ref[0] = carry
        carry_s[t] = carry

    @pl.when(s == nb + 1)
    def _():
        gather.relay(0, 3)

    @pl.when(s == 2 * nb - 2)
    def _():
        pl.when(me < n - 1)(halo.wait_send)
        pl.when(me > 0)(halo.wait_recv)
        tail[...] = jnp.where(me > 0, landed[...], 0.0)

    @pl.when(s == 2 * nb - 1)
    def _():
        w = send_ref.shape[2]
        for j in range(send_ref.shape[0]):
            at = slice(j * w, (j + 1) * w)
            state, through = ls_s[0, :, at], carry_s[0, 0:1, at]
            for b in range(1, ls_s.shape[0]):
                state = state * carry_s[b, 0:1, at] + ls_s[b, :, at]
                through = through * carry_s[b, 0:1, at]
            send_ref[j, :STATE] = state.astype(BF16)
            send_ref[j, STATE:] = jnp.broadcast_to(through, (16, w)).astype(BF16)
        gather.relay(3)
        gather.finish()


def block_mask(meta, t, transposed):
    col, row = meta.cols(t), meta.rows(t)
    return (meta.seq(col) == meta.seq(row)) & ((row >= col) if transposed else (col >= row))


def halves(x):
    lane = iota(x.shape, 1)
    zero = jnp.zeros_like(x)
    return jnp.where(lane < HEAD, x, zero), jnp.where(lane >= HEAD, x, zero)


def within_kernel(
    len_ref, id_ref, xs_ref, bm_ref, cm_ref, dt_ref, c2_ref, c2t_ref, e_ref, parts_ref, hb_ref, u_ref, up_ref, wall_ref,
    y_ref, z_ref, start_ref, thr_ref,
    xdt, sc, wv, first, starts, landed, s1, r1, s2, r2, w_sem,
):
    s = pl.program_id(0)
    nb = pl.num_programs(0) // 2
    meta = Meta(len_ref, id_ref, nb * SPAN)
    exchange = Exchange(
        parts_ref, lambda first, j: first[j, STATE:].astype(F32)[0:1], first, starts, landed, (s1, r1, s2, r2), False
    )
    weights = Resident(wall_ref, wv, w_sem, 0, INNER)

    @pl.when(s == 0)
    def _():
        hail(ctx_targets())
        weights.begin()

    @pl.when(s < nb)
    def _():
        sc[...] = jnp.where(block_mask(meta, s, False), nt(cm_ref[...], bm_ref[...]), 0.0)
        both = pairs(dt_ref[...])
        for c in range(0, INNER, 256):
            cs = slice(c, c + 256)
            xdt[:, cs] = (xs_ref[:, cs].astype(F32) * nn(both, e_ref[:, cs])).astype(BF16)
        c2 = c2_ref[...]

        def group(g, _):
            cols = pltpu.roll(c2, LANES - 8 * g, 1)
            rows = c2t_ref[0, pl.ds(pl.multiple_of(8 * g, 8), 8), :]
            for q in range(4):
                at = pl.ds(pl.multiple_of(g * 512 + q * 128, 128), 128)
                xa, xb = halves(xdt[:, at])
                mixes = []
                for h in (2 * q, 2 * q + 1):
                    col, row = cols[:, h : h + 1], rows[h : h + 1, :]

                    def mix(t, r):
                        decay = jnp.exp2(jnp.minimum(col[t : t + HALF] - row[:, r : r + HALF], 0.0))
                        return (sc[t : t + HALF, r : r + HALF] * decay).astype(BF16)

                    mixes.append((mix(0, 0), mix(HALF, 0), mix(HALF, HALF)))
                (a00, a10, a11), (b00, b10, b11) = mixes
                top = nn(jnp.concatenate([a00, b00], 1), jnp.concatenate([xa[:HALF], xb[:HALF]], 0))
                low = nn(jnp.concatenate([a10, a11, b10, b11], 1), jnp.concatenate([xa, xb], 0))
                y_ref[:HALF, at] = top.astype(BF16)
                y_ref[HALF:, at] = low.astype(BF16)
            return 0

        lax.fori_loop(0, HEADS // 8, group, 0)

    @pl.when(s == 0)
    def _():
        hailed(ctx_targets())
        exchange.begin()

    pl.when(s == nb)(weights.finish)

    @pl.when(s >= nb)
    def _():
        for c in range(0, INNER, 256):
            z_ref[:, c : c + 256] = (nt(hb_ref[...], wv[c : c + 256, :]) + nn(u_ref[...], up_ref[:, c : c + 256])).astype(BF16)

    pl.when(s == nb)(exchange.middle)

    @pl.when(s == 2 * nb - 1)
    def _():
        exchange.finish(start_ref)
        for j in range(thr_ref.shape[0]):
            thr_ref[j] = first[j, STATE:]


def out_kernel(
    len_ref, id_ref, y_ref, z_ref, xs_ref, cm_ref, reach_ref, x_ref, ls_ref, carry_ref, all_ref, e_ref, skip_ref, gain_ref,
    w_ref, down_ref, up_ref, where_ref,
    start_ref, next_ref, mixed_ref, nout_ref, v_ref, rstd_ref, sorted_ref,
    run, kept_rows, wide,
):
    i = pl.program_id(0)
    meta = Meta(len_ref, id_ref, kept_rows.shape[0])

    @pl.when(i == 0)
    def _():
        run[...] = all_ref[...].astype(F32)

    both = pairs(reach_ref[...])
    total = jnp.zeros((SPAN, LANES), F32)
    for c in range(0, INNER, 256):
        cs = slice(c, c + 256)
        now = run[:, cs]
        start = now.astype(BF16)
        start_ref[0, :, cs] = start
        later = now * carry_ref[0, 0:1, cs] + ls_ref[0, :, cs]
        run[:, cs] = later
        next_ref[0, :, cs] = later.astype(BF16)
        mixed = y_ref[:, cs].astype(F32) + nn(both, e_ref[:, cs]) * nn(cm_ref[...], start)
        mixed = mixed + skip_ref[:, cs] * xs_ref[:, cs].astype(F32)
        mixed_ref[:, cs] = mixed.astype(BF16)
        z = z_ref[:, cs].astype(F32)
        gated = mixed * (z * sigmoid(z))
        wide[:, cs] = gated
        sq = gated * gated
        total = total + sq[:, :LANES] + sq[:, LANES:]
    rstd = lax.rsqrt(jnp.sum(total, 1, keepdims=True) * (1.0 / INNER) + EPS)
    rstd_ref[...] = jnp.broadcast_to(rstd, (SPAN, LANES))
    for c in range(0, INNER, 256):
        cs = slice(c, c + 256)
        nout_ref[:, cs] = (wide[:, cs] * rstd * gain_ref[:, cs]).astype(BF16)
    pos = meta.cols(i)
    v = (nt(nout_ref[...], down_ref[...]) * meta.select(pos)).astype(BF16)
    v_ref[...] = v
    valid = meta.valid(pos)
    at = pl.ds(pl.multiple_of(i * SPAN, SPAN), SPAN)
    for c in range(0, w_ref.shape[1], 256):
        cs = slice(c, c + 256)
        branch = nn(nout_ref[...], w_ref[:, cs]) + nn(v, up_ref[:, cs])
        kept_rows[at, cs] = ((x_ref[:, cs].astype(F32) + branch) * valid).astype(BF16)

    @pl.when(i == pl.num_programs(0) - 1)
    def _():
        sort_rows(where_ref[...], kept_rows, sorted_ref)


def gate_back_kernel(
    len_ref, id_ref, mixed_ref, z_ref, nout_ref, v_ref, rstd_ref, xs_ref, cm_ref, reach_ref, start_ref, carry_ref, cot_ref,
    slot_ref, e_ref, skip_ref, gain_ref, w_ref, down_ref, up_ref,
    dout_ref, dm_ref, dz_ref, rs_ref, dcm_ref, dst_ref, own_ref, g_ref,
    own, through, gup, gdown, dn, prods, dproj,
):
    i = pl.program_id(0)
    rows = cot_ref.shape[0]
    meta = Meta(len_ref, id_ref, rows)

    @pl.when(i == 0)
    def _():
        own[...] = jnp.zeros_like(own)
        through[...] = jnp.ones_like(through)
        gup[...] = jnp.zeros_like(gup)
        gdown[...] = jnp.zeros_like(gdown)

    pos = meta.cols(i)
    hit = one_hot(iota((SPAN, rows), 0) + i * SPAN == slot_ref[...])
    valid = meta.valid(pos)
    for c in range(0, cot_ref.shape[1], 256):
        cs = slice(c, c + 256)
        dout_ref[:, cs] = (nn(hit, cot_ref[:, cs]) * valid).astype(BF16)
    dout = dout_ref[...]
    gup[...] += tn(v_ref[...], dout)
    dv = nt(dout, up_ref[...]).astype(BF16) * meta.select(pos).astype(BF16)
    rstd = rstd_ref[:, 0:1]
    total = jnp.zeros((SPAN, LANES), F32)
    for c in range(0, INNER, 256):
        cs = slice(c, c + 256)
        z = z_ref[:, cs].astype(F32)
        d = (nt(dout, w_ref[cs, :]) + nn(dv, down_ref[:, cs])) * gain_ref[:, cs]
        dn[:, cs] = d
        g = d * (mixed_ref[:, cs].astype(F32) * (z * sigmoid(z)))
        total = total + g[:, :LANES] + g[:, LANES:]
        gdown[:, cs] += tn(dv, nout_ref[:, cs])
    back = jnp.sum(total, 1, keepdims=True) * (1.0 / INNER) * rstd * rstd
    both = pairs(reach_ref[...])
    for c in range(0, INNER, 256):
        cs = slice(c, c + 256)
        z = z_ref[:, cs].astype(F32)
        sg = sigmoid(z)
        silu = z * sg
        mixed = mixed_ref[:, cs].astype(F32)
        dg = rstd * (dn[:, cs] - mixed * silu * back)
        dm = (dg * silu).astype(BF16)
        dm_ref[:, cs] = dm
        dz_ref[:, cs] = (dg * mixed * (sg + silu * (1.0 - sg))).astype(BF16)
        dm = dm.astype(F32)
        dp = (dm * nn(both, e_ref[:, cs])).astype(BF16)
        dproj[:, cs] = dp
        prods[:, cs] = (dm * (mixed - skip_ref[:, cs] * xs_ref[:, cs].astype(F32))).astype(BF16)
        dst = tn(cm_ref[...], dp)
        dst_ref[0, :, cs] = dst
        own[:, cs] += dst * through[0:1, cs]
    rs_ref[...] = nt(prods[...], e_ref[:LANES, :])
    dcm_ref[...] = nt(dproj[...], start_ref[0])
    through[...] = through[...] * carry_ref[0]

    @pl.when(i == pl.num_programs(0) - 1)
    def _():
        w = own_ref.shape[2]
        for j in range(own_ref.shape[0]):
            own_ref[j] = own[:, j * w : (j + 1) * w].astype(BF16)
        g_ref[:, :INNER] = gdown[...].astype(BF16)
        g_ref[:, INNER:] = gup[...].astype(BF16)


def mix_back_kernel(
    len_ref, id_ref, xs_ref, bm_ref, cm_ref, dm_ref, dt_ref, c2_ref, c2t_ref, dcm1_ref, e_ref, parts_ref, thr_ref,
    dst_ref, carry_ref, next_ref, dz_ref, u_ref, up_ref, wall_ref, g_ref,
    dxk_ref, dbm_ref, dcm_ref, dl_ref, dend_ref, dhz_ref, duz_ref, ga_ref,
    xdt, dte, sct, dsc, later, wv, gup, first, starts, landed, s1, r1, s2, r2, w_sem,
):
    s = pl.program_id(0)
    nb = pl.num_programs(0) // 2
    meta = Meta(len_ref, id_ref, nb * SPAN)
    exchange = Exchange(
        parts_ref, lambda first, j: thr_ref[j].astype(F32)[0:1], first, starts, landed, (s1, r1, s2, r2), True
    )
    weights = Resident(wall_ref, wv, w_sem, 0, INNER)

    @pl.when(s == 0)
    def _():
        hail(ctx_targets())
        weights.begin()
        gup[...] = jnp.zeros_like(gup)

    @pl.when(s < nb)
    def _():
        mask = block_mask(meta, s, True)
        sct[...] = jnp.where(mask, nt(bm_ref[...], cm_ref[...]), 0.0)
        dsc[...] = jnp.zeros_like(dsc)
        both = pairs(dt_ref[...])
        for c in range(0, INNER, 256):
            cs = slice(c, c + 256)
            wide = nn(both, e_ref[:, cs])
            dte[:, cs] = wide
            xdt[:, cs] = (xs_ref[:, cs].astype(F32) * wide).astype(BF16)
        c2 = c2_ref[...]

        def group(g, _):
            cols = pltpu.roll(c2, LANES - 8 * g, 1)
            rows = c2t_ref[0, pl.ds(pl.multiple_of(8 * g, 8), 8), :]
            for q in range(4):
                at = pl.ds(pl.multiple_of(g * 512 + q * 128, 128), 128)
                dm = dm_ref[:, at]
                da, db = halves(dm)
                mixes = []
                for h, x in zip((2 * q, 2 * q + 1), halves(xdt[:, at])):
                    col, row = cols[:, h : h + 1], rows[h : h + 1, :]
                    top = nt(x[:HALF], dm)
                    low = nt(x[HALF:], dm[HALF:])

                    def mix(r, t, d):
                        decay = jnp.exp2(jnp.minimum(row[:, t : t + HALF] - col[r : r + HALF], 0.0))
                        dsc[r : r + HALF, t : t + HALF] += d * decay
                        return (sct[r : r + HALF, t : t + HALF] * decay).astype(BF16)

                    mixes.append((mix(0, 0, top[:, :HALF]), mix(0, HALF, top[:, HALF:]), mix(HALF, HALF, low)))
                (a00, a01, a11), (b00, b01, b11) = mixes
                g_top = nn(jnp.concatenate([a00, a01, b00, b01], 1), jnp.concatenate([da, db], 0))
                g_low = nn(jnp.concatenate([a11, b11], 1), jnp.concatenate([da[HALF:], db[HALF:]], 0))
                dxk_ref[:HALF, at] = (g_top * dte[:HALF, at]).astype(BF16)
                dxk_ref[HALF:, at] = (g_low * dte[HALF:, at]).astype(BF16)
            return 0

        lax.fori_loop(0, HEADS // 8, group, 0)
        ds = jnp.where(mask, dsc[...], 0.0).astype(BF16)
        dbm_ref[...] = nn(ds, cm_ref[...])
        dcm_ref[...] = dcm1_ref[...] + tn(ds, bm_ref[...])

    @pl.when(s == 0)
    def _():
        hailed(ctx_targets())
        exchange.begin()

    pl.when(s == nb)(weights.finish)

    @pl.when(s >= nb)
    def _():
        dz = dz_ref[...]
        for c in range(0, dhz_ref.shape[1], 256):
            dhz_ref[:, c : c + 256] = nn(dz, wv[:, c : c + 256]).astype(BF16)
        duz_ref[...] = nt(dz, up_ref[:, :INNER])
        for c in range(0, INNER, 512):
            gup[:, c : c + 512] += tn(u_ref[...], dz_ref[:, c : c + 512])

    pl.when(s == nb)(exchange.middle)

    @pl.when(s == 2 * nb - 1)
    def _():
        base = g_ref.shape[1]
        ga_ref[:, :base] = g_ref[...]
        ga_ref[:, base : base + INNER] = gup[...].astype(BF16)
        if ga_ref.shape[1] > base + INNER:
            ga_ref[:, base + INNER :] = jnp.zeros((LOW, ga_ref.shape[1] - base - INNER), BF16)
        exchange.finish(later)
        for b in reversed(range(dl_ref.shape[0])):
            sums = []
            for c in range(0, INNER, 256):
                cs = slice(c, c + 256)
                a = later[:, cs]
                dl_ref[b, :, cs] = a.astype(BF16)
                sums.append(jnp.sum(a * next_ref[b, :, cs].astype(F32), 0, keepdims=True))
                later[:, cs] = dst_ref[b, :, cs] + carry_ref[b, 0:1, cs] * a
            total = jnp.broadcast_to(jnp.concatenate(sums, 1), (16, INNER))
            dend_ref[b] = sum(nt(p, e_ref[:LANES, :]) for p in split(total, 3))[:8]


def scan_back_kernel(
    len_ref, id_ref, dl_ref, dend_ref, xs_ref, bm_ref, dm_ref, dxk_ref, dbm_ref, dcm_ref, wts_ref, dtr_ref, rs_ref, dact_ref,
    cw_ref, e_ref, skip_ref, bias_ref, rate_ref, up_ref, u_ref, hb_ref, duz_ref, g_ref, pin_ref,
    dr_ref, du_ref, gin_ref, gout_ref,
    dacc, ddts, head, edge, landed, gup, gdown, prods, weighted, s_head, r_head, *bufs,
):
    s = pl.program_id(0)
    tiles = pl.num_programs(0) - 1
    n, me = lax.axis_size("ctx"), lax.axis_index("ctx")
    meta = Meta(len_ref, id_ref, tiles * SPAN)
    reduce = Reduce(g_ref, gout_ref, bufs)
    edge_copy = send(edge.at[0:3, :], landed.at[0:3, :], s_head, r_head, ctx=lax.rem(me + n - 1, n))
    targets = ctx_targets() + fsdp_targets()

    @pl.when(s == 0)
    def _():
        gup[...] = jnp.zeros_like(gup)
        gdown[...] = jnp.zeros_like(gdown)
        landed[...] = jnp.zeros_like(landed)
        hail(targets)

    now, before = lax.rem(s, 2), lax.rem(s + 1, 2)

    @pl.when(s < tiles)
    def _():
        both = pairs(wts_ref[...])
        for c in range(0, INNER, 256):
            cs = slice(c, c + 256)
            w = nn(both, e_ref[:, cs])
            xs = xs_ref[:, cs].astype(F32)
            dx = dxk_ref[:, cs].astype(F32) + nn(bm_ref[...], dl_ref[0, :, cs]) * w
            prods[:, cs] = (xs * dx).astype(BF16)
            dx = dx + skip_ref[:, cs] * dm_ref[:, cs].astype(F32)
            dacc[now, :, cs] = dx * dact_ref[:, cs].astype(F32)
            weighted[:, cs] = (xs * w).astype(BF16)
        dbm = dbm_ref[...] + nt(weighted[...], dl_ref[0])
        dacc[now, :, INNER : INNER + STATE] = dbm * dact_ref[:, INNER : INNER + STATE].astype(F32)
        dacc[now, :, INNER + STATE :] = dcm_ref[...] * dact_ref[:, INNER + STATE :].astype(F32)
        csum = nt(prods[...], e_ref[:LANES, :])
        last = iota((SPAN, 1), 0) == SPAN - 1
        dcum = rs_ref[...] - csum + jnp.where(last, dend_ref[0, 0:1, :], 0.0)
        tri = one_hot(iota((SPAN, SPAN), 0) <= iota((SPAN, SPAN), 1))
        dsteps = sum(nn(tri, p) for p in split(dcum, 3))
        v = dtr_ref[...] + bias_ref[...]
        sg = 1.0 / (1.0 + jnp.exp(-v))
        e = jnp.exp(jnp.minimum(v, 0.0))
        ratio = jnp.where(v < -12.0, 1.0 - 0.5 * e, sg / jnp.maximum(softplus(v), 1e-7))
        ddt = jnp.where(iota((SPAN, LANES), 1) < HEADS, csum * ratio + dsteps * rate_ref[...] * sg, 0.0).astype(BF16)
        ddts[now] = ddt
        head[...] = dacc[now, :8, :]

    @pl.when(s == 0)
    def _():
        edge[...] = dacc[0, :8, :]
        hailed(targets)
        pl.when(me > 0)(edge_copy.start)
        reduce.begin()

    @pl.when(s == tiles)
    def _():
        pl.when(me > 0)(edge_copy.wait_send)
        pl.when(me < n - 1)(edge_copy.wait_recv)
        head[...] = jnp.where(me < n - 1, landed[...], 0.0)

    @pl.when(s > 0)
    def _():
        pos = meta.cols(s - 1)
        seq = meta.seq(pos)
        masks = [(meta.seq(pos + j) == seq).astype(F32) for j in range(KERNEL)]
        for c in range(0, CONV_CH, 256):
            cs = slice(c, c + 256)
            cur = dacc[before, :, cs]
            ext = jnp.concatenate([cur, head[:, cs]], 0)
            total = cw_ref[3:4, cs] * cur
            for j in range(1, KERNEL):
                moved = pltpu.roll(ext, SPAN + 8 - j, 0)[:SPAN]
                total = total + (cw_ref[3 - j : 4 - j, cs] * moved) * masks[j]
            dr_ref[:, cs] = total.astype(BF16)
        dr_ref[:, CONV_CH:] = ddts[before][:, :HEADS]
        u, hb = u_ref[...], hb_ref[...]
        width = dr_ref.shape[1]
        for lo in range(0, width, 512):
            hi = min(lo + 512, width)
            gup[:, lo:hi] += tn(u, dr_ref[:, lo:hi])
        du = duz_ref[...] + nt(dr_ref[...], up_ref[:, INNER:])
        du = du.astype(BF16) * meta.select(pos).astype(BF16)
        du_ref[...] = du
        gdown[...] += tn(du, hb)

    pl.when(s == 1)(reduce.over_y)
    pl.when(s == 2)(reduce.scatter)
    pl.when(s == 3)(reduce.gather)

    @pl.when(s == tiles)
    def _():
        d, end = gdown.shape[1], gup.shape[1]
        gin_ref[:, :d] = gdown[...].astype(BF16)
        gin_ref[:, d : d + end] = gup[...].astype(BF16)
        if gin_ref.shape[1] > d + end:
            gin_ref[:, d + end :] = jnp.zeros((LOW, gin_ref.shape[1] - d - end), BF16)
        reduce.finish()


def tail_kernel(
    len_ref, id_ref, dhz_ref, dr_ref, du_ref, x_ref, dout_ref, wall_ref, down_ref, gain_ref, where_ref, g_ref, back_ref, tok_ref,
    out_ref, grad_ref, gsum_ref,
    wv, kept_rows, sorted_ref, got, dh, w_sem, s_sem, r_sem, own_sem, *bufs,
):
    s = pl.program_id(0)
    tiles = pl.num_programs(0) - 1
    n, me = lax.axis_size("ctx"), lax.axis_index("ctx")
    rows = kept_rows.shape[0]
    share = rows // n
    meta = Meta(len_ref, id_ref, rows)
    reduce = Reduce(g_ref, gsum_ref, bufs)
    weights = Resident(wall_ref, wv, w_sem, INNER, wall_ref.shape[1])
    targets = ctx_targets() + fsdp_targets()

    @pl.when(s == 0)
    def _():
        weights.begin()
        hail(targets)
        weights.finish()

    @pl.when(s < tiles)
    def _():
        pos = meta.cols(s)
        du = du_ref[...]
        for c in range(0, dh.shape[1], 256):
            cs = slice(c, c + 256)
            dh[:, cs] = dhz_ref[:, cs].astype(F32) + nn(dr_ref[...], wv[:, cs]) + nn(du, down_ref[:, cs])
        x = x_ref[...].astype(F32)
        rstd = lax.rsqrt(jnp.mean(x * x, 1, keepdims=True) + EPS)
        g = dh[...] * gain_ref[...]
        back = jnp.mean(g * x, 1, keepdims=True) * rstd * rstd
        dx = rstd * (g - x * back)
        dx = ((dout_ref[...].astype(F32) + dx) * meta.valid(pos)).astype(BF16)
        kept_rows[pl.ds(pl.multiple_of(s * SPAN, SPAN), SPAN), :] = dx

    @pl.when(s == 0)
    def _():
        hailed(targets)
        reduce.begin()

    pl.when(s == 1)(reduce.over_y)
    pl.when(s == 2)(reduce.scatter)

    @pl.when(s == tiles)
    def _():
        copies = [
            send(sorted_ref.at[place(to, share), :], got.at[place(me, share), :], s_sem.at[k - 1], r_sem.at[k - 1], ctx=to)
            for k, to, _ in peers("ctx")
        ]
        reduce.gather()
        sort_rows(where_ref[...], kept_rows, sorted_ref)
        for c in copies:
            c.start()
        got[place(me, share), :] = sorted_ref[place(me, share), :]
        sort_rows(tok_ref[...], back_ref, out_ref)
        reduce.finish()
        for c in copies:
            c.wait()
        sort_rows(tok_ref[...], got, grad_ref)


def shape(*dims, dtype=F32):
    return jax.ShapeDtypeStruct(dims, dtype)


def params(mib=56, remote=None):
    if remote is None:
        return pltpu.CompilerParams(vmem_limit_bytes=mib * MIB)
    return pltpu.CompilerParams(vmem_limit_bytes=mib * MIB, collective_id=remote, has_side_effects=True)


SMEM = pl.BlockSpec(memory_space=pltpu.SMEM)
VMEM = pl.BlockSpec(memory_space=pltpu.VMEM)
ANY = pl.BlockSpec(memory_space=pl.ANY)


def exchange_scratch(n, rows):
    owners = owners_of(n)
    w = INNER // owners
    return [
        pltpu.VMEM((n, rows, w), BF16), pltpu.VMEM((n, STATE, w), BF16), pltpu.VMEM((owners, STATE, w), BF16),
    ] + [pltpu.SemaphoreType.DMA((n - 1,))] * 4


def fixed(*dims):
    return pl.BlockSpec(dims, lambda i: (0,) * len(dims), pipeline_mode=pl.Buffered(1))


def kept(*dims):
    return pl.BlockSpec(dims, lambda i: (0,) * len(dims))


def row_tile(width, at=lambda i: i):
    return pl.BlockSpec((SPAN, width), lambda i: (at(i), 0))


def blocked(*dims, at=lambda i: i):
    return pl.BlockSpec((1,) + dims, lambda i: (at(i),) + (0,) * len(dims))


def a2a(x):
    return lax.all_to_all(x, "ctx", split_axis=0, concat_axis=0, tiled=True)


def local(
    tokens, cotangent, order, lengths, adapter_ids, in_weight, out_weight, in_down, in_up, out_down, out_up,
    norm_gain, conv_weight, conv_bias, dt_bias, a_log, skip_gain, gate_gain,
):
    n, nf = lax.axis_size("ctx"), lax.axis_size("fsdp")
    rows, width = tokens.shape[1:]
    nb = rows // SPAN
    share = rows // n
    log_rows = rows.bit_length() - 1
    assert rows == 1 << log_rows and rows <= 1024 and rows % SPAN == 0 and nb >= 4
    assert nf % 2 == 0 and share % 16 == 0
    proj_w = in_weight.shape[1]
    rest = proj_w - INNER
    bf = lambda *dims: shape(*dims, dtype=BF16)
    vm = pltpu.VMEM
    dma = pltpu.SemaphoreType.DMA
    padded = lambda c: -(-c // (n * LANES)) * LANES * n
    owners = owners_of(n)
    ow = INNER // owners
    wt, in_down_t, out_down_t = in_weight.T, in_down.T, out_down.T
    kw, ko, ka = wt.shape[1], out_weight.shape[0], in_down_t.shape[0]
    idx = shape(1, rows, dtype=jnp.int32)
    gain, gate, cb = norm_gain[None], gate_gain[None], conv_bias[None]
    seqs = (lengths, adapter_ids)

    parts_w = len(chunks_of(proj_w, WEIGHT_PARTS))
    got, cot_sorted, slot, where, tok, w_in, a_in, b_in, e, skip, bias, rate = pl.pallas_call(
        partial(arrive_kernel, log_rows, share),
        in_specs=[VMEM] * 9,
        out_specs=[ANY, VMEM, VMEM, VMEM, VMEM, ANY, ANY, ANY, VMEM, VMEM, VMEM, VMEM],
        out_shape=(
            bf(rows, width), bf(rows, width), idx, idx, idx, bf(nf, proj_w, kw), bf(LOW, width), bf(LOW, proj_w),
            bf(2 * LANES, INNER), shape(1, INNER), shape(1, LANES), shape(1, LANES),
        ),
        scratch_shapes=[vm((rows, width), BF16)] + spread_sems(n) + gather_sems(nf, 2 + parts_w),
        compiler_params=params(remote=1),
        name="arrive",
    )(order, tokens[0], cotangent[0], wt, in_down_t, in_up, dt_bias[None], a_log[None], skip_gain[None])
    got_cot = a2a(cot_sorted)

    lead = lambda s: (jnp.minimum(s, nb - 1) + nb - 1) % nb
    conv = lambda s: (jnp.maximum(s - nb, 0) + 1) % nb
    parts_o = 2 + len(chunks_of(ko, 2))
    (
        x, hb, u, dtr, xs, bm, cm, dact, dt, c2, c2t, wts, reach, ls, carry, parts, w_out, a_out, b_out,
    ) = pl.pallas_call(
        in_conv_kernel,
        grid=(2 * nb,),
        in_specs=[
            SMEM, SMEM, fixed(1, rows), fixed(rows, width), ANY, fixed(LOW, width), fixed(LOW, proj_w), fixed(1, width),
            fixed(KERNEL, CONV_CH), fixed(1, CONV_CH), fixed(1, LANES), fixed(1, LANES), fixed(2 * LANES, INNER),
            fixed(ko, width), fixed(ka, INNER), fixed(ka, width),
        ],
        out_specs=[
            row_tile(width, lead), row_tile(width, lead), row_tile(LOW, lead), row_tile(LANES, lead),
            row_tile(INNER, conv), row_tile(STATE, conv), row_tile(STATE, conv), row_tile(CONV_CH, conv),
            row_tile(LANES, conv), row_tile(LANES, conv), blocked(HEADS, SPAN, at=conv), row_tile(LANES, conv),
            row_tile(LANES, conv), blocked(STATE, INNER, at=conv), blocked(8, INNER, at=conv),
            kept(owners, STATE + 16, ow), ANY, ANY, ANY,
        ],
        out_shape=(
            bf(rows, width), bf(rows, width), bf(rows, LOW), shape(rows, LANES),
            bf(rows, INNER), bf(rows, STATE), bf(rows, STATE), bf(rows, CONV_CH),
            shape(rows, LANES), shape(rows, LANES), shape(nb, HEADS, SPAN), shape(rows, LANES),
            shape(rows, LANES), shape(nb, STATE, INNER), shape(nb, 8, INNER),
            bf(owners, STATE + 16, ow), bf(INNER, width), bf(LOW, INNER), bf(LOW, width),
        ),
        scratch_shapes=[
            vm((rest, width), BF16), vm((nb, SPAN, CONV_CH), BF16), vm((nb, SPAN, LANES), F32), vm((nb, STATE, INNER), F32),
            vm((nb, 8, INNER), F32), vm((8, CONV_CH), F32), vm((8, CONV_CH), F32), vm((8, CONV_CH), F32), dma((nf,)), dma, dma,
        ] + gather_sems(nf, parts_o),
        compiler_params=params(remote=2),
        name="in_conv",
    )(*seqs, slot, got, w_in, a_in, b_in, gain, conv_weight, cb, bias, rate, e, out_weight, out_down_t, out_up)

    early = lambda s: jnp.minimum(s, nb - 1)
    late = lambda s: jnp.maximum(s - nb, 0)
    y, z, start_in, thr = pl.pallas_call(
        within_kernel,
        grid=(2 * nb,),
        in_specs=[
            SMEM, SMEM, row_tile(INNER, early), row_tile(STATE, early), row_tile(STATE, early), row_tile(LANES, early),
            row_tile(LANES, early), blocked(HEADS, SPAN, at=early), fixed(2 * LANES, INNER), VMEM, row_tile(width, late),
            row_tile(LOW, late), fixed(LOW, proj_w), ANY,
        ],
        out_specs=[row_tile(INNER, early), row_tile(INNER, late), kept(STATE, INNER), kept(n, 16, ow)],
        out_shape=(bf(rows, INNER), bf(rows, INNER), bf(STATE, INNER), bf(n, 16, ow)),
        scratch_shapes=[vm((SPAN, INNER), BF16), vm((SPAN, SPAN), F32), vm((INNER, width), BF16)]
        + exchange_scratch(n, STATE + 16) + [dma((nf,))],
        compiler_params=params(remote=3),
        name="within",
    )(*seqs, xs, bm, cm, dt, c2, c2t, e, parts, hb, u, b_in, w_in)

    start, after, mixed, nout, v, rstd, result = pl.pallas_call(
        out_kernel,
        grid=(nb,),
        in_specs=[
            SMEM, SMEM, row_tile(INNER), row_tile(INNER), row_tile(INNER), row_tile(STATE), row_tile(LANES), row_tile(width),
            blocked(STATE, INNER), blocked(8, INNER), fixed(STATE, INNER), fixed(2 * LANES, INNER), fixed(1, INNER),
            fixed(1, INNER), fixed(INNER, width), fixed(LOW, INNER), fixed(LOW, width), fixed(1, rows),
        ],
        out_specs=[
            blocked(STATE, INNER), blocked(STATE, INNER), row_tile(INNER), row_tile(INNER), row_tile(LOW), row_tile(LANES),
            kept(rows, width),
        ],
        out_shape=(
            bf(nb, STATE, INNER), bf(nb, STATE, INNER), bf(rows, INNER), bf(rows, INNER), bf(rows, LOW),
            shape(rows, LANES), bf(rows, width),
        ),
        scratch_shapes=[vm((STATE, INNER), F32), vm((rows, width), BF16), vm((SPAN, INNER), F32)],
        compiler_params=params(),
        name="gate_out",
    )(*seqs, y, z, xs, cm, reach, x, ls, carry, start_in, e, skip, gate, w_out, a_out, b_out, where)
    back_out = a2a(result)

    dout, dm, dz, rs, dcm1, dst, own, g_out = pl.pallas_call(
        gate_back_kernel,
        grid=(nb,),
        in_specs=[
            SMEM, SMEM, row_tile(INNER), row_tile(INNER), row_tile(INNER), row_tile(LOW), row_tile(LANES), row_tile(INNER),
            row_tile(STATE), row_tile(LANES), blocked(STATE, INNER), blocked(8, INNER), fixed(rows, width), fixed(1, rows),
            fixed(2 * LANES, INNER), fixed(1, INNER), fixed(1, INNER), fixed(INNER, width), fixed(LOW, INNER),
            fixed(LOW, width),
        ],
        out_specs=[
            row_tile(width), row_tile(INNER), row_tile(INNER), row_tile(LANES), row_tile(STATE), blocked(STATE, INNER),
            kept(owners, STATE, ow), kept(LOW, INNER + width),
        ],
        out_shape=(
            bf(rows, width), bf(rows, INNER), bf(rows, INNER), shape(rows, LANES), shape(rows, STATE),
            shape(nb, STATE, INNER), bf(owners, STATE, ow), bf(LOW, INNER + width),
        ),
        scratch_shapes=[
            vm((STATE, INNER), F32), vm((8, INNER), F32), vm((LOW, width), F32), vm((LOW, INNER), F32),
            vm((SPAN, INNER), F32), vm((SPAN, INNER), BF16), vm((SPAN, INNER), BF16),
        ],
        compiler_params=params(),
        name="gate_back",
    )(*seqs, mixed, z, nout, v, rstd, xs, cm, reach, start, carry, got_cot, slot, e, skip, gate, w_out, a_out, b_out)

    cols_a = padded(2 * INNER + width)
    dxk, dbm, dcm, dl, dend, dhz, duz, g_a = pl.pallas_call(
        mix_back_kernel,
        grid=(2 * nb,),
        in_specs=[
            SMEM, SMEM, row_tile(INNER, early), row_tile(STATE, early), row_tile(STATE, early), row_tile(INNER, early),
            row_tile(LANES, early), row_tile(LANES, early), blocked(HEADS, SPAN, at=early), row_tile(STATE, early),
            fixed(2 * LANES, INNER), VMEM, VMEM, fixed(nb, STATE, INNER), fixed(nb, 8, INNER), fixed(nb, STATE, INNER),
            row_tile(INNER, late), row_tile(LOW, late), fixed(LOW, proj_w), ANY, fixed(LOW, INNER + width),
        ],
        out_specs=[
            row_tile(INNER, early), row_tile(STATE, early), row_tile(STATE, early), kept(nb, STATE, INNER),
            kept(nb, 8, LANES), row_tile(width, late), row_tile(LOW, late), kept(LOW, cols_a),
        ],
        out_shape=(
            bf(rows, INNER), shape(rows, STATE), shape(rows, STATE), bf(nb, STATE, INNER), shape(nb, 8, LANES),
            bf(rows, width), shape(rows, LOW), bf(LOW, cols_a),
        ),
        scratch_shapes=[
            vm((SPAN, INNER), BF16), vm((SPAN, INNER), F32), vm((SPAN, SPAN), F32), vm((SPAN, SPAN), F32),
            vm((STATE, INNER), F32), vm((INNER, width), BF16), vm((LOW, INNER), F32),
        ] + exchange_scratch(n, STATE) + [dma((nf,))],
        compiler_params=params(remote=4),
        name="mix_back",
    )(*seqs, xs, bm, cm, dm, dt, c2, c2t, dcm1, e, own, thr, dst, carry, after, dz, u, b_in, w_in, g_out)

    cols_b = padded(width + rest)
    behind = lambda s: jnp.maximum(s - 1, 0)
    dr, du, g_b, sums_a = pl.pallas_call(
        scan_back_kernel,
        grid=(nb + 1,),
        in_specs=[
            SMEM, SMEM, blocked(STATE, INNER, at=early), blocked(8, LANES, at=early), row_tile(INNER, early),
            row_tile(STATE, early), row_tile(INNER, early), row_tile(INNER, early), row_tile(STATE, early),
            row_tile(STATE, early), row_tile(LANES, early), row_tile(LANES, early), row_tile(LANES, early),
            row_tile(CONV_CH, early), fixed(KERNEL, CONV_CH), fixed(2 * LANES, INNER), fixed(1, INNER), fixed(1, LANES),
            fixed(1, LANES), fixed(LOW, proj_w), row_tile(LOW, behind), row_tile(width, behind), row_tile(LOW, behind),
            fixed(LOW, cols_a), ANY,
        ],
        out_specs=[row_tile(rest, behind), row_tile(LOW, behind), kept(LOW, cols_b), kept(LOW // nf, cols_a)],
        out_shape=(bf(rows, rest), bf(rows, LOW), bf(LOW, cols_b), shape(LOW // nf, cols_a)),
        scratch_shapes=[
            vm((2, SPAN, CONV_CH), F32), vm((2, SPAN, LANES), BF16), vm((8, CONV_CH), F32), vm((8, CONV_CH), F32),
            vm((8, CONV_CH), F32), vm((LOW, rest), F32), vm((LOW, width), F32), vm((SPAN, INNER), BF16),
            vm((SPAN, INNER), BF16), dma, dma,
        ] + reduce_scratch(n, nf, cols_a // n),
        compiler_params=params(remote=5),
        name="scan_back",
    )(
        *seqs, dl, dend, xs, bm, dm, dxk, dbm, dcm, wts, dtr, rs, dact, conv_weight, e, skip, bias, rate, b_in, u, hb, duz,
        g_a, back_out,
    )

    block_output, input_grad, sums_b = pl.pallas_call(
        tail_kernel,
        grid=(nb + 1,),
        in_specs=[
            SMEM, SMEM, row_tile(width, early), row_tile(rest, early), row_tile(LOW, early), row_tile(width, early),
            row_tile(width, early), ANY, fixed(LOW, width), fixed(1, width), fixed(1, rows), fixed(LOW, cols_b),
            fixed(rows, width), fixed(1, rows),
        ],
        out_specs=[kept(rows, width), kept(rows, width), kept(LOW // nf, cols_b)],
        out_shape=(bf(rows, width), bf(rows, width), shape(LOW // nf, cols_b)),
        scratch_shapes=[
            vm((rest, width), BF16), vm((rows, width), BF16), vm((rows, width), BF16), vm((rows, width), BF16),
            vm((SPAN, width), F32), dma((nf,)),
        ] + spread_sems(n) + reduce_scratch(n, nf, cols_b // n),
        compiler_params=params(remote=6),
        name="tail",
    )(*seqs, dhz, dr, du, x, dout, w_in, a_in, gain, where, g_b, back_out, tok)
    up_a = INNER + width
    return (
        block_output[None], input_grad[None], sums_b[:, :width].T,
        jnp.concatenate([sums_a[:, up_a : up_a + INNER], sums_b[:, width : width + rest]], 1),
        sums_a[:, :INNER].T, sums_a[:, INNER:up_a],
    )


def solution(mesh):
    placed = (
        P("fsdp", "ctx", None),
        P("fsdp", "ctx", None),
        P("fsdp", None),
        P("fsdp", None),
        P("fsdp", None),
        P("fsdp", None),
        P("fsdp", None),
        P(None, "fsdp"),
        P("fsdp", None),
        P(None, "fsdp"),
        P("fsdp", None),
        P(),
        P(),
        P(),
        P(),
        P(),
        P(),
        P(),
    )
    return jax.shard_map(
        local,
        mesh=mesh,
        in_specs=placed,
        out_specs=(
            P("fsdp", "ctx", None),
            P("fsdp", "ctx", None),
            P(None, "fsdp"),
            P("fsdp", None),
            P(None, "fsdp"),
            P("fsdp", None),
        ),
        check_vma=False,
    )
```

time: 898 us -> 406 us (0.45)
  Pallas kernels: 0 us -> 375 us
  waiting for transfers between devices: 234 us -> 0.01 us
  other arithmetic: 211 us -> 0.85 us
  matrix products: 184 us -> 0 us
  local copies, waits for them, and re-layouts: 164 us -> 11 us
  blocking collectives: 43.5 us -> 0 us
  starting transfers between devices: 33.3 us -> 13.3 us
  between operations: 16.4 us -> 0.97 us
    pallas_call x0 -> x8, Pallas kernels: none -> 375 us  [the longest x1 81.4 us: local(): pl.pallas_call(tail_kernel, grid=(nb + 1,), in_specs=[SMEM, SMEM, row_til...]
    dot_general x28 -> x0, matrix products: 184 us -> none  [the longest x6 46.5 us: outer_cols(): lax.dot_general(left, right, (((1,), (1,)), ((), ())), preferred_element_...]
    all_to_all x4 -> x2, waiting for transfers between devices: 107 us -> 0.01 us  [a2a(): return lax.all_to_all(x, 'ctx', split_axis=0, concat_axis=0, tiled=True)]
    psum x1 -> x0, waiting for transfers between devices: 71.8 us -> none  [local(): lax.psum(grads[0].astype(jnp.bfloat16), 'ctx').astype(jnp.float32)]
    another operation x14 -> x0, other arithmetic: 59.7 us -> none
    gather x9 -> x0, local copies, waits for them, and re-layouts: 54.8 us -> none  [the longest x1 8.32 us: local(): sent_tokens = jnp.take(tokens[0], send_order, axis=0)]
    all_gather x4 -> x0, blocking collectives: 43.5 us -> none  [the longest x1 19.6 us: prefix(): lax.all_gather(part.astype(kind), axis)]
    reduce_scatter x4 -> x0, waiting for transfers between devices: 43.5 us -> none  [the longest x1 28.9 us: local(): lax.psum_scatter(totals[1].astype(jnp.bfloat16), 'fsdp', scatter_dimensio...]
  transfers between devices with their start and end apart: 16 -> 2, of which waited for: 7 -> 0; matrix products, arithmetic and copies ran while one was open for 32% -> 0% of each run, Pallas kernels for 0% -> 47%
where the time goes in v3:
time: 406 us; the launch traced here: 401 us
  Pallas kernels  375 us (92%)
  starting transfers between devices  13.3 us (3%)
  local copies, waits for them, and re-layouts  11 us (3%)
    pallas_call x1, Pallas kernels, local(): pl.pallas_call(tail_kernel, grid=(nb + 1,), in_specs=[SMEM, SMEM, row_til...  81.4 us
    pallas_call x1, Pallas kernels, local(): pl.pallas_call(partial(arrive_kernel, log_rows, share), in_specs=[VMEM] *...  67.8 us
    pallas_call x1, Pallas kernels, local(): pl.pallas_call(in_conv_kernel, grid=(2 * nb,), in_specs=[SMEM, SMEM, fixe...  54.4 us
    pallas_call x1, Pallas kernels, local(): pl.pallas_call(mix_back_kernel, grid=(2 * nb,), in_specs=[SMEM, SMEM, row...  43.7 us
    pallas_call x1, Pallas kernels, local(): pl.pallas_call(scan_back_kernel, grid=(nb + 1,), in_specs=[SMEM, SMEM, bl...  37.5 us
    pallas_call x1, Pallas kernels, local(): pl.pallas_call(within_kernel, grid=(2 * nb,), in_specs=[SMEM, SMEM, row_t...  35.1 us
    pallas_call x1, Pallas kernels, local(): pl.pallas_call(gate_back_kernel, grid=(nb,), in_specs=[SMEM, SMEM, row_ti...  30.4 us
    pallas_call x1, Pallas kernels, local(): pl.pallas_call(out_kernel, grid=(nb,), in_specs=[SMEM, SMEM, row_tile(INN...  24.5 us
  transfers between devices with their start and end apart: 2, of which 0 were waited for; matrix products, arithmetic and copies ran while one was open for 0% of the time, Pallas kernels for 47%

profile of v3, /device:TPU:10, one launch (start us, length us, event | category | flops | bytes accessed | tf_op | source)
XLA Modules:
  0.0 401.0 jit_solution(5823166219217084541)
XLA Ops:
  0.6 67.8 %arrive.1 = (bf16[1024,1024]{1,0:T(8,128)(2,1)}, bf16[1024,1024]{1,0:T(8,128)(2,1)}, s32[1,1024]{1,0:T(1,128)}, s32[1,1024]{1,0:T(1,128)}, s32[1,1024]{1,0:T(1,1...) custom-call(s32[1,8192]{1,0:T(1,128)} %order_ref.1, ...), custom_call_target="tpu_custom_call" | custom-call | tf_op jit(solution)/shard_map/arrive/pallas_call | solution.py:1141
  68.4 0.0 copy-start.5
  68.5 6.5 %all-to-all-start = ((bf16[8,128,1024]{2,1,0:T(8,128)(2,1)}), bf16[8,128,1024]{2,1,0:T(8,128)(2,1)S(1)}, u32[]{:S(2)}, u32[]{:S(2)}) async-start(bf16[8,128,1024]{2,1,0:T(8,128)(2,1)} %bitcast.27), calls=%async_computation | async-start | bytes 4194304 | tf_op jit(solution)/shard_map/all_to_all | solution.py:1112
  74.9 0.0 copy-done.5
  74.9 0.6 broadcast_in_dim.28.cb_ref
  75.5 54.4 %in_conv.1 = (bf16[1024,1024]{1,0:T(8,128)(2,1)}, bf16[1024,1024]{1,0:T(8,128)(2,1)}, bf16[1024,128]{1,0:T(8,128)(2,1)}, f32[1024,128]{1,0:T(8,128)}, bf16[1024,...) custom-call(s32[1,3]{1,0:T(1,128)} %len_ref.13, ...), custom_call_target="tpu_custom_call" | custom-call | tf_op jit(solution)/shard_map/in_conv/pallas_call | solution.py:1160
  130.0 35.1 %within.1 = (bf16[1024,2048]{1,0:T(8,128)(2,1)}, bf16[1024,2048]{1,0:T(8,128)(2,1)}, bf16[128,2048]{1,0:T(8,128)(2,1)}, bf16[8,16,256]{2,1,0:T(8,128)(2,1)}) custom-call(s32[1,3]{1,0:T(1,128)} %len_ref.13, s32[1,3]{1,0:T(1,128)} %id_ref.13, bf16[1024,2048]{1,0:T(8,128)(2,1)} %get-tuple-element.79.xs_ref, bf16[1024,128]{1,0:T(8,128)(2,1)} %get-tuple-element.80.bm_ref, ...), custom_call_target="tpu_custom_call" | custom-call | tf_op jit(solution)/shard_map/within/pallas_call | solution.py:1192
  165.0 24.5 %gate_out.1 = (bf16[4,128,2048]{2,1,0:T(8,128)(2,1)}, bf16[4,128,2048]{2,1,0:T(8,128)(2,1)}, bf16[1024,2048]{1,0:T(8,128)(2,1)}, bf16[1024,2048]{1,0:T(8,128)(2,...) custom-call(s32[1,3]{1,0:T(1,128)} %len_ref.13, s32[1,3]{1,0:T(1,128)} %id_ref.13, ...), custom_call_target="tpu_custom_call" | custom-call | tf_op jit(solution)/shard_map/gate_out/pallas_call | solution.py:1208
  189.5 0.0 all-to-all-done
  189.6 0.0 copy-start.1
  189.6 1.3 copy-done.1
  190.9 6.8 %all-to-all-start.1 = ((bf16[8,128,1024]{2,1,0:T(8,128)(2,1)}), bf16[8,128,1024]{2,1,0:T(8,128)(2,1)S(1)}, u32[]{:S(2)}, u32[]{:S(2)}) async-start(bf16[8,128,1024]{2,1,0:T(8,128)(2,1)} %bitcast.26), calls=%async_computation.1 | async-start | bytes 4194304 | tf_op jit(solution)/shard_map/all_to_all | solution.py:1112
  197.7 30.4 %gate_back.1 = (bf16[1024,1024]{1,0:T(8,128)(2,1)}, bf16[1024,2048]{1,0:T(8,128)(2,1)}, bf16[1024,2048]{1,0:T(8,128)(2,1)}, f32[1024,128]{1,0:T(8,128)}, f32[102...) custom-call(s32[1,3]{1,0:T(1,128)} %len_ref.13, ...), custom_call_target="tpu_custom_call" | custom-call | tf_op jit(solution)/shard_map/gate_back/pallas_call | solution.py:1230
  228.1 43.7 %mix_back.1 = (bf16[1024,2048]{1,0:T(8,128)(2,1)}, f32[1024,128]{1,0:T(8,128)}, f32[1024,128]{1,0:T(8,128)}, bf16[4,128,2048]{2,1,0:T(8,128)(2,1)}, f32[4,8,128]...) custom-call(s32[1,3]{1,0:T(1,128)} %len_ref.13, s32[1,3]{1,0:T(1,128)} %id_ref.13, ...), custom_call_target="tpu_custom_call" | custom-call | tf_op jit(solution)/shard_map/mix_back/pallas_call | solution.py:1256
  271.8 0.0 all-to-all-done.1
  271.9 0.0 copy-start
  271.9 1.3 copy-done
  273.2 37.5 %scan_back.1 = (bf16[1024,2336]{1,0:T(8,128)(2,1)}, bf16[1024,128]{1,0:T(8,128)(2,1)}, bf16[128,4096]{1,0:T(8,128)(2,1)}, f32[32,5120]{1,0:T(8,128)}) custom-call(s32[1,3]{1,0:T(1,128)} %len_ref.13, s32[1,3]{1,0:T(1,128)} %id_ref.13, bf16[4,128,2048]{2,1,0:T(8,128)(2,1)} %get-tuple-element.115.dl_ref, f32[4,8,128]{2,1,0:T(8,128)} %get-tuple-element.116.dend_ref, ...), custom_call_target="tpu_custom_call" | custom-call | tf_op jit(solution)/shard_map/scan_back/pallas_call | solution.py:1283
  310.7 0.0 copy-start.4
  310.7 81.4 %tail.1 = (bf16[1024,1024]{1,0:T(8,128)(2,1)}, bf16[1024,1024]{1,0:T(8,128)(2,1)}, f32[32,4096]{1,0:T(8,128)}) custom-call(s32[1,3]{1,0:T(1,128)} %len_ref.13, s32[1,3]{1,0:T(1,128)} %id_ref.13, bf16[1024,1024]{1,0:T(8,128)(2,1)} %get-tuple-element.114.dhz_ref, bf16[1024,2336]{1,0:T(8,128)(2,1)} %get-tuple-element.127.dr_ref, ...), custom_call_target="tpu_custom_call" | custom-call | tf_op jit(solution)/shard_map/tail/pallas_call | solution.py:1308
  392.1 0.0 copy-start.3
  392.2 1.7 slice_bitcast_fusion.1
  393.9 1.0 slice.17
  394.9 0.0 copy-done.4
  394.9 0.7 slice.19
  395.5 0.7 slice_bitcast_fusion
  396.3 0.8 pad_maximum_fusion
  397.1 0.0 copy-done.3
  397.1 0.0 copy-start.2
  397.1 1.3 copy.26
  398.4 1.0 copy-done.2
  399.5 1.3 copy.27
Async XLA Ops:
  68.4 6.5 %copy-start.5 = (f32[2304]{0:T(1024)S(1)}, f32[2304]{0:T(1024)}, u32[]{:S(2)}) copy-start(f32[2304]{0:T(1024)} %param.31) | copy-start | bytes 27652
  68.5 121.1 %all-to-all-start = ((bf16[8,128,1024]{2,1,0:T(8,128)(2,1)}), bf16[8,128,1024]{2,1,0:T(8,128)(2,1)S(1)}, u32[]{:S(2)}, u32[]{:S(2)}) async-start(bf16[8,128,1024]{2,1,0:T(8,128)(2,1)} %bitcast.27), calls=%async_computation | async-start | bytes 4194304 | tf_op jit(solution)/shard_map/all_to_all | solution.py:1112
  189.6 1.3 copy-start.1
  190.9 81.0 %all-to-all-start.1 = ((bf16[8,128,1024]{2,1,0:T(8,128)(2,1)}), bf16[8,128,1024]{2,1,0:T(8,128)(2,1)S(1)}, u32[]{:S(2)}, u32[]{:S(2)}) async-start(bf16[8,128,1024]{2,1,0:T(8,128)(2,1)} %bitcast.26), calls=%async_computation.1 | async-start | bytes 4194304 | tf_op jit(solution)/shard_map/all_to_all | solution.py:1112
  271.9 1.3 copy-start
  310.7 84.1 %copy-start.4 = (f32[32,5120]{1,0:T(8,128)S(1)}, f32[32,5120]{1,0:T(8,128)}, u32[]{:S(2)}) copy-start(f32[32,5120]{1,0:T(8,128)} %get-tuple-element.135) | copy-start | bytes 1966084
  392.1 5.0 %copy-start.3 = (bf16[1024,1024]{1,0:T(8,128)(2,1)S(1)}, bf16[1024,1024]{1,0:T(8,128)(2,1)}, u32[]{:S(2)}) copy-start(bf16[1024,1024]{1,0:T(8,128)(2,1)} %get-tuple-element.132) | copy-start | bytes 6291460
  397.1 2.3 copy-start.2

commit v4 on v0

v4 whole, which is shorter than its diff:
```python
from functools import partial

import jax
import jax.numpy as jnp
from jax import lax
from jax.experimental import pallas as pl
from jax.experimental.pallas import tpu as pltpu
from jax.sharding import PartitionSpec as P

HEADS = 32
HEAD = 64
STATE = 128
KERNEL = 4
SPAN = 256
RANK = 16
ADAPTERS = 8
SEQS = 3
CONV_CH = 2304
INNER = HEADS * HEAD
LOW = ADAPTERS * RANK
LANES = 128
HALF = SPAN // 2
EPS = 1e-05
LOG2E = 1.4426950408889634

F32 = jnp.float32
BF16 = jnp.bfloat16
MIB = 1 << 20
MESH = pl.DeviceIdType.MESH


def nn(a, b):
    return jnp.dot(a, b, preferred_element_type=F32)


def nt(a, b):
    return lax.dot_general(a, b, (((1,), (1,)), ((), ())), preferred_element_type=F32)


def tn(a, b):
    return lax.dot_general(a, b, (((0,), (0,)), ((), ())), preferred_element_type=F32)


def iota(shape, dim):
    return lax.broadcasted_iota(jnp.int32, shape, dim)


def one_hot(cond):
    return jnp.where(cond, 1.0, 0.0).astype(BF16)


def split(v, parts):
    out = []
    for _ in range(parts):
        piece = v.astype(BF16)
        out.append(piece)
        v = v - piece.astype(F32)
    return out


def pairs(v):
    return jnp.concatenate(split(v, 2), 1)


class Meta:
    def __init__(self, len_ref, id_ref, rows):
        self.start = lax.axis_index("ctx") * rows
        self.ends = []
        for k in range(SEQS):
            self.ends.append(len_ref[0, k] + (self.ends[-1] if k else 0))
        self.ids = [id_ref[0, k] for k in range(SEQS)]

    def seq(self, pos):
        found = sum((pos >= end).astype(jnp.int32) for end in self.ends)
        return jnp.where(pos >= 0, found, -1)

    def valid(self, pos):
        return (pos < self.ends[-1]).astype(F32)

    def select(self, pos):
        seq = self.seq(pos)
        ids = sum(jnp.where(seq == k, self.ids[k], 0) for k in range(SEQS))
        shape = (pos.shape[0], LOW)
        return jnp.where(iota(shape, 1) // RANK == ids, 1.0, 0.0) * self.valid(pos)

    def cols(self, tile):
        return self.start + tile * SPAN + iota((SPAN, 1), 0)

    def rows(self, tile):
        return self.start + tile * SPAN + iota((1, SPAN), 1)


def sigmoid(v):
    return 0.5 * jnp.tanh(0.5 * v) + 0.5


def running_count(mask):
    width = mask.shape[1]
    tri = one_hot(iota((SPAN, SPAN), 0) <= iota((SPAN, SPAN), 1))
    pieces, before = [], jnp.zeros((mask.shape[0], 1), F32)
    for c in range(0, width, SPAN):
        part = mask[:, c : c + SPAN]
        pieces.append(nn(part.astype(BF16), tri) + before)
        before = before + jnp.sum(part, 1, keepdims=True)
    return jnp.concatenate(pieces, 1)


def two_rows(v):
    first = jnp.broadcast_to(v >> 5, (16, v.shape[1]))
    second = jnp.broadcast_to(v & 31, (16, v.shape[1]))
    row = iota((16, v.shape[1]), 0)
    return jnp.where(row == 0, first, jnp.where(row == 1, second, 0)).astype(F32).astype(BF16)


def from_two(r):
    return (r[0:1] * 32.0 + r[1:2]).astype(jnp.int32)


def invert(idx):
    width = idx.shape[1]
    values = two_rows(iota((1, width), 1))
    pieces = []
    for t in range(0, width, SPAN):
        hit = one_hot(iota((SPAN, width), 0) + t == idx)
        pieces.append(from_two(nt(values, hit)))
    return jnp.concatenate(pieces, 1)


def peers(axis):
    n, me = lax.axis_size(axis), lax.axis_index(axis)
    return [(k, lax.rem(me + k, n), lax.rem(me + n - k, n)) for k in range(1, n)]


def send(src, dst, send_sem, recv_sem, **where):
    return pltpu.make_async_remote_copy(
        src_ref=src, dst_ref=dst, send_sem=send_sem, recv_sem=recv_sem, device_id=where, device_id_type=MESH
    )


def hail(targets):
    barrier = pltpu.get_barrier_semaphore()
    for where in targets:
        pl.semaphore_signal(barrier, inc=1, device_id=where, device_id_type=MESH)


def hailed(targets):
    pl.semaphore_wait(pltpu.get_barrier_semaphore(), len(targets))


def place(which, share):
    return pl.ds(pl.multiple_of(which * share, share), share)


def halves_of(n):
    near = [k for k in range(1, n) if k <= n // 2 and (k % 2 == 1 or k == n // 2)]
    return near, [k for k in range(1, n) if k not in near]


class Spread:
    def __init__(self, src, dst, send_sem, recv_sem, own_sem, steps):
        n, me = lax.axis_size("ctx"), lax.axis_index("ctx")
        share = src.shape[0] // n
        self.copies = [
            send(src.at[place(to, share), :], dst.at[place(me, share), :], send_sem.at[k - 1], recv_sem.at[k - 1], ctx=to)
            for k, to, _ in peers("ctx") if k in steps
        ]
        self.own = None
        if own_sem is not None:
            self.own = pltpu.make_async_copy(src.at[place(me, share), :], dst.at[place(me, share), :], own_sem)

    def begin(self):
        for c in self.copies:
            c.start()
        if self.own is not None:
            self.own.start()

    def finish(self):
        for c in self.copies:
            c.wait()
        if self.own is not None:
            self.own.wait()


def spread_sems(n):
    return [pltpu.SemaphoreType.DMA((n - 1,)), pltpu.SemaphoreType.DMA((n - 1,)), pltpu.SemaphoreType.DMA]


def ring_targets():
    n, me = lax.axis_size("ctx"), lax.axis_index("ctx")
    return [{"ctx": lax.rem(me + 1, n)}, {"ctx": lax.rem(me + n - 1, n)}]


def ctx_targets():
    return [{"ctx": p} for _, p, _ in peers("ctx")]


def fsdp_sides():
    nf, f = lax.axis_size("fsdp"), lax.axis_index("fsdp")
    sides = [lax.rem(f + 2 * k, nf) for k in range(1, nf // 2)]
    backs = [lax.rem(f + nf - 2 * k, nf) for k in range(1, nf // 2)]
    return f, f + 1 - 2 * lax.rem(f, 2), sides, backs


def fsdp_targets():
    _, pair, sides, _ = fsdp_sides()
    return [{"fsdp": p} for p in sides + [pair]]


class Gather:
    def __init__(self, pieces, sems, kept=None):
        s_y, r_y, s_c, r_c, keep = sems
        f, pair, sides, backs = fsdp_sides()
        self.across = [
            [send(src, dst(f), s_y.at[k, m], r_y.at[k, m], fsdp=side) for m, (src, dst) in enumerate(pieces)]
            for k, side in enumerate(sides)
        ]
        self.inside = [[send(src, dst(f), s_c.at[0, m], r_c.at[0, m], fsdp=pair) for m, (src, dst) in enumerate(pieces)]]
        self.inside += [
            [send(dst(back), dst(back), s_c.at[k + 1, m], r_c.at[k + 1, m], fsdp=pair) for m, (src, dst) in enumerate(pieces)]
            for k, back in enumerate(backs)
        ]
        self.keep = [pltpu.make_async_copy(src, dst(f), keep.at[m]) for m, (src, dst) in enumerate(pieces[:kept])]

    def begin(self):
        for group in self.across:
            for c in group:
                c.start()
        for c in self.inside[0] + self.keep:
            c.start()

    def relay(self, lo=0, hi=None):
        for k, group in enumerate(self.across):
            for c, forward in list(zip(group, self.inside[k + 1]))[lo:hi]:
                c.wait_recv()
                forward.start()

    def finish(self, lo=0, hi=None):
        for group in self.inside:
            for c in group[lo:hi]:
                c.wait()
        for group in self.across:
            for c in group[lo:hi]:
                c.wait_send()
        for c in self.keep[lo:hi]:
            c.wait()


def gather_sems(nf, pieces):
    dma = pltpu.SemaphoreType.DMA
    side = max(nf // 2 - 1, 1)
    return [dma((side, pieces)), dma((side, pieces)), dma((nf // 2, pieces)), dma((nf // 2, pieces)), dma((pieces,))]


def stacked(ref, h):
    return lambda which: ref.at[place(which, h), :]


def chunks_of(total, parts):
    step = -(-total // (16 * parts)) * 16
    return [(lo, min(lo + step, total)) for lo in range(0, total, step)]


WEIGHT_PARTS = 4
SPLIT = 1024


def arrive_kernel(
    log_rows, share, order_ref, x_ref, cot_ref, wt_ref, down_ref, up_ref, bias_in, log_in, skip_in,
    got_ref, cots_ref, slot_ref, where_ref, tok_ref, wall_ref, dall_ref, uall_ref, e_ref, skip_ref, bias_ref, rate_ref,
    sorted_ref, s_tok, r_tok, own_sem, *sems,
):
    n, me = lax.axis_size("ctx"), lax.axis_index("ctx")
    rows = x_ref.shape[0]
    targets = ctx_targets() + fsdp_targets()
    hail(targets)
    pieces = [(down_ref, stacked(dall_ref, down_ref.shape[0])), (up_ref, stacked(uall_ref, up_ref.shape[0]))]
    for lo, hi in chunks_of(wt_ref.shape[0] - SPLIT, WEIGHT_PARTS):
        pieces.append((wt_ref.at[SPLIT + lo : SPLIT + hi, :], lambda which, lo=lo, hi=hi: wall_ref.at[which, lo:hi, :]))
    gather = Gather(pieces, sems)

    own_order = order_ref[:, pl.ds(pl.multiple_of(me * rows, rows), rows)]
    dest = own_order >> log_rows
    hot = jnp.where(iota((max(n, 16), rows), 0) == dest, 1.0, 0.0)
    rank = jnp.sum(hot * (running_count(hot) - 1.0), axis=0, keepdims=True)
    spos = dest * share + rank.astype(jnp.int32)
    sort_rows(spos, x_ref, sorted_ref)
    hailed(targets)
    gather.begin()
    tokens = [
        send(
            sorted_ref.at[place(to, share), :], got_ref.at[place(me, share), :], s_tok.at[k - 1], r_tok.at[k - 1], ctx=to
        )
        for k, to, _ in peers("ctx")
    ]
    for c in tokens:
        c.start()
    own = pltpu.make_async_copy(sorted_ref.at[place(me, share), :], got_ref.at[place(me, share), :], own_sem)
    own.start()

    sort_rows(spos, cot_ref, cots_ref)
    by_source = [order_ref[:, s * rows : (s + 1) * rows] for s in range(n)]
    order = jnp.concatenate(by_source + [jnp.full((1, rows), -1, jnp.int32)] * (-n % 16), 0)
    mine = jnp.where(order >> log_rows == me, 1.0, 0.0)
    mark = jnp.where(mine > 0.0, running_count(mine) - 1.0, -1.0).astype(jnp.int32)
    for s in range(n):
        hit = one_hot(iota((share, rows), 0) == mark[s : s + 1, :])
        slot = by_source[s] & (rows - 1)
        slot_ref[:, s * share : (s + 1) * share] = from_two(nt(two_rows(slot), hit))
    where_ref[...] = invert(slot_ref[...])
    tok_ref[...] = invert(spos)
    e_ref[...] = one_hot((iota((2 * LANES, INNER), 0) & (LANES - 1)) == iota((2 * LANES, INNER), 1) // HEAD)
    pad = jnp.zeros((1, LANES - HEADS), F32)
    wide = jnp.broadcast_to(jnp.concatenate([skip_in[...], pad], 1), (16, LANES))
    skip_ref[...] = sum(nn(p, e_ref[:LANES, :]) for p in split(wide, 3))[0:1]
    bias_ref[...] = jnp.concatenate([bias_in[...], pad], 1)
    rate_ref[...] = jnp.concatenate([-jnp.exp(log_in[...]), pad], 1)

    gather.relay()
    gather.finish()
    for c in tokens:
        c.wait()
    own.wait()


def sort_rows(idx, src, dst):
    rows = src.shape[0]

    def body(t):
        hit = one_hot(iota((SPAN, rows), 0) + t * SPAN == idx)
        for cs in wide_chunks(src.shape[1]):
            dst[tile_rows(t), cs] = nn(hit, src[:, cs]).astype(BF16)

    each_tile(rows // SPAN, body)


def owners_of(n):
    return min(n, INNER // LANES)


def each_owner(n, which, act):
    if owners_of(n) == n:
        act()
    else:
        pl.when(which < owners_of(n))(act)


class Exchange:
    def __init__(self, parts, through, first, starts, landed, sems, reverse):
        self.parts, self.through, self.first, self.starts, self.landed = parts, through, first, starts, landed
        self.s1, self.r1, self.s2, self.r2 = sems
        self.reverse = reverse
        self.n, self.me = lax.axis_size("ctx"), lax.axis_index("ctx")

    def out(self, k, to):
        return send(self.parts.at[to], self.first.at[self.me], self.s1.at[k - 1], self.r1.at[k - 1], ctx=to)

    def back(self, k, to):
        return send(self.starts.at[to], self.landed.at[self.me], self.s2.at[k - 1], self.r2.at[k - 1], ctx=to)

    def begin(self):
        for k, to, _ in peers("ctx"):
            each_owner(self.n, to, lambda: self.out(k, to).start())

    def middle(self):
        n, me = self.n, self.me

        def act():
            self.first[me] = self.parts[me]
            for k, to, _ in peers("ctx"):
                self.out(k, to).wait_recv()

            def lap(t, running):
                j = n - 1 - t if self.reverse else t
                self.starts[j] = running.astype(BF16)
                part = self.first[j].astype(F32)
                through = self.through(self.first, j)
                return running * through + part[:STATE]

            lax.fori_loop(0, n, lap, jnp.zeros((STATE, self.first.shape[2]), F32))
            self.landed[me] = self.starts[me]
            for k, to, _ in peers("ctx"):
                self.back(k, to).start()

        each_owner(n, me, act)

    def finish(self, result):
        n, me = self.n, self.me
        for k, to, back in peers("ctx"):
            each_owner(n, back, lambda: self.back(k, to).wait_recv())
        w = self.landed.shape[2]
        for j in range(owners_of(n)):
            result[:, j * w : (j + 1) * w] = self.landed[j].astype(result.dtype)
        for k, to, _ in peers("ctx"):
            each_owner(n, to, lambda: self.out(k, to).wait_send())

        def act():
            for k, to, _ in peers("ctx"):
                self.back(k, to).wait_send()

        each_owner(n, me, act)


class Reduce:
    def __init__(self, g_ref, outs, bufs):
        self.g, self.outs = g_ref, outs
        self.pair_in, self.pair_sum, self.side_in, self.total, self.ctx_in, self.piece, self.all_in, sems = bufs
        self.n, self.me = lax.axis_size("ctx"), lax.axis_index("ctx")
        nf = lax.axis_size("fsdp")
        self.f, pair, sides, _ = fsdp_sides()
        self.core = lax.rem(self.f, 2)
        self.h, self.cw = g_ref.shape[0] // nf, g_ref.shape[1] // self.n
        self.first = [
            send(g_ref.at[place(2 * y + 1 - self.core, self.h), :], self.pair_in.at[y], sems.at[0, y], sems.at[1, y], fsdp=pair)
            for y in range(nf // 2)
        ]
        self.second = [
            send(self.pair_sum.at[side // 2], self.side_in.at[k], sems.at[2, k], sems.at[3, k], fsdp=side)
            for k, side in enumerate(sides)
        ]
        self.third = [
            send(self.total.at[to], self.ctx_in.at[k - 1], sems.at[4, k - 1], sems.at[5, k - 1], ctx=to)
            for k, to, _ in peers("ctx")
        ]
        self.fourth = [
            send(self.piece, self.all_in.at[self.me], sems.at[6, k - 1], sems.at[7, k - 1], ctx=to)
            for k, to, _ in peers("ctx")
        ]

    def parts(self, body):
        def step(j, _):
            body(pl.ds(pl.multiple_of(j * self.cw, LANES), self.cw), j)
            return 0

        lax.fori_loop(0, self.n, step, 0)

    def begin(self):
        for c in self.first:
            c.start()

    def over_y(self):
        for y, c in enumerate(self.first):
            c.wait_recv()

            def add(cs, j, y=y):
                both = self.g[place(2 * y + self.core, self.h), cs].astype(F32) + self.pair_in[y, :, cs].astype(F32)
                self.pair_sum[y, :, cs] = both.astype(BF16)

            self.parts(add)
        for c in self.second:
            c.start()

    def scatter(self):
        for c in self.second:
            c.wait_recv()

        def add(cs, j):
            mine = self.pair_sum[self.f // 2, :, cs].astype(F32)
            for k in range(len(self.second)):
                mine = mine + self.side_in[k, :, cs].astype(F32)
            self.total[j] = mine.astype(BF16)

        self.parts(add)
        for c in self.third:
            c.start()

    def gather(self):
        mine = self.total[self.me].astype(F32)
        for k, c in enumerate(self.third):
            c.wait_recv()
            mine = mine + self.ctx_in[k].astype(F32)
        self.piece[...] = mine.astype(BF16)
        for c in self.fourth:
            c.start()
        self.all_in[self.me] = self.piece[...]

    def finish(self):
        for c in self.fourth:
            c.wait_recv()

        for j in range(self.n):
            for ref, at, lo, hi in self.outs:
                a, b = max(lo, j * self.cw), min(hi, (j + 1) * self.cw)
                if a < b:
                    part = self.all_in[j, :, a - j * self.cw : b - j * self.cw]
                    ref[:, at + a - lo : at + b - lo] = part.astype(F32)
        for c in self.first + self.second + self.third + self.fourth:
            c.wait_send()


def reduce_scratch(n, nf, cw):
    half, low = nf // 2, LOW // nf
    return [
        pltpu.VMEM((half, low, n * cw), BF16), pltpu.VMEM((half, low, n * cw), BF16),
        pltpu.VMEM((max(half - 1, 1), low, n * cw), BF16), pltpu.VMEM((n, low, cw), BF16),
        pltpu.VMEM((n - 1, low, cw), BF16), pltpu.VMEM((low, cw), BF16), pltpu.VMEM((n, low, cw), BF16),
        pltpu.SemaphoreType.DMA((8, max(n, half))),
    ]


class Mover:
    def __init__(self, sems):
        self.sems, self.used = sems, 0

    def go(self, src, dst):
        c = pltpu.make_async_copy(src, dst, self.sems.at[self.used])
        self.used += 1
        c.start()
        return c

    def tiles(self, src, dst):
        return [self.go(src.at[t : t + SPAN, :], dst.at[t : t + SPAN, :]) for t in range(0, dst.shape[0], SPAN)]


MOVES = 64


def each_tile(n, body):
    def step(t, _):
        body(t)
        return 0

    lax.fori_loop(0, n, step, 0)


def tile_rows(t):
    return pl.ds(pl.multiple_of(t * SPAN, SPAN), SPAN)


def each_chunk(width, body, step=256):
    def run(c, _):
        body(lambda base=0: pl.ds(pl.multiple_of(base + c * step, LANES), step))
        return 0

    lax.fori_loop(0, width // step, run, 0)


def wide_chunks(width, step=256):
    return [slice(c, min(c + step, width)) for c in range(0, width, step)]


class Resident:
    def __init__(self, wall_ref, dst, sems, lo, hi, early=None):
        nf, _, kw = wall_ref.shape
        f = lax.axis_index("fsdp")
        self.copies, at = [], 0
        for j in range(nf):
            which = lax.rem(f + j, nf)
            cols = pl.ds(pl.multiple_of(which * kw, LANES), kw)
            if early is not None:
                own, others = early
                src = own.at[0:SPLIT, :] if j == 0 else others.at[which]
                self.copies.append(pltpu.make_async_copy(src, dst.at[0:SPLIT, cols], sems.at[nf + j]))
            start = max(lo, SPLIT)
            src = wall_ref.at[which, start - SPLIT : hi - SPLIT, :]
            self.copies.append(pltpu.make_async_copy(src, dst.at[start - lo : hi - lo, cols], sems.at[j]))

    def begin(self):
        for c in self.copies:
            c.start()

    def finish(self):
        for c in self.copies:
            c.wait()


def softplus(v):
    e = jnp.exp(-jnp.abs(v))
    series = e * (1.0 - e * (0.5 - e * (1.0 / 3.0 - 0.25 * e)))
    return jnp.maximum(v, 0.0) + jnp.where(e < 0.01, series, jnp.log(1.0 + e))


def block_mask(meta, t, transposed):
    col, row = meta.cols(t), meta.rows(t)
    return (meta.seq(col) == meta.seq(row)) & ((row >= col) if transposed else (col >= row))


def halves(x):
    lane = iota(x.shape, 1)
    zero = jnp.zeros_like(x)
    return jnp.where(lane < HEAD, x, zero), jnp.where(lane >= HEAD, x, zero)


DTR, DT, C2, WTS, RS, DCM = (slice(k * LANES, (k + 1) * LANES) for k in range(6))
SMALL = 6 * LANES


def front_kernel(
    len_ref, id_ref, slot_ref, where_ref, gain_ref, cw_ref, cb_ref, bias_ref, rate_ref, skip_ref, gate_ref, od_ref, ou_ref,
    got_h, wall_h, dall_h, uall_h, e_h, cots_h, wo_h, wt_h,
    x_h, hb_h, u_h, act_h, dact_h, small_h, c2t_h, carry_h, next_h, thr_h, dout_h, dm_h, dz_h, dst_h, own_ref, g_ref,
    back_h, woall_h, wzall_h,
    wv, down, up, odown, oup, e, got, x, hb, u, v, dv, raw, act, ls, y, nout, states, sorted_ref, cot, small, reaches, c2t, carry,
    wide, prods, low, run, through, sc, tails, landed, parts, first, starts, slices,
    move_sems, w_sem, s_halo, r_halo, s_cot, r_cot, own_cot, s_out, r_out, own_out, s1, r1, s2, r2, *g_sems,
):
    n, me = lax.axis_size("ctx"), lax.axis_index("ctx")
    nf, f = lax.axis_size("fsdp"), lax.axis_index("fsdp")
    rows, width = x.shape
    nb = rows // SPAN
    mid = INNER + CONV_CH
    meta = Meta(len_ref, id_ref, rows)
    targets = ctx_targets() + fsdp_targets()
    landed[...] = jnp.zeros_like(landed)
    hail(targets)
    mover = Mover(move_sems)
    in_got = mover.go(got_h, got)
    in_down = mover.go(dall_h, down)
    proj_w = wt_h.shape[0]
    first_weights = Resident(wall_h, wv, w_sem.at[0], INNER, proj_w)
    first_weights.begin()
    in_up = mover.go(uall_h, up)
    in_e = mover.go(e_h, e)
    halo = send(tails.at[nb, 5:8, :], landed.at[5:8, :], s_halo, r_halo, ctx=lax.rem(me + 1, n))
    cots = Spread(cots_h, cot, s_cot, r_cot, own_cot, halves_of(n)[0])
    late_cots = Spread(cots_h, cot, s_cot, r_cot, None, halves_of(n)[1])
    kw = wo_h.shape[0]
    pieces = [
        (od_ref, stacked(odown, od_ref.shape[0])), (ou_ref, stacked(oup, ou_ref.shape[0])),
        (wt_h.at[0:SPLIT, :], lambda which: wzall_h.at[which]), (wo_h, stacked(woall_h, kw)),
    ]
    gather = Gather(pieces, g_sems, kept=2)
    exchange = Exchange(
        parts, lambda first, j: first[j, STATE:].astype(F32)[0:1], first, starts, slices, (s1, r1, s2, r2), False
    )
    in_got.wait()
    in_down.wait()

    def norm(t):
        at = tile_rows(t)
        pos = meta.cols(t)
        hit = one_hot(iota((SPAN, rows), 0) + t * SPAN == slot_ref[...])
        valid = meta.valid(pos)
        total = jnp.zeros((SPAN, LANES), F32)
        for cs in wide_chunks(width):
            xt = nn(hit, got[:, cs]) * valid
            x[at, cs] = xt.astype(BF16)
            sq = xt * xt
            total = total + sq[:, :LANES] + sq[:, LANES:]
        rstd = lax.rsqrt(jnp.sum(total, 1, keepdims=True) * (1.0 / width) + EPS)
        for cs in wide_chunks(width):
            hb[at, cs] = (x[at, cs].astype(F32) * rstd * gain_ref[:, cs]).astype(BF16)
        u[at, :] = (nt(hb[at, :], down[...]) * meta.select(pos)).astype(BF16)

    in_up.wait()
    first_weights.finish()

    def project(s):
        t = nb - 1 - s
        norm(t)
        at = tile_rows(t)
        for cs in wide_chunks(CONV_CH):
            raw[at, cs] = (nt(hb[at, :], wv[cs, :]) + nn(u[at, :], up[:, INNER + cs.start : INNER + cs.stop])).astype(BF16)
        last = nt(hb[at, :], wv[CONV_CH:, :]) + nn(u[at, :], up[:, mid:])
        small[at, DTR] = jnp.concatenate([last, jnp.zeros((SPAN, LANES - HEADS), F32)], 1)
        tails[t + 1] = raw[pl.ds(pl.multiple_of(t * SPAN + SPAN - 16, 16), 16), :].astype(F32)[8:]

        @pl.when(t == nb - 1)
        def _():
            hailed(targets)
            pl.when(me < n - 1)(halo.start)
            gather.begin()
            cots.begin()

    each_tile(nb, project)
    done = [mover.go(x, x_h), mover.go(hb, hb_h), mover.go(u, u_h)]
    hb_out = done[1]
    in_e.wait()

    def conv(s):
        t = lax.rem(s + 1, nb)
        at = tile_rows(t)

        @pl.when(t == 0)
        def _():
            pl.when(me > 0)(halo.wait_recv)
            tails[0] = jnp.where(me > 0, landed[...], 0.0)

        pos = meta.cols(t)
        seq = meta.seq(pos)
        masks = [(meta.seq(pos - j) == seq).astype(F32) for j in range(KERNEL)]
        for cs in wide_chunks(CONV_CH):
            cur = raw[at, cs].astype(F32)
            ext = jnp.concatenate([tails[t, :, cs], cur], 0)
            acc = cb_ref[:, cs] + cw_ref[3:4, cs] * cur
            for j in range(1, KERNEL):
                moved = pltpu.roll(ext, j, 0)[8:]
                acc = acc + (cw_ref[3 - j : 4 - j, cs] * moved) * masks[j]
            sg = sigmoid(acc)
            val = acc * sg
            raw[at, cs] = (sg + val * (1.0 - sg)).astype(BF16)
            act[at, cs] = val.astype(BF16)
        dt = softplus(small[at, DTR] + bias_ref[...])
        small[at, DT] = dt
        tri = one_hot(iota((SPAN, SPAN), 0) >= iota((SPAN, SPAN), 1))
        cum = sum(nn(tri, p) for p in split(dt * rate_ref[...], 3))
        start = meta.start + t * SPAN
        end_same = (seq == meta.seq(start + SPAN - 1)).astype(F32)
        passing = (seq == meta.seq(start - 1)).astype(F32)
        wts = jnp.exp(cum[SPAN - 1 : SPAN, :] - cum) * dt * end_same
        small[at, WTS] = wts
        reach = jnp.exp(cum) * passing
        reaches[at, :] = reach
        c2 = cum * LOG2E
        small[at, C2] = c2
        c2t[t] = c2.T[:HEADS]
        both = pairs(wts)
        bm = act[at, INNER : INNER + STATE]
        for cs in wide_chunks(INNER):
            weighted = (act[at, cs].astype(F32) * nn(both, e[:, cs])).astype(BF16)
            ls[t, :, cs] = tn(bm, weighted)
        ends = split(jnp.broadcast_to(reach[SPAN - 1 : SPAN, :], (16, LANES)), 3)
        carry[t] = sum(nn(p, e[:LANES, :]) for p in ends)[:8]

    each_tile(nb, conv)
    dact_out = mover.go(raw, dact_h)
    done += [mover.go(act, act_h), mover.go(c2t, c2t_h), mover.go(carry, carry_h)]
    ow = parts.shape[2]
    for j in range(parts.shape[0]):
        at = slice(j * ow, (j + 1) * ow)
        state, reached = ls[0, :, at], carry[0, 0:1, at]
        for b in range(1, nb):
            state = state * carry[b, 0:1, at] + ls[b, :, at]
            reached = reached * carry[b, 0:1, at]
        parts[j, :STATE] = state.astype(BF16)
        parts[j, STATE:] = jnp.broadcast_to(reached, (16, ow)).astype(BF16)
    exchange.begin()

    def mix_tile(t):
        at = tile_rows(t)
        bm, cm = act[at, INNER : INNER + STATE], act[at, INNER + STATE :]
        sc[...] = jnp.where(block_mask(meta, t, False), nt(cm, bm), 0.0)
        both = pairs(small[at, DT])
        for cs in wide_chunks(INNER):
            low[:, cs] = (act[at, cs].astype(F32) * nn(both, e[:, cs])).astype(BF16)
        c2 = small[at, C2]
        top_rows, low_rows = pl.ds(pl.multiple_of(t * SPAN, HALF), HALF), pl.ds(pl.multiple_of(t * SPAN + HALF, HALF), HALF)

        def group(g, _):
            cols = pltpu.roll(c2, LANES - 4 * g, 1)
            rws = c2t[t, pl.ds(pl.multiple_of(8 * (g // 2), 8), 8), :]
            rws = pltpu.roll(rws, 4 * lax.rem(g, 2), 0)
            for q in range(2):
                lanes = pl.ds(pl.multiple_of(g * 256 + q * 128, 128), 128)
                xa, xb = halves(low[:, lanes])
                mixes = []
                for h in (2 * q, 2 * q + 1):
                    col, row = cols[:, h : h + 1], rws[h : h + 1, :]

                    def mix(i, j):
                        decay = jnp.exp2(jnp.minimum(col[i : i + HALF] - row[:, j : j + HALF], 0.0))
                        return (sc[i : i + HALF, j : j + HALF] * decay).astype(BF16)

                    mixes.append((mix(0, 0), mix(HALF, 0), mix(HALF, HALF)))
                (a00, a10, a11), (b00, b10, b11) = mixes
                top = nn(jnp.concatenate([a00, b00], 1), jnp.concatenate([xa[:HALF], xb[:HALF]], 0))
                bot = nn(jnp.concatenate([a10, a11, b10, b11], 1), jnp.concatenate([xa, xb], 0))
                y[top_rows, lanes] = top.astype(BF16)
                y[low_rows, lanes] = bot.astype(BF16)
            return 0

        lax.fori_loop(0, HEADS // 4, group, 0)

    each_tile(nb, mix_tile)
    gather.relay(0, 3)
    gather.finish(0, 3)
    second_weights = Resident(wall_h, wv, w_sem.at[1], 0, INNER, (wt_h, wzall_h))
    second_weights.begin()
    dact_out.wait()
    gather.relay(3)
    second_weights.finish()

    def gate_tile(t):
        at = tile_rows(t)
        for cs in wide_chunks(INNER):
            raw[at, cs] = (nt(hb[at, :], wv[cs, :]) + nn(u[at, :], up[:, cs])).astype(BF16)
        pl.when(t == nb // 2)(exchange.middle)

    each_tile(nb, gate_tile)
    late_cots.begin()
    gather.finish(3)
    out_weights = [mover.go(wo_h, wv.at[place(f, kw), :])]
    for j in range(1, nf):
        which = lax.rem(f + j, nf)
        out_weights.append(mover.go(woall_h.at[place(which, kw), :], wv.at[place(which, kw), :]))
    exchange.finish(run)
    for j in range(thr_h.shape[0]):
        thr_h[j] = first[j, STATE:]
    for c in out_weights:
        c.wait()

    def out_tile(t):
        at = tile_rows(t)
        both = pairs(reaches[at, :])
        cm = act[at, INNER + STATE :]
        total = jnp.zeros((SPAN, LANES), F32)
        for cs in wide_chunks(INNER):
            now = run[:, cs]
            start = now.astype(BF16)
            states[t, :, cs] = start
            later = now * carry[t, 0:1, cs] + ls[t, :, cs]
            run[:, cs] = later
            mixed = y[at, cs].astype(F32) + nn(both, e[:, cs]) * nn(cm, start)
            mixed = mixed + skip_ref[:, cs] * act[at, cs].astype(F32)
            y[at, cs] = mixed.astype(BF16)
            z = raw[at, cs].astype(F32)
            gated = mixed * (z * sigmoid(z))
            wide[:, cs] = gated
            sq = gated * gated
            total = total + sq[:, :LANES] + sq[:, LANES:]
        rstd = lax.rsqrt(jnp.sum(total, 1, keepdims=True) * (1.0 / INNER) + EPS)
        small[at, RS] = jnp.broadcast_to(rstd, (SPAN, LANES))
        for cs in wide_chunks(INNER):
            nout[at, cs] = (wide[:, cs] * rstd * gate_ref[:, cs]).astype(BF16)
        pos = meta.cols(t)
        vt = (nt(nout[at, :], odown[...]) * meta.select(pos)).astype(BF16)
        v[at, :] = vt
        valid = meta.valid(pos)
        for cs in wide_chunks(width):
            branch = nn(nout[at, :], wv[:INNER, cs]) + nn(vt, oup[:, cs])
            got[at, cs] = ((x[at, cs].astype(F32) + branch) * valid).astype(BF16)

    each_tile(nb, out_tile)
    states[nb] = run[...].astype(BF16)
    next_out = mover.go(states.at[1 : nb + 1], next_h)
    sort_rows(where_ref[...], got, sorted_ref)
    results = Spread(sorted_ref, back_h, s_out, r_out, own_out, range(1, n))
    results.begin()
    cots.finish()
    late_cots.finish()
    hb_out.wait()

    def dout_tile(t):
        at = tile_rows(t)
        pos = meta.cols(t)
        hit = one_hot(iota((SPAN, rows), 0) + t * SPAN == slot_ref[...])
        valid = meta.valid(pos)
        for cs in wide_chunks(width):
            hb[at, cs] = (nn(hit, cot[:, cs]) * valid).astype(BF16)
        dv[at, :] = nt(hb[at, :], oup[...]).astype(BF16) * meta.select(pos).astype(BF16)

    each_tile(nb, dout_tile)
    done.append(mover.go(hb, dout_h))

    def down_grad(at):
        g_ref[:, at()] = tn(dv[...], nout[:, at()]).astype(BF16)

    def up_grad(at):
        g_ref[:, at(INNER)] = tn(v[...], hb[:, at()]).astype(BF16)

    each_chunk(INNER, down_grad)
    each_chunk(width, up_grad)
    run[...] = jnp.zeros_like(run)
    through[...] = jnp.ones_like(through)
    next_out.wait()

    def back_tile(t):
        at = tile_rows(t)
        dout, dvt = hb[at, :], dv[at, :]
        rstd = small[at, RS][:, 0:1]
        cm = act[at, INNER + STATE :]
        total = jnp.zeros((SPAN, LANES), F32)
        for cs in wide_chunks(INNER):
            z = raw[at, cs].astype(F32)
            d = (nt(dout, wv[cs, :]) + nn(dvt, odown[:, cs])) * gate_ref[:, cs]
            wide[:, cs] = d
            g = d * (y[at, cs].astype(F32) * (z * sigmoid(z)))
            total = total + g[:, :LANES] + g[:, LANES:]
        back = jnp.sum(total, 1, keepdims=True) * (1.0 / INNER) * rstd * rstd
        both = pairs(reaches[at, :])
        dcm = jnp.zeros((SPAN, STATE), F32)
        for cs in wide_chunks(INNER):
            z = raw[at, cs].astype(F32)
            sg = sigmoid(z)
            silu = z * sg
            mixed = y[at, cs].astype(F32)
            dg = rstd * (wide[:, cs] - mixed * silu * back)
            dm = (dg * silu).astype(BF16)
            nout[at, cs] = dm
            raw[at, cs] = (dg * mixed * (sg + silu * (1.0 - sg))).astype(BF16)
            dm = dm.astype(F32)
            dp = (dm * nn(both, e[:, cs])).astype(BF16)
            prods[:, cs] = (dm * (mixed - skip_ref[:, cs] * act[at, cs].astype(F32))).astype(BF16)
            dcm = dcm + nt(dp, states[t, :, cs])
            dst = tn(cm, dp)
            states[t, :, cs] = dst.astype(BF16)
            run[:, cs] += dst * through[0:1, cs]
        small[at, RS] = nt(prods[...], e[:LANES, :])
        small[at, DCM] = dcm
        through[...] = through[...] * carry[t]

    each_tile(nb, back_tile)
    for j in range(own_ref.shape[0]):
        own_ref[j] = run[:, j * ow : (j + 1) * ow].astype(BF16)
    done += [mover.go(nout, dm_h), mover.go(raw.at[:, 0:INNER], dz_h), mover.go(states.at[0:nb], dst_h), mover.go(small, small_h)]
    pl.when(me < n - 1)(halo.wait_send)
    results.finish()
    for k, c in enumerate(done):
        if k != 1:
            c.wait()


def back_kernel(
    len_ref, id_ref, where_ref, tok_ref, gain_ref, cw_ref, bias_ref, rate_ref, skip_ref, thr_ref, parts,
    g_out, wall_h, dall_h, uall_h, e_h, act_h, dact_h, small_h, c2t_h, carry_h, next_h, dm_h, dz_h, dst_h, hb_h, u_h, x_h, dout_h, back_h,
    wt_h, wzall_h,
    out_h, grad_h, indown_ref, inup_ref, outdown_ref, outup_ref, land_h,
    wv, down, up, e, act, dact, ddt, small, c2t, carry, states, dm, dz, dst, hb, u, du, duz, dhz, dbm, ga, gb,
    wide, low, prods, sct, dsc, later, head, edge, landed, first, starts, slices,
    move_sems, w_sem, s_head, r_head, s_grad, r_grad, s1, r1, s2, r2, *bufs,
):
    n, me = lax.axis_size("ctx"), lax.axis_index("ctx")
    rows, width = hb.shape
    nb = rows // SPAN
    mid, end = INNER + CONV_CH, INNER + CONV_CH + HEADS
    meta = Meta(len_ref, id_ref, rows)
    targets = ctx_targets() + fsdp_targets()
    landed[...] = jnp.zeros_like(landed)
    hail(targets)
    mover = Mover(move_sems)
    proj_w = wt_h.shape[0]
    second_weights = Resident(wall_h, wv, w_sem.at[0], 0, INNER, (wt_h, wzall_h))
    second_weights.begin()
    in_dz = mover.tiles(dz_h, dz)
    in_up = mover.go(uall_h, up)
    in_u = mover.go(u_h, u)
    base = g_out.shape[1]
    in_g = mover.go(g_out, ga.at[:, 0:base])
    for_mix = [mover.go(e_h, e), mover.go(small_h, small), mover.go(c2t_h, c2t), mover.go(act_h, act), mover.go(dm_h, dm)]
    for_chain = [mover.go(next_h, states), mover.go(dst_h, dst), mover.go(carry_h, carry)]
    for_scan = [mover.go(dact_h, dact), mover.go(hb_h, hb), mover.go(dall_h, down)]
    exchange = Exchange(parts, lambda first, j: thr_ref[j].astype(F32)[0:1], first, starts, slices, (s1, r1, s2, r2), True)
    count = len(bufs) // 2
    up_a, up_b = INNER + width, width + proj_w - INNER
    sum_a = Reduce(
        ga, [(outdown_ref, 0, 0, INNER), (outup_ref, 0, INNER, up_a), (inup_ref, 0, up_a, up_a + INNER)], bufs[:count]
    )
    sum_b = Reduce(gb, [(indown_ref, 0, 0, width), (inup_ref, INNER, width, up_b)], bufs[count:])
    second_weights.finish()
    in_up.wait()
    for c in in_dz:
        c.wait()

    def gate_tile(t):
        at = tile_rows(t)
        for cs in wide_chunks(width):
            dhz[at, cs] = nn(dz[at, :], wv[:INNER, cs]).astype(BF16)
        duz[at, :] = nt(dz[at, :], up[:, :INNER])

        @pl.when(t == 0)
        def _():
            hailed(targets)
            exchange.begin()

    each_tile(nb, gate_tile)
    first_weights = Resident(wall_h, wv, w_sem.at[1], INNER, proj_w)
    first_weights.begin()
    in_u.wait()

    def gate_grad(at):
        ga[:, at(base)] = tn(u[...], dz[:, at()]).astype(BF16)

    each_chunk(INNER, gate_grad)
    if ga.shape[1] > base + INNER:
        ga[:, base + INNER :] = jnp.zeros((LOW, ga.shape[1] - base - INNER), BF16)
    for c in for_mix:
        c.wait()

    def mix_tile(t):
        at = tile_rows(t)
        bm, cm = act[at, INNER : INNER + STATE], act[at, INNER + STATE :]
        mask = block_mask(meta, t, True)
        sct[...] = jnp.where(mask, nt(bm, cm), 0.0)
        dsc[...] = jnp.zeros_like(dsc)
        both = pairs(small[at, DT])
        for cs in wide_chunks(INNER):
            dt = nn(both, e[:, cs])
            wide[:, cs] = dt
            low[:, cs] = (act[at, cs].astype(F32) * dt).astype(BF16)
        c2 = small[at, C2]
        top_rows, low_rows = pl.ds(pl.multiple_of(t * SPAN, HALF), HALF), pl.ds(pl.multiple_of(t * SPAN + HALF, HALF), HALF)

        def group(g, _):
            cols = pltpu.roll(c2, LANES - 4 * g, 1)
            rws = c2t[t, pl.ds(pl.multiple_of(8 * (g // 2), 8), 8), :]
            rws = pltpu.roll(rws, 4 * lax.rem(g, 2), 0)
            for q in range(2):
                lanes = pl.ds(pl.multiple_of(g * 256 + q * 128, 128), 128)
                dmt = dm[at, lanes]
                da, db = halves(dmt)
                mixes = []
                for h, xh in zip((2 * q, 2 * q + 1), halves(low[:, lanes])):
                    col, row = cols[:, h : h + 1], rws[h : h + 1, :]
                    top = nt(xh[:HALF], dmt)
                    bot = nt(xh[HALF:], dmt[HALF:])

                    def mix(i, j, d):
                        decay = jnp.exp2(jnp.minimum(row[:, j : j + HALF] - col[i : i + HALF], 0.0))
                        dsc[i : i + HALF, j : j + HALF] += d * decay
                        return (sct[i : i + HALF, j : j + HALF] * decay).astype(BF16)

                    mixes.append((mix(0, 0, top[:, :HALF]), mix(0, HALF, top[:, HALF:]), mix(HALF, HALF, bot)))
                (a00, a01, a11), (b00, b01, b11) = mixes
                g_top = nn(jnp.concatenate([a00, a01, b00, b01], 1), jnp.concatenate([da, db], 0))
                g_low = nn(jnp.concatenate([a11, b11], 1), jnp.concatenate([da[HALF:], db[HALF:]], 0))
                dz[top_rows, lanes] = (g_top * wide[:HALF, lanes]).astype(BF16)
                dz[low_rows, lanes] = (g_low * wide[HALF:, lanes]).astype(BF16)
            return 0

        lax.fori_loop(0, HEADS // 4, group, 0)
        ds = jnp.where(mask, dsc[...], 0.0).astype(BF16)
        dbm[at, :] = nn(ds, cm)
        small[at, DCM] += tn(ds, bm)
        pl.when(t == nb // 2)(exchange.middle)

    each_tile(nb, mix_tile)
    in_g.wait()
    sum_a.begin()
    for c in for_chain:
        c.wait()
    exchange.finish(later)
    dend = []
    for b in reversed(range(nb)):
        sums = []
        for cs in wide_chunks(INNER):
            a = later[:, cs]
            sums.append(jnp.sum(a * states[b, :, cs].astype(F32), 0, keepdims=True))
            states[b, :, cs] = a.astype(BF16)
            later[:, cs] = dst[b, :, cs].astype(F32) + carry[b, 0:1, cs] * a
        total = jnp.broadcast_to(jnp.concatenate(sums, 1), (16, INNER))
        head[b : b + 1, :LANES] = sum(nt(p, e[:LANES, :]) for p in split(total, 3))[:1]
    for c in for_scan:
        c.wait()

    def edge_rows(k, t):
        at = pl.ds(pl.multiple_of(t * SPAN, SPAN), k)
        both = pairs(small[at, WTS])
        bm = act[at, INNER : INNER + STATE]
        for cs in wide_chunks(INNER):
            w = nn(both, e[:, cs])
            xs = act[at, cs].astype(F32)
            dx = dz[at, cs].astype(F32) + nn(bm, states[t, :, cs]) * w
            prods[:k, cs] = (xs * dx).astype(BF16)
            dx = dx + skip_ref[:, cs] * dm[at, cs].astype(F32)
            wide[:k, cs] = dx * dact[at, cs].astype(F32)
            low[:k, cs] = (xs * w).astype(BF16)
        bcols, ccols = slice(INNER, INNER + STATE), slice(INNER + STATE, CONV_CH)
        wide[:k, bcols] = (dbm[at, :] + nt(low[:k, :], states[t])) * dact[at, bcols].astype(F32)
        wide[:k, ccols] = small[at, DCM] * dact[at, ccols].astype(F32)

    edge_rows(16, 0)
    edge[...] = wide[:8, :]
    edge_copy = send(edge.at[0:3, :], landed.at[0:3, :], s_head, r_head, ctx=lax.rem(me + n - 1, n))
    pl.when(me > 0)(edge_copy.start)
    sum_a.over_y()

    def scan_tile(s):
        t = nb - 1 - s
        at = tile_rows(t)
        ends = head[pl.ds(t, 1), :LANES]
        edge_rows(SPAN, t)
        csum = nt(prods[...], e[:LANES, :])
        last = iota((SPAN, 1), 0) == SPAN - 1
        dcum = small[at, RS] - csum + jnp.where(last, ends, 0.0)
        tri = one_hot(iota((SPAN, SPAN), 0) <= iota((SPAN, SPAN), 1))
        dsteps = sum(nn(tri, p) for p in split(dcum, 3))
        val = small[at, DTR] + bias_ref[...]
        sg = 1.0 / (1.0 + jnp.exp(-val))
        ex = jnp.exp(jnp.minimum(val, 0.0))
        ratio = jnp.where(val < -12.0, 1.0 - 0.5 * ex, sg / jnp.maximum(softplus(val), 1e-7))
        steps = csum * ratio + dsteps * rate_ref[...] * sg
        ddt[at, :] = jnp.where(iota((SPAN, LANES), 1) < HEADS, steps, 0.0).astype(BF16)
        pos = meta.cols(t)
        seq = meta.seq(pos)
        masks = [(meta.seq(pos + j) == seq).astype(F32) for j in range(KERNEL)]
        for cs in wide_chunks(CONV_CH):
            cur = wide[:, cs]
            ext = jnp.concatenate([cur, edge[:, cs]], 0)
            total = cw_ref[3:4, cs] * cur
            for j in range(1, KERNEL):
                moved = pltpu.roll(ext, SPAN + 8 - j, 0)[:SPAN]
                total = total + (cw_ref[3 - j : 4 - j, cs] * moved) * masks[j]
            dact[at, cs] = total.astype(BF16)
        edge[...] = wide[:8, :]
        dut = duz[at, :] + nt(dact[at, :], up[:, INNER:mid]) + nt(ddt[at, :HEADS], up[:, mid:end])
        du[at, :] = dut.astype(BF16) * meta.select(pos).astype(BF16)
        pl.when(s == 0)(sum_a.scatter)
        pl.when(s == 2)(sum_a.gather)

    pl.when(me > 0)(edge_copy.wait_send)
    pl.when(me < n - 1)(edge_copy.wait_recv)
    edge[...] = jnp.where(me < n - 1, landed[...], 0.0)
    each_tile(nb, scan_tile)

    def down_grad(at):
        gb[:, at()] = tn(du[...], hb[:, at()]).astype(BF16)

    def conv_grad(at):
        gb[:, at(width)] = tn(u[...], dact[:, at()]).astype(BF16)

    each_chunk(width, down_grad)
    each_chunk(CONV_CH, conv_grad)
    gb[:, width + CONV_CH :] = jnp.zeros((LOW, gb.shape[1] - width - CONV_CH), BF16)
    gb[:, width + CONV_CH : width + CONV_CH + HEADS] = tn(u[...], ddt[:, :HEADS]).astype(BF16)
    sum_b.begin()
    xs, douts = dm.at[:, 0:width], dm.at[:, width : 2 * width]
    for_last = [mover.go(x_h, xs), mover.go(dout_h, douts)]
    first_weights.finish()
    sum_a.finish()
    for c in for_last:
        c.wait()

    def last_tile(t):
        at = tile_rows(t)
        squares, crosses = jnp.zeros((SPAN, LANES), F32), jnp.zeros((SPAN, LANES), F32)
        for cs in wide_chunks(width):
            dh = (
                dhz[at, cs].astype(F32) + nn(dact[at, :], wv[:CONV_CH, cs]) + nn(ddt[at, :HEADS], wv[CONV_CH:, cs])
                + nn(du[at, :], down[:, cs])
            )
            g = dh * gain_ref[:, cs]
            wide[:, cs] = g
            xt = dm[at, cs].astype(F32)
            sq, cross = xt * xt, g * xt
            squares = squares + sq[:, :LANES] + sq[:, LANES:]
            crosses = crosses + cross[:, :LANES] + cross[:, LANES:]
        rstd = lax.rsqrt(jnp.sum(squares, 1, keepdims=True) * (1.0 / width) + EPS)
        back = jnp.sum(crosses, 1, keepdims=True) * (1.0 / width) * rstd * rstd
        valid = meta.valid(meta.cols(t))
        for cs in wide_chunks(width):
            dx = rstd * (wide[:, cs] - dm[at, cs].astype(F32) * back)
            dout = dm[at, width + cs.start : width + cs.stop].astype(F32)
            hb[at, cs] = ((dout + dx) * valid).astype(BF16)
        pl.when(t == 0)(sum_b.over_y)
        pl.when(t == nb - 1)(sum_b.scatter)

    each_tile(nb, last_tile)
    share = rows // n
    sort_rows(where_ref[...], hb, act.at[:, 0:width])
    copies = [
        send(
            act.at[place(to, share), 0:width], land_h.at[place(me, share), :], s_grad.at[k - 1], r_grad.at[k - 1], ctx=to
        )
        for k, to, _ in peers("ctx")
    ]
    for c in copies:
        c.start()
    dhz[place(me, share), :] = act[place(me, share), 0:width]
    mover.go(back_h, dm.at[:, 0:width]).wait()
    sort_rows(tok_ref[...], dm.at[:, 0:width], dz.at[:, 0:width])
    out_done = mover.go(dz.at[:, 0:width], out_h)
    sum_b.gather()
    sum_b.finish()
    arrived = []
    for c, (_, _, back) in zip(copies, peers("ctx")):
        c.wait_recv()
        arrived.append(mover.go(land_h.at[place(back, share), :], dhz.at[place(back, share), :]))
    for c in arrived:
        c.wait()
    for c in copies:
        c.wait_send()
    tok, grads = tok_ref[...], []
    for t in range(0, rows, SPAN):
        hit = one_hot(iota((SPAN, rows), 0) + t == tok)
        for cs in wide_chunks(width):
            hb[t : t + SPAN, cs] = nn(hit, dhz[:, cs]).astype(BF16)
        grads.append(mover.go(hb.at[t : t + SPAN, :], grad_h.at[t : t + SPAN, :]))
    for c in grads + [out_done]:
        c.wait()


def shape(*dims, dtype=F32):
    return jax.ShapeDtypeStruct(dims, dtype)


def params(mib=60, remote=None):
    if remote is None:
        return pltpu.CompilerParams(vmem_limit_bytes=mib * MIB)
    return pltpu.CompilerParams(vmem_limit_bytes=mib * MIB, collective_id=remote, has_side_effects=True)


SMEM = pl.BlockSpec(memory_space=pltpu.SMEM)
VMEM = pl.BlockSpec(memory_space=pltpu.VMEM)
ANY = pl.BlockSpec(memory_space=pl.ANY)


def exchange_scratch(n, rows):
    owners = owners_of(n)
    w = INNER // owners
    return [
        pltpu.VMEM((n, rows, w), BF16), pltpu.VMEM((n, STATE, w), BF16), pltpu.VMEM((owners, STATE, w), BF16),
    ] + [pltpu.SemaphoreType.DMA((n - 1,))] * 4


def local(
    tokens, cotangent, order, lengths, adapter_ids, in_weight, out_weight, in_down, in_up, out_down, out_up,
    norm_gain, conv_weight, conv_bias, dt_bias, a_log, skip_gain, gate_gain,
):
    n, nf = lax.axis_size("ctx"), lax.axis_size("fsdp")
    rows, width = tokens.shape[1:]
    nb = rows // SPAN
    share = rows // n
    log_rows = rows.bit_length() - 1
    assert rows == 1 << log_rows and rows <= 1024 and rows % SPAN == 0 and nb >= 4
    assert nf % 2 == 0 and share % 16 == 0
    proj_w = in_weight.shape[1]
    rest = proj_w - INNER
    bf = lambda *dims: shape(*dims, dtype=BF16)
    vm = pltpu.VMEM
    dma = pltpu.SemaphoreType.DMA
    padded = lambda c: -(-c // (n * LANES)) * LANES * n
    owners = owners_of(n)
    ow = INNER // owners
    wt, in_down_t, out_down_t = in_weight.T, in_down.T, out_down.T
    kw, ko, ka = wt.shape[1], out_weight.shape[0], in_down_t.shape[0]
    idx = shape(1, rows, dtype=jnp.int32)
    gain, gate, cb = norm_gain[None], gate_gain[None], conv_bias[None]
    seqs = (lengths, adapter_ids)

    parts_w = len(chunks_of(proj_w - SPLIT, WEIGHT_PARTS))
    got, cot_sorted, slot, where, tok, w_in, a_in, b_in, e, skip, bias, rate = pl.pallas_call(
        partial(arrive_kernel, log_rows, share),
        in_specs=[VMEM] * 9,
        out_specs=[ANY, VMEM, VMEM, VMEM, VMEM, ANY, ANY, ANY, VMEM, VMEM, VMEM, VMEM],
        out_shape=(
            bf(rows, width), bf(rows, width), idx, idx, idx, bf(nf, proj_w - SPLIT, kw), bf(LOW, width), bf(LOW, proj_w),
            bf(2 * LANES, INNER), shape(1, INNER), shape(1, LANES), shape(1, LANES),
        ),
        scratch_shapes=[vm((rows, width), BF16)] + spread_sems(n) + gather_sems(nf, 2 + parts_w),
        compiler_params=params(remote=1),
        name="arrive",
    )(order, tokens[0], cotangent[0], wt, in_down_t, in_up, dt_bias[None], a_log[None], skip_gain[None])

    f32 = shape
    front_out = [
        bf(rows, width), bf(rows, width), bf(rows, LOW), bf(rows, CONV_CH), bf(rows, CONV_CH), f32(rows, SMALL),
        f32(nb, HEADS, SPAN), f32(nb, 8, INNER), bf(nb, STATE, INNER), bf(n, 16, ow), bf(rows, width), bf(rows, INNER),
        bf(rows, INNER), bf(nb, STATE, INNER), bf(owners, STATE, ow), bf(LOW, INNER + width), bf(rows, width),
        bf(INNER, width), bf(nf, SPLIT, kw),
    ]
    x, hb, u, act, dact, small, c2t, carry, after, thr, dout, dm, dz, dst, own, g_out, back_out, _, w_early = pl.pallas_call(
        front_kernel,
        in_specs=[SMEM, SMEM] + [VMEM] * 11 + [ANY] * 8,
        out_specs=[ANY] * 9 + [VMEM] + [ANY] * 4 + [VMEM, VMEM] + [ANY] * 3,
        out_shape=front_out,
        scratch_shapes=[
            vm((rest, width), BF16), vm((LOW, width), BF16), vm((LOW, proj_w), BF16), vm((LOW, INNER), BF16),
            vm((LOW, width), BF16), vm((2 * LANES, INNER), BF16), vm((rows, width), BF16), vm((rows, width), BF16),
            vm((rows, width), BF16), vm((rows, LOW), BF16), vm((rows, LOW), BF16), vm((rows, LOW), BF16),
            vm((rows, CONV_CH), BF16), vm((rows, CONV_CH), BF16), vm((nb, STATE, INNER), F32), vm((rows, INNER), BF16),
            vm((rows, INNER), BF16), vm((nb + 1, STATE, INNER), BF16), vm((rows, width), BF16), vm((rows, width), BF16),
            vm((rows, SMALL), F32), vm((rows, LANES), F32), vm((nb, HEADS, SPAN), F32), vm((nb, 8, INNER), F32),
            vm((SPAN, INNER), F32), vm((SPAN, INNER), BF16), vm((SPAN, INNER), BF16), vm((STATE, INNER), F32),
            vm((8, INNER), F32),
            vm((SPAN, SPAN), F32), vm((nb + 1, 8, CONV_CH), F32), vm((8, CONV_CH), F32),
            vm((owners, STATE + 16, ow), BF16), vm((n, STATE + 16, ow), BF16), vm((n, STATE, ow), BF16),
            vm((owners, STATE, ow), BF16), dma((MOVES,)), dma((2, 2 * nf)), dma, dma,
        ] + spread_sems(n) + spread_sems(n) + [dma((n - 1,))] * 4 + gather_sems(nf, 4),
        compiler_params=params(remote=2),
        name="front",
    )(
        *seqs, slot, where, gain, conv_weight, cb, bias, rate, skip, gate, out_down_t, out_up, got, w_in, a_in, b_in, e,
        cot_sorted, out_weight, wt,
    )

    cols_a, cols_b = padded(2 * INNER + width), padded(width + rest)
    low = LOW // nf
    block_output, input_grad, g_in_down, g_in_up, g_out_down, g_out_up, _ = pl.pallas_call(
        back_kernel,
        in_specs=[SMEM, SMEM] + [VMEM] * 9 + [ANY] * 21,
        out_specs=[ANY, ANY, VMEM, VMEM, VMEM, VMEM, ANY],
        out_shape=(
            bf(rows, width), bf(rows, width), f32(low, width), f32(low, proj_w), f32(low, INNER), f32(low, width),
            bf(rows, width),
        ),
        scratch_shapes=[
            vm((rest, width), BF16), vm((LOW, width), BF16), vm((LOW, proj_w), BF16), vm((2 * LANES, INNER), BF16),
            vm((rows, CONV_CH), BF16), vm((rows, CONV_CH), BF16), vm((rows, LANES), BF16), vm((rows, SMALL), F32),
            vm((nb, HEADS, SPAN), F32), vm((nb, 8, INNER), F32), vm((nb, STATE, INNER), BF16), vm((rows, INNER), BF16),
            vm((rows, INNER), BF16), vm((nb, STATE, INNER), BF16), vm((rows, width), BF16), vm((rows, LOW), BF16),
            vm((rows, LOW), BF16), vm((rows, LOW), F32), vm((rows, width), BF16), vm((rows, STATE), F32), vm((LOW, cols_a), BF16), vm((LOW, cols_b), BF16), vm((SPAN, CONV_CH), F32),
            vm((SPAN, INNER), BF16), vm((SPAN, INNER), BF16), vm((SPAN, SPAN), F32), vm((SPAN, SPAN), F32),
            vm((STATE, INNER), F32), vm((8, LANES), F32), vm((8, CONV_CH), F32), vm((8, CONV_CH), F32),
            vm((n, STATE, ow), BF16), vm((n, STATE, ow), BF16), vm((owners, STATE, ow), BF16),
            dma((MOVES,)), dma((2, 2 * nf)), dma, dma,
        ] + [dma((n - 1,))] * 6 + reduce_scratch(n, nf, cols_a // n) + reduce_scratch(n, nf, cols_b // n),
        compiler_params=params(62, remote=3),
        name="back",
    )(
        *seqs, where, tok, gain, conv_weight, bias, rate, skip, thr, own, g_out, w_in, a_in, b_in, e, act, dact, small, c2t,
        carry, after, dm, dz, dst, hb, u, x, dout, back_out, wt, w_early,
    )
    return block_output[None], input_grad[None], g_in_down.T, g_in_up, g_out_down.T, g_out_up


def solution(mesh):
    placed = (
        P("fsdp", "ctx", None),
        P("fsdp", "ctx", None),
        P("fsdp", None),
        P("fsdp", None),
        P("fsdp", None),
        P("fsdp", None),
        P("fsdp", None),
        P(None, "fsdp"),
        P("fsdp", None),
        P(None, "fsdp"),
        P("fsdp", None),
        P(),
        P(),
        P(),
        P(),
        P(),
        P(),
        P(),
    )
    return jax.shard_map(
        local,
        mesh=mesh,
        in_specs=placed,
        out_specs=(
            P("fsdp", "ctx", None),
            P("fsdp", "ctx", None),
            P(None, "fsdp"),
            P("fsdp", None),
            P(None, "fsdp"),
            P("fsdp", None),
        ),
        check_vma=False,
    )
```

time: 898 us -> 367 us (0.41)
  Pallas kernels: 0 us -> 355 us
  waiting for transfers between devices: 234 us -> 0 us
  other arithmetic: 211 us -> 0 us
  matrix products: 184 us -> 0 us
  local copies, waits for them, and re-layouts: 164 us -> 8.7 us
  blocking collectives: 43.5 us -> 0 us
  starting transfers between devices: 33.3 us -> 0 us
  between operations: 16.4 us -> 0.68 us
    pallas_call x0 -> x3, Pallas kernels: none -> 355 us  [the longest x1 157 us: local(): pl.pallas_call(front_kernel, in_specs=[SMEM, SMEM] + [VMEM] * 11 + [ANY]...]
    dot_general x28 -> x0, matrix products: 184 us -> none  [the longest x6 46.5 us: outer_cols(): lax.dot_general(left, right, (((1,), (1,)), ((), ())), preferred_element_...]
    all_to_all x4 -> x0, waiting for transfers between devices: 107 us -> none  [the longest x1 54.6 us: local(): lax.all_to_all(sent_cot, 'ctx', split_axis=0, concat_axis=0, tiled=True)]
    psum x1 -> x0, waiting for transfers between devices: 71.8 us -> none  [local(): lax.psum(grads[0].astype(jnp.bfloat16), 'ctx').astype(jnp.float32)]
    another operation x14 -> x0, other arithmetic: 59.7 us -> none
    gather x9 -> x0, local copies, waits for them, and re-layouts: 54.8 us -> none  [the longest x1 8.32 us: local(): sent_tokens = jnp.take(tokens[0], send_order, axis=0)]
    all_gather x4 -> x0, blocking collectives: 43.5 us -> none  [the longest x1 19.6 us: prefix(): lax.all_gather(part.astype(kind), axis)]
    reduce_scatter x4 -> x0, waiting for transfers between devices: 43.5 us -> none  [the longest x1 28.9 us: local(): lax.psum_scatter(totals[1].astype(jnp.bfloat16), 'fsdp', scatter_dimensio...]
  transfers between devices with their start and end apart: 16 -> 0, of which waited for: 7 -> 0; matrix products, arithmetic and copies ran while one was open for 32% -> 0% of each run, Pallas kernels for 0% -> 0%
where the time goes in v4:
time: 367 us; the launch traced here: 365 us
  Pallas kernels  355 us (97%)
  local copies, waits for them, and re-layouts  8.7 us (2%)
    pallas_call x1, Pallas kernels, local(): pl.pallas_call(front_kernel, in_specs=[SMEM, SMEM] + [VMEM] * 11 + [ANY]...  157 us
    pallas_call x1, Pallas kernels, local(): pl.pallas_call(back_kernel, in_specs=[SMEM, SMEM] + [VMEM] * 9 + [ANY] *...  141 us
    pallas_call x1, Pallas kernels, local(): pl.pallas_call(partial(arrive_kernel, log_rows, share), in_specs=[VMEM] *...  56.9 us
    unnamed x16, local copies, waits for them, and re-layouts  7.39 us

profile of v4, /device:TPU:10, one launch (start us, length us, event | category | flops | bytes accessed | tf_op | source)
XLA Modules:
  0.0 364.7 jit_solution(6232924698016590252)
XLA Ops:
  0.6 1.3 broadcast_in_dim.28.cb_ref
  1.9 56.9 %arrive.1 = (bf16[1024,1024]{1,0:T(8,128)(2,1)}, bf16[1024,1024]{1,0:T(8,128)(2,1)}, s32[1,1024]{1,0:T(1,128)}, s32[1,1024]{1,0:T(1,128)}, s32[1,1024]{1,0:T(1,1...) custom-call(s32[1,8192]{1,0:T(1,128)} %order_ref.1, ...), custom_call_target="tpu_custom_call" | custom-call | tf_op jit(solution)/shard_map/arrive/pallas_call | solution.py:1220
  58.8 157.2 %front.1 = (bf16[1024,1024]{1,0:T(8,128)(2,1)}, bf16[1024,1024]{1,0:T(8,128)(2,1)}, bf16[1024,128]{1,0:T(8,128)(2,1)}, bf16[1024,2304]{1,0:T(8,128)(2,1)}, bf16[...) custom-call(s32[1,3]{1,0:T(1,128)} %len_ref.3, ...), custom_call_target="tpu_custom_call" | custom-call | tf_op jit(solution)/shard_map/front/pallas_call | solution.py:1240
  216.1 141.2 %back.1 = (bf16[1024,1024]{1,0:T(8,128)(2,1)}, bf16[1024,1024]{1,0:T(8,128)(2,1)}, f32[32,1024]{1,0:T(8,128)}, f32[32,4384]{1,0:T(8,128)}, f32[32,2048]{1,0:T(8,...) custom-call(s32[1,3]{1,0:T(1,128)} %len_ref.3, s32[1,3]{1,0:T(1,128)} %id_ref.3, ...), custom_call_target="tpu_custom_call" | custom-call | tf_op jit(solution)/shard_map/back/pallas_call | solution.py:1267
  357.3 0.0 copy-start
  357.3 3.2 copy.30
  360.5 0.0 copy-done
  360.5 0.0 copy-start.4
  360.5 0.0 copy-start.1
  360.5 0.0 copy-start.2
  360.5 0.0 copy-start.3
  360.5 1.3 copy.31
  361.8 0.0 copy-done.4
  361.8 0.7 copy.32
  362.5 0.0 copy-done.1
  362.5 0.8 copy.33
  363.3 0.0 copy-done.2
  363.3 0.7 copy.34
  364.0 0.0 copy-done.3
  364.0 0.7 copy.35
Async XLA Ops:
  357.3 3.2 copy-start
  360.5 1.3 copy-start.4
  360.5 2.0 copy-start.1
  360.5 2.8 copy-start.2
  360.5 3.5 copy-start.3
